TPU v7x, 32 devices: a whole 2x2x4 slice. The times are simulated.
32 devices in a mesh: dp: 8 (over z, y), tensor: 4 (over x, core).
Axes of the slice: x: 2, y: 2, z: 4, core: 2. Of those that a mesh axis runs over, the one named last changes fastest.
Arguments:
- inputs: bfloat16 [65536, 1024], P(('dp', 'tensor')), may hold values from -6 to 6
- query_weight: bfloat16 [1024, 1024], P('tensor'), may hold values from -0.1875 to 0.1875
- key_weight: bfloat16 [1024, 1024], P('tensor'), may hold values from -0.1875 to 0.1875
- value_weight: bfloat16 [1024, 1024], P('tensor'), may hold values from -0.1875 to 0.1875
- output_weight: bfloat16 [1024, 1024], P('tensor'), may hold values from -3 to 3
- inner_weight: bfloat16 [1024, 4096], P(None, 'tensor'), may hold values from -0.1875 to 0.1875
- inner_bias: float32 [4096], P('tensor'), may hold values from -3 to 3
- outer_weight: bfloat16 [4096, 1024], P('tensor'), may hold values from -0.09375 to 0.09375
- outer_bias: float32 [1024], replicated, may hold values from -3 to 3
- first_gain: float32 [1024], replicated, may hold values from 0.1 to 1.9
- first_shift: float32 [1024], replicated, may hold values from -2 to 2
- second_gain: float32 [1024], replicated, may hold values from 0.1 to 1.9
- second_shift: float32 [1024], replicated, may hold values from -2 to 2
- item_lengths: int32 [16], P('dp'), may hold values from 1024 to 4096, as said below
- key_mask: int32 [65536], P('dp'), may hold values from 0 to 1, as said below
- random_blocks: int32 [16, 16, 64, 3], P('dp', 'tensor'), may hold values from 0 to 63
- cotangent: bfloat16 [65536, 1024], P(('dp', 'tensor')), may hold values from -6 to 6
Outputs:
- outputs: bfloat16 [65536, 1024], P(('dp', 'tensor'))
- input_grad: float32 [65536, 1024], P(('dp', 'tensor'))
- query_weight_grad: float32 [1024, 1024], P('tensor')
- key_weight_grad: float32 [1024, 1024], P('tensor')
- value_weight_grad: float32 [1024, 1024], P('tensor')
- output_weight_grad: float32 [1024, 1024], P('tensor')
- inner_weight_grad: float32 [1024, 4096], P(None, 'tensor')
- inner_bias_grad: float32 [4096], P('tensor')
- outer_weight_grad: float32 [4096, 1024], P('tensor')
- outer_bias_grad: float32 [1024], replicated
- first_gain_grad: float32 [1024], replicated
- first_shift_grad: float32 [1024], replicated
- second_gain_grad: float32 [1024], replicated
- second_shift_grad: float32 [1024], replicated
Inputs may be any that keep to these rules, and one draw needn't show every extreme that they name: `item_lengths`: multiples of 64; in every draw some item uses all 4096 rows. `key_mask`: the first row of every item is 1.
All inputs are finite; a program needn't handle non-finite values.
Results may differ from a plain program's by a relative error of at most 0.012.
The roundings to bfloat16 on the way count: a program that leaves them out, or rounds other values in their place, can miss the bound.
Values may be sent and summed in bfloat16 or wider, within the bound.
No kernel may reach another device: no remote copies, remote signals or barrier semaphores. Data moves between devices by JAX's collectives and lax.ppermute only.
A program may use at most 384 MiB of HBM per device.

v0:
```python
import jax
import jax.numpy as jnp
from jax import lax
from jax.sharding import PartitionSpec as P

EPSILON = 1e-05
MASKED = -1e30
HIGHEST = lax.Precision.HIGHEST


def contract_rows(left, right):
    return lax.dot_general(
        left, right, (((0,), (0,)), ((), ())), preferred_element_type=jnp.float32
    )


def contract_cols(left, right):
    return lax.dot_general(
        left, right, (((1,), (1,)), ((), ())), preferred_element_type=jnp.float32
    )


def block_lists(blocks_used, random_pick):
    block_count = random_pick.shape[0]
    places = jnp.arange(block_count, dtype=jnp.int32)[:, None]
    fixed_cols = jnp.zeros_like(places)
    chosen = jnp.concatenate(
        [
            places - 1,
            places,
            places + 1,
            fixed_cols,
            fixed_cols + blocks_used - 1,
            random_pick % blocks_used,
        ],
        axis=1,
    )
    inside = (chosen >= 0) & (chosen < blocks_used)
    slot_count = chosen.shape[1]
    before = jnp.arange(slot_count)[:, None] < jnp.arange(slot_count)[None, :]
    repeated = jnp.any(
        (chosen[:, :, None] == chosen[:, None, :]) & inside[:, :, None] & before[None], axis=1
    )
    return (jnp.clip(chosen, 0, block_count - 1), inside & jnp.logical_not(repeated))


def norm_rows(resid, gain, shift):
    center = jnp.mean(resid, axis=1, keepdims=True)
    deviation = resid - center
    inverse = lax.rsqrt(jnp.mean(deviation * deviation, axis=1, keepdims=True) + EPSILON)
    unit_rows = deviation * inverse
    normed = (unit_rows * gain + shift).astype(jnp.bfloat16)
    return (normed, unit_rows, inverse)


def gather_normed(normed):
    return lax.all_gather(normed, "tensor", axis=0, tiled=True)


def norm_back(grad_normed, unit_rows, inverse, gain):
    scaled = grad_normed * gain
    plain_mean = jnp.mean(scaled, axis=1, keepdims=True)
    cross_mean = jnp.mean(scaled * unit_rows, axis=1, keepdims=True)
    resid_grad = inverse * (scaled - plain_mean - unit_rows * cross_mean)
    return (resid_grad, jnp.sum(grad_normed * unit_rows, axis=0), jnp.sum(grad_normed, axis=0))


def gather_grads(grad_slice):
    return lax.all_gather(grad_slice, "tensor", axis=0, tiled=True)


def sum_inputs(term):
    return lax.psum_scatter(term, "tensor", scatter_dimension=0, tiled=True)


def selection(chosen):
    block_count = chosen.shape[0]
    return chosen[:, :, None] == jnp.arange(block_count, dtype=jnp.int32)[None, None, :]


def sparse_parts(query_rows, key_rows, value_rows, chosen, usable, key_ok):
    block_count = chosen.shape[0]
    item_span, head_size = query_rows.shape
    block_len = item_span // block_count
    select = selection(chosen)
    select_low = select.astype(jnp.bfloat16)
    query_blocks = query_rows.reshape(block_count, block_len, head_size)
    key_blocks = (
        jnp.einsum(
            "nsm,mld->nsld",
            select_low,
            key_rows.reshape(block_count, block_len, head_size),
            preferred_element_type=jnp.float32,
        )
        .astype(jnp.bfloat16)
        .reshape(block_count, -1, head_size)
    )
    value_blocks = (
        jnp.einsum(
            "nsm,mld->nsld",
            select_low,
            value_rows.reshape(block_count, block_len, head_size),
            preferred_element_type=jnp.float32,
        )
        .astype(jnp.bfloat16)
        .reshape(block_count, -1, head_size)
    )
    okay_blocks = key_ok.reshape(block_count, block_len).astype(jnp.float32)
    picked_ok = (
        jnp.einsum("nsm,ml->nsl", select.astype(jnp.float32), okay_blocks, precision=HIGHEST) > 0.5
    )
    allowed = (usable[:, :, None] & picked_ok).reshape(block_count, 1, -1)
    scores = jnp.einsum(
        "nqd,nkd->nqk", query_blocks, key_blocks, preferred_element_type=jnp.float32
    ) * head_size ** (-0.5)
    return (query_blocks, key_blocks, value_blocks, jnp.where(allowed, scores, MASKED), select)


def global_parts(query_rows, key_rows, offset, block_len, key_ok):
    global_rows = jnp.concatenate(
        [query_rows[:block_len], lax.dynamic_slice_in_dim(query_rows, offset, block_len, 0)], axis=0
    )
    scores = contract_cols(global_rows, key_rows) * query_rows.shape[1] ** (-0.5)
    return (global_rows, jnp.where(key_ok[None, :], scores, MASKED))


def softmax_parts(scores):
    row_max = jnp.max(scores, axis=-1, keepdims=True)
    shifted = jnp.exp(scores - row_max)
    row_total = jnp.sum(shifted, axis=-1, keepdims=True)
    return (shifted / row_total, row_max + jnp.log(row_total))


def attend_forward(group_rows):
    query_rows, key_rows, value_rows, random_pick, blocks_used, key_ok = group_rows
    block_count = random_pick.shape[0]
    item_span, head_size = query_rows.shape
    block_len = item_span // block_count
    chosen, usable = block_lists(blocks_used, random_pick)
    query_blocks, key_blocks, value_blocks, scores, select = sparse_parts(
        query_rows, key_rows, value_rows, chosen, usable, key_ok
    )
    probs, log_total = softmax_parts(scores)
    attended = jnp.einsum(
        "nqk,nkd->nqd", probs.astype(jnp.bfloat16), value_blocks, preferred_element_type=jnp.float32
    ).reshape(item_span, head_size)
    offset = (blocks_used - 1) * block_len
    global_rows, global_scores = global_parts(query_rows, key_rows, offset, block_len, key_ok)
    global_probs, global_log = softmax_parts(global_scores)
    global_out = jnp.dot(
        global_probs.astype(jnp.bfloat16), value_rows, preferred_element_type=jnp.float32
    )
    attended = attended.at[:block_len].set(global_out[:block_len])
    attended = lax.dynamic_update_slice_in_dim(attended, global_out[block_len:], offset, 0)
    return (attended, log_total, global_log)


def attend_backward(group_rows):
    (
        query_rows,
        key_rows,
        value_rows,
        random_pick,
        blocks_used,
        key_ok,
        grad_out,
        log_total,
        global_log,
    ) = group_rows
    block_count = random_pick.shape[0]
    item_span, head_size = query_rows.shape
    block_len = item_span // block_count
    factor = head_size ** (-0.5)
    chosen, usable = block_lists(blocks_used, random_pick)
    query_blocks, key_blocks, value_blocks, scores, select = sparse_parts(
        query_rows, key_rows, value_rows, chosen, usable, key_ok
    )
    probs = jnp.exp(scores - log_total)
    offset = (blocks_used - 1) * block_len
    block_ids = jnp.arange(item_span, dtype=jnp.int32) // block_len
    in_global = (block_ids == 0) | (block_ids == blocks_used - 1)
    sparse_grad = jnp.where(in_global[:, None], jnp.zeros_like(grad_out), grad_out).reshape(
        block_count, block_len, head_size
    )
    grad_probs = jnp.einsum(
        "nqd,nkd->nqk", sparse_grad, value_blocks, preferred_element_type=jnp.float32
    )
    score_grad = (
        probs * (grad_probs - jnp.sum(probs * grad_probs, axis=-1, keepdims=True))
    ).astype(jnp.bfloat16)
    query_grad = (
        jnp.einsum("nqk,nkd->nqd", score_grad, key_blocks, preferred_element_type=jnp.float32)
        * factor
    ).reshape(item_span, head_size)
    key_slots = (
        jnp.einsum("nqk,nqd->nkd", score_grad, query_blocks, preferred_element_type=jnp.float32)
        * factor
    )
    value_slots = jnp.einsum(
        "nqk,nqd->nkd", probs.astype(jnp.bfloat16), sparse_grad, preferred_element_type=jnp.float32
    )
    select_full = select.astype(jnp.float32)
    key_grad = jnp.einsum(
        "nsm,nsld->mld",
        select_full,
        key_slots.reshape(block_count, -1, block_len, head_size),
        precision=HIGHEST,
    ).reshape(item_span, head_size)
    value_grad = jnp.einsum(
        "nsm,nsld->mld",
        select_full,
        value_slots.reshape(block_count, -1, block_len, head_size),
        precision=HIGHEST,
    ).reshape(item_span, head_size)
    global_rows, global_scores = global_parts(query_rows, key_rows, offset, block_len, key_ok)
    global_probs = jnp.exp(global_scores - global_log)
    global_grad = jnp.concatenate(
        [grad_out[:block_len], lax.dynamic_slice_in_dim(grad_out, offset, block_len, 0)], axis=0
    )
    global_dprobs = contract_cols(global_grad, value_rows)
    global_sgrad = (
        global_probs
        * (global_dprobs - jnp.sum(global_probs * global_dprobs, axis=-1, keepdims=True))
    ).astype(jnp.bfloat16)
    global_qgrad = jnp.dot(global_sgrad, key_rows, preferred_element_type=jnp.float32) * factor
    key_grad = key_grad + contract_rows(global_sgrad, global_rows) * factor
    value_grad = value_grad + contract_rows(global_probs.astype(jnp.bfloat16), global_grad)
    query_grad = query_grad.at[:block_len].set(global_qgrad[:block_len])
    query_grad = lax.dynamic_update_slice_in_dim(query_grad, global_qgrad[block_len:], offset, 0)
    return (
        query_grad.astype(jnp.bfloat16),
        key_grad.astype(jnp.bfloat16),
        value_grad.astype(jnp.bfloat16),
    )


def per_device(
    inputs,
    query_weight,
    key_weight,
    value_weight,
    output_weight,
    inner_weight,
    inner_bias,
    outer_weight,
    outer_bias,
    first_gain,
    first_shift,
    second_gain,
    second_shift,
    item_lengths,
    key_mask,
    random_blocks,
    cotangent,
):
    item_count = item_lengths.shape[0]
    local_rows = inputs.shape[0]
    row_count = local_rows * lax.axis_size("tensor")
    item_span = row_count // item_count
    head_count = random_blocks.shape[1]
    local_width = query_weight.shape[0]
    head_size = local_width // head_count
    block_count = random_blocks.shape[2]
    block_len = item_span // block_count
    places = jnp.arange(item_span, dtype=jnp.int32)
    item_live = places[None, :] < item_lengths[:, None]
    key_ok = item_live & (key_mask.reshape(item_count, item_span) == 1)
    blocks_used = item_lengths // block_len
    live_rows = item_live.reshape(row_count, 1)

    def split_heads(block):
        return (
            block.reshape(item_count, item_span, head_count, head_size)
            .transpose(0, 2, 1, 3)
            .reshape(item_count * head_count, item_span, head_size)
        )

    def join_heads(block):
        return (
            block.reshape(item_count, head_count, item_span, head_size)
            .transpose(0, 2, 1, 3)
            .reshape(row_count, local_width)
        )

    group_info = (
        random_blocks.reshape(item_count * head_count, block_count, -1),
        jnp.repeat(blocks_used, head_count),
        jnp.repeat(key_ok, head_count, axis=0),
    )
    resid = inputs.astype(jnp.float32)
    grad_top = cotangent.astype(jnp.float32)
    first_local, first_unit, first_inverse = norm_rows(resid, first_gain, first_shift)
    first_normed = gather_normed(first_local)
    joint_weight = jnp.concatenate([query_weight, key_weight, value_weight], axis=0)
    packed = contract_cols(first_normed, joint_weight).astype(jnp.bfloat16)
    query_heads = split_heads(packed[:, :local_width])
    key_heads = split_heads(packed[:, local_width : 2 * local_width])
    value_heads = split_heads(packed[:, 2 * local_width :])
    attended, log_total, global_log = lax.map(
        attend_forward, (query_heads, key_heads, value_heads) + group_info
    )
    joined = join_heads(attended)
    merged = jnp.where(live_rows, joined, jnp.zeros_like(joined)).astype(jnp.bfloat16)
    middle = resid + lax.psum_scatter(
        jnp.dot(merged, output_weight, preferred_element_type=jnp.float32),
        "tensor",
        scatter_dimension=0,
        tiled=True,
    )
    second_local, second_unit, second_inverse = norm_rows(middle, second_gain, second_shift)
    second_normed = gather_normed(second_local)
    inner_pre = (
        jnp.dot(second_normed, inner_weight, preferred_element_type=jnp.float32) + inner_bias
    )
    hidden_act = jax.nn.gelu(inner_pre, approximate=True).astype(jnp.bfloat16)
    ffn_branch = lax.psum_scatter(
        jnp.dot(hidden_act, outer_weight, preferred_element_type=jnp.float32).astype(jnp.bfloat16),
        "tensor",
        scatter_dimension=0,
        tiled=True,
    ).astype(jnp.float32)
    outputs = (middle + ffn_branch + outer_bias).astype(jnp.bfloat16)
    grad_full = gather_grads(cotangent)
    outer_part = contract_rows(hidden_act, grad_full)
    hidden_grad = contract_cols(grad_full, outer_weight)
    gelu_pull = jax.vjp(lambda pre_act: jax.nn.gelu(pre_act, approximate=True), inner_pre)[1]
    inner_grad = gelu_pull(hidden_grad)[0].astype(jnp.bfloat16)
    inner_part = contract_rows(second_normed, inner_grad)
    bias_part = jnp.sum(inner_grad.astype(jnp.float32), axis=0)
    second_grad = sum_inputs(contract_cols(inner_grad, inner_weight))
    second_resid, second_gain_grad, second_shift_grad = norm_back(
        second_grad, second_unit, second_inverse, second_gain
    )
    middle_grad = grad_top + second_resid
    branch_full = gather_grads(middle_grad.astype(jnp.bfloat16))
    output_part = contract_rows(merged, branch_full)
    merged_grad = jnp.where(
        live_rows,
        contract_cols(branch_full, output_weight).astype(jnp.bfloat16),
        jnp.zeros((), jnp.bfloat16),
    )
    query_grads, key_grads, value_grads = lax.map(
        attend_backward,
        (query_heads, key_heads, value_heads)
        + group_info
        + (split_heads(merged_grad), log_total, global_log),
    )
    packed_grad = jnp.concatenate(
        [join_heads(query_grads), join_heads(key_grads), join_heads(value_grads)], axis=1
    )
    joint_grad = contract_rows(packed_grad, first_normed)
    query_part = joint_grad[:local_width]
    key_part = joint_grad[local_width : 2 * local_width]
    value_part = joint_grad[2 * local_width :]
    first_grad = sum_inputs(jnp.dot(packed_grad, joint_weight, preferred_element_type=jnp.float32))
    first_resid, first_gain_grad, first_shift_grad = norm_back(
        first_grad, first_unit, first_inverse, first_gain
    )
    input_grad = middle_grad + first_resid
    summed = lax.psum(
        (query_part, key_part, value_part, output_part, inner_part, outer_part, bias_part), "dp"
    )
    vectors = lax.psum(
        (
            jnp.sum(grad_top, axis=0),
            first_gain_grad,
            first_shift_grad,
            second_gain_grad,
            second_shift_grad,
        ),
        ("dp", "tensor"),
    )
    return (
        outputs,
        input_grad,
        summed[0],
        summed[1],
        summed[2],
        summed[3],
        summed[4],
        summed[6],
        summed[5],
        vectors[0],
        vectors[1],
        vectors[2],
        vectors[3],
        vectors[4],
    )


def solution(mesh):
    placed = (
        P(("dp", "tensor"), None),
        P("tensor", None),
        P("tensor", None),
        P("tensor", None),
        P("tensor", None),
        P(None, "tensor"),
        P("tensor"),
        P("tensor", None),
        P(),
        P(),
        P(),
        P(),
        P(),
        P("dp"),
        P("dp"),
        P("dp", "tensor", None, None),
        P(("dp", "tensor"), None),
    )
    return jax.shard_map(
        per_device,
        mesh=mesh,
        in_specs=placed,
        out_specs=(
            P(("dp", "tensor"), None),
            P(("dp", "tensor"), None),
            P("tensor", None),
            P("tensor", None),
            P("tensor", None),
            P("tensor", None),
            P(None, "tensor"),
            P("tensor"),
            P("tensor", None),
            P(),
            P(),
            P(),
            P(),
            P(),
        ),
        check_vma=False,
    )
```

profile of v0, /device:TPU:18, one launch (start us, length us, event | category | flops | bytes accessed | tf_op | source)
XLA Modules:
  0.0 4006.4 jit_solution(17345301351408476467)
XLA Ops:
  21.9 101.3 %all-gather.5.cloned.1.call-done = bf16[8192,1024]{1,0:T(8,128)(2,1)} async-done(((bf16[2048,1024]{1,0:T(8,128)(2,1)}), bf16[8192,1024]{1,0:T(8,128)(2,1)}) %all-gather.5.cloned.1.call-update) | async-done | bytes 16777232 | tf_op jit(solution)/shard_map/all_gather | solution.py:57
  222.2 549.7 %while.36 = (s32[]{:T(128)}, bf16[8,4096,64]{2,1,0:T(8,128)(2,1)}, f32[8,64,64,1]{2,1,3,0:T(8,128)}, f32[8,128,1]{1,2,0:T(1,128)}, s32[8]{0:T(128)S(1)}, /*index...) while((s32[]{:T(128)}, bf16[8,4096,64]{2,1,0:T(8,128)(2,1)}, ...), condition=%wide.region_8.9_spmd, body=%wide.region_2.8_spmd.sunk | while | flops 1245922688 | bytes 67248432 | solution.py:299
  814.5 235.0 %reduce-scatter.5.cloned.1.call-done = f32[2048,1024]{1,0:T(8,128)} async-done(((f32[8192,1024]{1,0:T(8,128)}), f32[2048,1024]{1,0:T(8,128)}) %reduce-scatter.5.cloned.1.call-update) | async-done | bytes 8388624 | tf_op jit(solution)/shard_map/reduce_scatter | solution.py:304
  1062.4 105.4 %all-gather.7.cloned.1.call-done = bf16[8192,1024]{1,0:T(8,128)(2,1)} async-done(((bf16[2048,1024]{1,0:T(8,128)(2,1)}), bf16[8192,1024]{1,0:T(8,128)(2,1)}) %all-gather.7.cloned.1.call-update) | async-done | bytes 16777232 | tf_op jit(solution)/shard_map/all_gather | solution.py:57
  1167.9 26.9 fusion.129
  1194.8 80.5 %all-gather.9.cloned.1.call-done = bf16[8192,1024]{1,0:T(8,128)(2,1)} async-done(((bf16[2048,1024]{1,0:T(8,128)(2,1)}), bf16[8192,1024]{1,0:T(8,128)(2,1)}) %all-gather.9.cloned.1.call-update) | async-done | bytes 16777232 | tf_op jit(solution)/shard_map/all_gather | solution.py:69
  1275.2 50.0 %convert_reduce_fusion = (f32[1024]{0:T(1024)}, bf16[8192,1024]{1,0:T(8,128)(2,1)}, bf16[8192,1024]{1,0:T(8,128)(2,1)}) fusion(f32[8192,1024]{1,0:T(8,128)} %fusion.129, f32[1024]{0:T(1024)S(1)} %copy-done.51, bf16[8192,1024]{1,0:T(8,128)(2,1)} %all-gather.9.cloned.1.call-done, bf16[1024,1024]{1,0:T(8,128)(2,1)S(1)} %copy-done), kind=kOutput, calls=%fused_computation.171 | convolution fusion | flops 17389584384 | bytes 85991424 | tf_op jit(solution)/shard_map/dot_general | solution.py:18
  1325.2 26.4 fusion.130
  1351.7 26.5 convolution_convert_fusion.4
  1378.3 208.5 %reduce-scatter.9.cloned.1.call-done = f32[2048,1024]{1,0:T(8,128)} async-done(((f32[8192,1024]{1,0:T(8,128)}), f32[2048,1024]{1,0:T(8,128)}) %reduce-scatter.9.cloned.1.call-update) | async-done | bytes 8388624 | tf_op jit(solution)/shard_map/reduce_scatter | solution.py:73
  1595.1 120.3 %reduce-scatter.7.cloned.1.call-done = bf16[2048,1024]{1,0:T(8,128)(2,1)} async-done(((bf16[8192,1024]{1,0:T(8,128)(2,1)}), bf16[2048,1024]{1,0:T(8,128)(2,1)}) %reduce-scatter.7.cloned.1.call-update) | async-done | bytes 4194320 | tf_op jit(solution)/shard_map/reduce_scatter | solution.py:316
  1732.6 106.0 %all-gather.11.cloned.1.call-done = bf16[8192,1024]{1,0:T(8,128)(2,1)} async-done(((bf16[2048,1024]{1,0:T(8,128)(2,1)}), bf16[8192,1024]{1,0:T(8,128)(2,1)}) %all-gather.11.cloned.1.call-update) | async-done | bytes 16777232 | tf_op jit(solution)/shard_map/all_gather | solution.py:69
  1869.3 1392.9 %while.37 = (s32[]{:T(128)}, bf16[8,4096,64]{2,1,0:T(8,128)(2,1)}, bf16[8,4096,64]{1,2,0:T(8,128)(2,1)}, bf16[8,4096,64]{1,2,0:T(8,128)(2,1)}, s32[8]{0:T(128)S(...) while((s32[]{:T(128)}, bf16[8,4096,64]{2,1,0:T(8,128)(2,1)}, ...), condition=%wide.region_20.21_spmd, body=%wide.region_16.20_spmd.sunk | while | flops 5485024768 | bytes 269683680 | solution.py:342
  1977.0 22.0 fusion.259
  2017.1 22.1 fusion.262
  2150.1 22.0 fusion.259
  2190.2 22.3 fusion.262
  2323.4 22.0 fusion.259
  2363.6 22.0 fusion.262
  2536.7 22.1 fusion.262
  2669.8 22.0 fusion.259
  2709.9 22.3 fusion.262
  2883.3 22.0 fusion.262
  3056.4 22.1 fusion.262
  3189.4 22.0 fusion.259
  3229.6 22.3 fusion.262
  3317.3 22.6 fusion.131
  3339.9 25.4 fusion.134
  3365.3 26.7 fusion.133
  3443.2 131.7 %reduce-scatter.11.cloned.1.call-done = f32[2048,1024]{1,0:T(8,128)} async-done(((f32[8192,1024]{1,0:T(8,128)}), f32[2048,1024]{1,0:T(8,128)}) %reduce-scatter.11.cloned.1.call-update) | async-done | bytes 8388624 | tf_op jit(solution)/shard_map/reduce_scatter | solution.py:73
  3581.3 46.1 %all-reduce = (f32[1024]{0:T(1024)}, f32[1024]{0:T(1024)}, f32[1024]{0:T(1024)}, f32[1024]{0:T(1024)}, f32[1024]{0:T(1024)}) all-reduce(f32[1024]{0:T(1024)S(1)} %copy-done.44, f32[1024]{0:T(1024)S(1)} %get-tuple-element.498, f32[1024]{0:T(1024)S(1)} %get-tuple-element.503, ...), channel_id=1, replica_groups=mesh['dp'=8,'tensor'=4] {'dp','tensor'}, use_global_device_ids=true, to_apply=%region_33.34 | all-reduce | flops 5120 | bytes 40960 | tf_op jit(solution)/shard_map/psum | solution.py:363
  3639.7 345.6 %all-reduce.4.cloned.1.call-done = (f32[256,1024]{1,0:T(8,128)}, f32[256,1024]{1,0:T(8,128)}, f32[256,1024]{1,0:T(8,128)}, f32[256,1024]{1,0:T(8,128)}, f32[1024,1024]{1,0:T(8,128)}, /*index=5*/f32[1024,1024]{1,0:T(8,128)}) async-done(((f32[256,1024]{1,0:T(8,128)}, f32[256,1024]{1,0:T(8,128)}, f32[256,1024]{1,0:T(8,128)}, f32[256,1024]{1,0:T(8,128)}, f32[1024,1024]{1,0:T(8,128)}, ...) | async-done | bytes 12582928 | tf_op jit(solution)/shard_map/psum | solution.py:360
  (1125 shorter events, 1975.7 us)
Async XLA Ops:
  7.2 1268.1 %copy-start = (bf16[1024,1024]{1,0:T(8,128)(2,1)S(1)}, bf16[1024,1024]{1,0:T(8,128)(2,1)}, u32[]{:S(2)}) copy-start(bf16[1024,1024]{1,0:T(8,128)(2,1)} %param.32) | copy-start | bytes 6291460
  7.2 116.0 %all-gather.5.cloned.1.call-start = ((), (), s32[]{:S(2)}) async-start(), calls=%async_computation.4 | async-start | bytes 20971520 | tf_op jit(solution)/shard_map/all_gather | solution.py:57
  17.0 1032.5 %reduce-scatter.5.cloned.1.call-start = ((), (), s32[]{:S(2)}) async-start(), calls=%async_computation.5 | async-start | bytes 41943040 | tf_op jit(solution)/shard_map/reduce_scatter | solution.py:304
  771.9 21.5 copy-start.19
  814.5 353.4 %all-gather.7.cloned.1.call-start = ((), (), s32[]{:S(2)}) async-start(), calls=%async_computation.6 | async-start | bytes 20971520 | tf_op jit(solution)/shard_map/all_gather | solution.py:57
  1061.8 213.5 %all-gather.9.cloned.1.call-start = ((), (), s32[]{:S(2)}) async-start(), calls=%async_computation.8 | async-start | bytes 20971520 | tf_op jit(solution)/shard_map/all_gather | solution.py:69
  1062.4 212.9 %copy-start.51 = (f32[1024]{0:T(1024)S(1)}, f32[1024]{0:T(1024)}, u32[]{:S(2)}) copy-start(f32[1024]{0:T(1024)} %param.31) | copy-start | bytes 12292
  1062.4 524.4 %reduce-scatter.9.cloned.1.call-start = ((), (), s32[]{:S(2)}) async-start(), calls=%async_computation.9 | async-start | bytes 41943040 | tf_op jit(solution)/shard_map/reduce_scatter | solution.py:73
  1351.6 363.7 %reduce-scatter.7.cloned.1.call-start = ((), (), s32[]{:S(2)}) async-start(), calls=%async_computation.7 | async-start | bytes 20971520 | tf_op jit(solution)/shard_map/reduce_scatter | solution.py:316
  1378.2 208.6 %copy-start.28 = (f32[2048]{0:T(1024)S(1)}, f32[2048]{0:T(1024)}, u32[]{:S(2)}) copy-start(f32[2048]{0:T(1024)} %copy-done.27) | copy-start | bytes 24580
  1378.2 208.6 %copy-start.32 = (f32[2048]{0:T(1024)S(1)}, f32[2048]{0:T(1024)}, u32[]{:S(2)}) copy-start(f32[2048]{0:T(1024)} %copy-done.31) | copy-start | bytes 24580
  1378.2 208.6 %copy-start.40 = (f32[1024]{0:T(1024)S(1)}, f32[1024]{0:T(1024)}, u32[]{:S(2)}) copy-start(f32[1024]{0:T(1024)} %param.36) | copy-start | bytes 12292
  1378.2 337.2 %copy-start.49 = (f32[1024]{0:T(1024)S(1)}, f32[1024]{0:T(1024)}, u32[]{:S(2)}) copy-start(f32[1024]{0:T(1024)} %param.33) | copy-start | bytes 12292
  1378.2 460.3 %all-gather.11.cloned.1.call-start = ((), (), s32[]{:S(2)}) async-start(), calls=%async_computation.10 | async-start | bytes 20971520 | tf_op jit(solution)/shard_map/all_gather | solution.py:69
  1715.4 123.2 %copy-start.22 = (bf16[256,1024]{1,0:T(8,128)(2,1)S(1)}, bf16[256,1024]{1,0:T(8,128)(2,1)}, u32[]{:S(2)}) copy-start(bf16[256,1024]{1,0:T(8,128)(2,1)} %param.29) | copy-start | bytes 1572868
  1715.4 123.2 %copy-start.35 = (pred[8192]{0:T(1024)(128)(4,1)S(1)}, pred[8192]{0:T(1024)(128)(4,1)}, u32[]{:S(2)}) copy-start(pred[8192]{0:T(1024)(128)(4,1)} %lt.184) | copy-start | bytes 24580
  1732.5 1842.4 %reduce-scatter.11.cloned.1.call-start = ((), (), s32[]{:S(2)}) async-start(), calls=%async_computation.11 | async-start | bytes 41943040 | tf_op jit(solution)/shard_map/reduce_scatter | solution.py:73
  1977.0 24.9 copy-start.5
  2150.1 24.9 copy-start.5
  2323.4 24.9 copy-start.5
  2496.6 24.9 copy-start.5
  2669.8 24.9 copy-start.5
  2843.1 24.9 copy-start.5
  3016.2 24.9 copy-start.5
  3189.4 24.9 copy-start.5
  3339.9 645.5 %all-reduce.4.cloned.1.call-start = ((), (), s32[]{:S(2)}) async-start(), calls=%async_computation.12 | async-start | bytes 25165824 | tf_op jit(solution)/shard_map/psum | solution.py:360
  3426.2 148.7 %copy-start.26 = (f32[2048]{0:T(1024)S(1)}, f32[2048]{0:T(1024)}, u32[]{:S(2)}) copy-start(f32[2048]{0:T(1024)} %copy-done.25) | copy-start | bytes 24580
  3426.2 148.7 %copy-start.30 = (f32[2048]{0:T(1024)S(1)}, f32[2048]{0:T(1024)}, u32[]{:S(2)}) copy-start(f32[2048]{0:T(1024)} %copy-done.29) | copy-start | bytes 24580
  3426.2 148.7 %copy-start.38 = (f32[1024]{0:T(1024)S(1)}, f32[1024]{0:T(1024)}, u32[]{:S(2)}) copy-start(f32[1024]{0:T(1024)} %param.34) | copy-start | bytes 12292
  3426.2 155.1 %copy-start.42 = (f32[1024]{0:T(1024)S(1)}, f32[1024]{0:T(1024)}, u32[]{:S(2)}) copy-start(f32[1024]{0:T(1024)} %get-tuple-element.496) | copy-start | bytes 12292
  3426.2 155.1 %copy-start.43 = (f32[1024]{0:T(1024)S(1)}, f32[1024]{0:T(1024)}, u32[]{:S(2)}) copy-start(f32[1024]{0:T(1024)} %get-tuple-element.502) | copy-start | bytes 12292
  3426.2 155.1 %copy-start.44 = (f32[1024]{0:T(1024)S(1)}, f32[1024]{0:T(1024)}, u32[]{:S(2)}) copy-start(f32[1024]{0:T(1024)} %get-tuple-element.598) | copy-start | bytes 12292
  (108 other events, 775.9 us)
Sparse Core Ops, SparseCore 0:
  17.2 106.0 all-gather.4
  814.6 234.8 reduce-scatter.4
  1061.9 105.9 all-gather.6
  1169.3 105.9 all-gather.8
  1351.8 234.9 reduce-scatter.8
  1589.2 126.1 reduce-scatter.6
  1732.6 105.9 all-gather.10
  3340.0 234.8 reduce-scatter.10
  3581.8 403.5 all-reduce.3
where the time goes:
time: 4030 us; the launch traced here: 4010 us
  waiting for transfers between devices  1440 us (36%)
  matrix products  1400 us (35%)
  local copies, waits for them, and re-layouts  862 us (21%)
  other arithmetic  188 us (5%)
  blocking collectives  62.4 us (2%)
  loops' own time  44.2 us (1%)
    psum x1, waiting for transfers between devices, per_device(): lax.psum((query_part, key_part, value_part, output_part, inner_part, oute...  346 us
    reduce_scatter x2, waiting for transfers between devices, sum_inputs(): return lax.psum_scatter(term, 'tensor', scatter_dimension=0, tiled=True)  340 us
    reduce_scatter x1, waiting for transfers between devices, per_device(): lax.psum_scatter(jnp.dot(merged, output_weight, preferred_element_type=jn...  235 us
    all_gather x2, waiting for transfers between devices, gather_normed(): return lax.all_gather(normed, 'tensor', axis=0, tiled=True)  207 us
    all_gather x2, waiting for transfers between devices, gather_grads(): return lax.all_gather(grad_slice, 'tensor', axis=0, tiled=True)  186 us
    dot_general x8, matrix products, attend_backward(): jnp.einsum('nsm,nsld->mld', select_full, value_slots.reshape(block_count,...  177 us
    dot_general x8, matrix products, attend_backward(): jnp.einsum('nsm,nsld->mld', select_full, key_slots.reshape(block_count, -...  176 us
    dot_general x16, matrix products, sparse_parts(): jnp.einsum('nqd,nkd->nqk', query_blocks, key_blocks, preferred_element_ty...  151 us
  transfers between devices with their start and end apart: 9, of which 9 were waited for; matrix products, arithmetic and copies ran while one was open for 4% of the time, Pallas kernels for 0%

commit v1 on v0

v1 whole, which is shorter than its diff:
```python
import functools

import jax
import jax.numpy as jnp
from jax import lax
from jax.experimental import pallas as pl
from jax.experimental.pallas import tpu as pltpu
from jax.sharding import PartitionSpec as P

EPSILON = 1e-05
MASKED = -1e30
LOG2E = 1.4426950408889634
SHARED = 5
KEY_CHUNK = 512
MEGA = 2**20


def contract_rows(left, right):
    return lax.dot_general(
        left, right, (((0,), (0,)), ((), ())), preferred_element_type=jnp.float32
    )


def contract_cols(left, right):
    return lax.dot_general(
        left, right, (((1,), (1,)), ((), ())), preferred_element_type=jnp.float32
    )


def matmul(left, right):
    return lax.dot_general(
        left, right, (((1,), (0,)), ((), ())), preferred_element_type=jnp.float32
    )


def block_lists(blocks_used, random_pick):
    block_count = random_pick.shape[0]
    places = jnp.arange(block_count, dtype=jnp.int32)[:, None]
    fixed_cols = jnp.zeros_like(places)
    chosen = jnp.concatenate(
        [
            places - 1,
            places,
            places + 1,
            fixed_cols,
            fixed_cols + blocks_used - 1,
            random_pick % blocks_used,
        ],
        axis=1,
    )
    inside = (chosen >= 0) & (chosen < blocks_used)
    slot_count = chosen.shape[1]
    before = jnp.arange(slot_count)[:, None] < jnp.arange(slot_count)[None, :]
    repeated = jnp.any(
        (chosen[:, :, None] == chosen[:, None, :]) & inside[:, :, None] & before[None], axis=1
    )
    return (jnp.clip(chosen, 0, block_count - 1), inside & jnp.logical_not(repeated))


def norm_rows(resid, gain, shift):
    center = jnp.mean(resid, axis=1, keepdims=True)
    deviation = resid - center
    inverse = lax.rsqrt(jnp.mean(deviation * deviation, axis=1, keepdims=True) + EPSILON)
    unit_rows = deviation * inverse
    normed = (unit_rows * gain + shift).astype(jnp.bfloat16)
    return (normed, unit_rows, inverse)


def norm_back(grad_normed, unit_rows, inverse, gain):
    scaled = grad_normed * gain
    plain_mean = jnp.mean(scaled, axis=1, keepdims=True)
    cross_mean = jnp.mean(scaled * unit_rows, axis=1, keepdims=True)
    resid_grad = inverse * (scaled - plain_mean - unit_rows * cross_mean)
    return (resid_grad, jnp.sum(grad_normed * unit_rows, axis=0), jnp.sum(grad_normed, axis=0))


class Shape:
    def __init__(self, span, heads, head_size, blocks, slots):
        self.span, self.heads, self.head_size, self.blocks, self.slots = (
            span,
            heads,
            head_size,
            blocks,
            slots,
        )
        self.length = span // blocks
        self.lanes = heads * head_size
        self.columns = heads * self.length
        self.wide = max(1, min(heads, 128 // head_size))
        self.tile = self.wide * head_size
        self.chunk = min(KEY_CHUNK, span)
        self.bias_lanes = min(128, self.columns)


def rows_of(index, length):
    return pl.ds(pl.multiple_of(index * length, length), length)


def spread_heads(block, sh):
    lane = lax.broadcasted_iota(jnp.int32, block.shape, 1) // sh.head_size
    zero = jnp.zeros_like(block)
    return jnp.concatenate([jnp.where(lane == h, block, zero) for h in range(sh.heads)], axis=0)


def pick_heads(stacked, sh):
    lane = lax.broadcasted_iota(jnp.int32, (sh.length, sh.lanes), 1) // sh.head_size
    out = stacked[: sh.length]
    for h in range(1, sh.heads):
        out = jnp.where(lane == h, stacked[h * sh.length : (h + 1) * sh.length], out)
    return out


def mixed_slot(load, idx, j, s, sh):
    cols = []
    for t in range(sh.heads // sh.wide):
        out = None
        for i in range(sh.wide):
            at = idx[((t * sh.wide + i) * sh.blocks + j) * sh.slots + s]
            piece = load(rows_of(at, sh.length), t)
            if i == 0:
                out = piece
            else:
                lane = lax.broadcasted_iota(jnp.int32, piece.shape, 1) // sh.head_size
                out = jnp.where(lane == i, piece, out)
        cols.append(out)
    return cols[0] if len(cols) == 1 else jnp.concatenate(cols, axis=1)


def gather_rows(ref, first, idx, j, sh):
    parts = [
        ref[rows_of(idx[j * sh.slots + s], sh.length), first : first + sh.lanes]
        for s in range(SHARED)
    ]

    def load(rows, t):
        return ref[rows, first + t * sh.tile : first + (t + 1) * sh.tile]

    for s in range(SHARED, sh.slots):
        parts.append(mixed_slot(load, idx, j, s, sh))
    return jnp.concatenate(parts, axis=0)


def widen(bias, sh):
    reps = sh.columns // sh.bias_lanes
    return bias if reps == 1 else jnp.concatenate([bias] * reps, axis=1)


def gather_bias(ref, idx, j, sh):
    parts = [
        widen(ref[rows_of(idx[j * sh.slots + s], sh.length), : sh.bias_lanes], sh)
        for s in range(SHARED)
    ]

    def load(rows, t):
        return ref[rows, : sh.bias_lanes]

    for s in range(SHARED, sh.slots):
        parts.append(mixed_slot(load, idx, j, s, sh))
    return jnp.concatenate(parts, axis=0)


def scatter_rows(ref, value, idx, j, sh):
    length, tile = sh.length, sh.tile
    for s in range(SHARED):
        ref[rows_of(idx[j * sh.slots + s], length), :] += value[s * length : (s + 1) * length]
    for s in range(SHARED, sh.slots):
        for h in range(sh.heads):
            t, i = h // sh.wide, h % sh.wide
            at = rows_of(idx[(h * sh.blocks + j) * sh.slots + s], length)
            piece = value[s * length : (s + 1) * length, t * tile : (t + 1) * tile]
            if sh.wide > 1:
                lane = lax.broadcasted_iota(jnp.int32, piece.shape, 1) // sh.head_size
                piece = jnp.where(lane == i, piece, 0.0)
            ref[at, t * tile : (t + 1) * tile] += piece


def each_block(count, unroll, block):
    def many(i, carry):
        for u in range(unroll):
            block(1 + i * unroll + u)
        return carry

    lax.fori_loop(0, count // unroll, many, 0)

    def one(j, carry):
        block(j)
        return carry

    lax.fori_loop(1 + count // unroll * unroll, 1 + count, one, 0)


def forward_kernel(sh, pieces, unroll, used, member, idx, bidx, *refs):
    packed, bias_ref = refs[:pieces], refs[pieces]
    outs = refs[pieces + 1 : 2 * pieces + 1]
    rows, o_scr, s_scr, sems = refs[2 * pieces + 1 :]
    c = used[0]
    scale = sh.head_size ** (-0.5) * LOG2E
    rows_each = sh.span // pieces
    query, key, value = 0, sh.lanes, 2 * sh.lanes

    def place(r):
        return rows_of(lax.rem(member[0] + r, pieces), rows_each)

    loads = [pltpu.make_async_copy(packed[r], rows.at[place(r)], sems.at[r]) for r in range(pieces)]
    for copy in loads:
        copy.start()
    o_scr[...] = jnp.zeros_like(o_scr)
    for copy in loads:
        copy.wait()

    def block(j):
        at = rows_of(j, sh.length)
        q_all = spread_heads(rows[at, query : query + sh.lanes], sh)
        scores = contract_cols(gather_rows(rows, key, idx, j, sh), q_all) * scale
        scores = scores + gather_bias(bias_ref, bidx, j, sh)
        shifted = jnp.exp2(scores - jnp.max(scores, axis=0, keepdims=True))
        inverse = 1.0 / jnp.sum(shifted, axis=0, keepdims=True)
        probs = (shifted * inverse).astype(jnp.bfloat16)
        out = pick_heads(contract_rows(probs, gather_rows(rows, value, idx, j, sh)), sh)
        o_scr[at, :] = out.astype(o_scr.dtype)

    each_block(c - 2, unroll, block)

    chunks = pl.cdiv(c * sh.length, sh.chunk)
    line = (1, sh.columns)
    for j in (0, c - 1):
        at = rows_of(j, sh.length)
        q_all = spread_heads(rows[at, query : query + sh.lanes], sh)

        def first(i, top):
            keys = rows_of(i, sh.chunk)
            scores = contract_cols(rows[keys, key : key + sh.lanes], q_all) * scale
            scores = scores + widen(bias_ref[keys, : sh.bias_lanes], sh)
            s_scr[keys, :] = scores
            return jnp.maximum(top, jnp.max(scores, axis=0, keepdims=True))

        top = lax.fori_loop(0, chunks, first, jnp.full(line, MASKED, jnp.float32))

        def second(i, total):
            keys = rows_of(i, sh.chunk)
            shifted = jnp.exp2(s_scr[keys, :] - top)
            s_scr[keys, :] = shifted
            return total + jnp.sum(shifted, axis=0, keepdims=True)

        inverse = 1.0 / lax.fori_loop(0, chunks, second, jnp.zeros(line, jnp.float32))

        def third(i, total):
            keys = rows_of(i, sh.chunk)
            probs = (s_scr[keys, :] * inverse).astype(jnp.bfloat16)
            return total + contract_rows(probs, rows[keys, value : value + sh.lanes])

        total = lax.fori_loop(0, chunks, third, jnp.zeros((sh.columns, sh.lanes), jnp.float32))
        o_scr[at, :] = pick_heads(total, sh).astype(o_scr.dtype)

    stores = [
        pltpu.make_async_copy(o_scr.at[place(r)], outs[r], sems.at[pieces + r])
        for r in range(pieces)
    ]
    for copy in stores:
        copy.start()
    for copy in stores:
        copy.wait()


def backward_kernel(sh, pieces, unroll, used, member, idx, bidx, *refs):
    packed, tops, bias_ref = refs[:pieces], refs[pieces : 2 * pieces], refs[2 * pieces]
    outs = refs[2 * pieces + 1 : 3 * pieces + 1]
    rows, grads, d_scr, ka_scr, va_scr, s_scr, p_scr, sems = refs[3 * pieces + 1 :]
    c = used[0]
    factor = sh.head_size ** (-0.5)
    scale = factor * LOG2E
    rows_each = sh.span // pieces
    query, key, value = 0, sh.lanes, 2 * sh.lanes

    def place(r):
        return rows_of(lax.rem(member[0] + r, pieces), rows_each)

    loads = [pltpu.make_async_copy(packed[r], rows.at[place(r)], sems.at[r]) for r in range(pieces)]
    loads += [
        pltpu.make_async_copy(tops[r], grads.at[place(r)], sems.at[pieces + r])
        for r in range(pieces)
    ]
    for copy in loads:
        copy.start()
    d_scr[:, : sh.lanes] = jnp.zeros((sh.span, sh.lanes), d_scr.dtype)
    ka_scr[...] = jnp.zeros_like(ka_scr)
    va_scr[...] = jnp.zeros_like(va_scr)
    for copy in loads:
        copy.wait()

    def block(j):
        at = rows_of(j, sh.length)
        q_all = spread_heads(rows[at, query : query + sh.lanes], sh)
        g_all = spread_heads(grads[at, :], sh)
        k_all = gather_rows(rows, key, idx, j, sh)
        scores = contract_cols(k_all, q_all) * scale + gather_bias(bias_ref, bidx, j, sh)
        prob_grad = contract_cols(gather_rows(rows, value, idx, j, sh), g_all)
        shifted = jnp.exp2(scores - jnp.max(scores, axis=0, keepdims=True))
        probs = shifted * (1.0 / jnp.sum(shifted, axis=0, keepdims=True))
        delta = jnp.sum(probs * prob_grad, axis=0, keepdims=True)
        score_grad = (probs * (prob_grad - delta)).astype(jnp.bfloat16)
        query_grad = pick_heads(contract_rows(score_grad, k_all), sh) * factor
        d_scr[at, : sh.lanes] = query_grad.astype(d_scr.dtype)
        scatter_rows(ka_scr, matmul(score_grad, q_all), idx, j, sh)
        scatter_rows(va_scr, matmul(probs.astype(jnp.bfloat16), g_all), idx, j, sh)

    each_block(c - 2, unroll, block)

    chunks = pl.cdiv(c * sh.length, sh.chunk)
    line = (1, sh.columns)
    for j in (0, c - 1):
        at = rows_of(j, sh.length)
        q_all = spread_heads(rows[at, query : query + sh.lanes], sh)
        g_all = spread_heads(grads[at, :], sh)

        def first(i, carry):
            top, total, cross = carry
            keys = rows_of(i, sh.chunk)
            scores = contract_cols(rows[keys, key : key + sh.lanes], q_all) * scale
            scores = scores + widen(bias_ref[keys, : sh.bias_lanes], sh)
            prob_grad = contract_cols(rows[keys, value : value + sh.lanes], g_all)
            s_scr[keys, :] = scores
            p_scr[keys, :] = prob_grad
            higher = jnp.maximum(top, jnp.max(scores, axis=0, keepdims=True))
            shifted = jnp.exp2(scores - higher)
            fade = jnp.exp2(top - higher)
            return (
                higher,
                total * fade + jnp.sum(shifted, axis=0, keepdims=True),
                cross * fade + jnp.sum(shifted * prob_grad, axis=0, keepdims=True),
            )

        zero = jnp.zeros(line, jnp.float32)
        top, total, cross = lax.fori_loop(
            0, chunks, first, (jnp.full(line, MASKED, jnp.float32), zero, zero)
        )
        inverse = 1.0 / total
        delta = cross * inverse

        def second(i, total):
            keys = rows_of(i, sh.chunk)
            probs = jnp.exp2(s_scr[keys, :] - top) * inverse
            score_grad = (probs * (p_scr[keys, :] - delta)).astype(jnp.bfloat16)
            ka_scr[keys, :] += matmul(score_grad, q_all)
            va_scr[keys, :] += matmul(probs.astype(jnp.bfloat16), g_all)
            return total + contract_rows(score_grad, rows[keys, key : key + sh.lanes])

        total = lax.fori_loop(0, chunks, second, jnp.zeros((sh.columns, sh.lanes), jnp.float32))
        d_scr[at, : sh.lanes] = (pick_heads(total, sh) * factor).astype(d_scr.dtype)

    d_scr[:, key : key + sh.lanes] = (ka_scr[...] * factor).astype(d_scr.dtype)
    d_scr[:, value : value + sh.lanes] = va_scr[...].astype(d_scr.dtype)
    stores = [
        pltpu.make_async_copy(d_scr.at[place(r)], outs[r], sems.at[2 * pieces + r])
        for r in range(pieces)
    ]
    for copy in stores:
        copy.start()
    for copy in stores:
        copy.wait()


ANYWHERE = pl.BlockSpec(memory_space=pl.ANY)
ON_CHIP = pl.BlockSpec(memory_space=pltpu.VMEM)
SCALARS = pl.BlockSpec(memory_space=pltpu.SMEM)


def attend_cost(sh, products):
    flops = products * 2 * (sh.blocks + 2 * sh.blocks // sh.slots) * sh.length * sh.slots
    flops *= sh.length * sh.head_size * sh.heads * 4
    return pl.CostEstimate(flops=flops, bytes_accessed=16 * sh.span * sh.lanes, transcendentals=0)


def attend_forward(sh, packed, lists, unroll=4):
    pieces = len(packed)
    used, member, idx, bidx, bias = lists
    rows_each = sh.span // pieces
    return pl.pallas_call(
        functools.partial(forward_kernel, sh, pieces, unroll),
        in_specs=[SCALARS] * 4 + [ANYWHERE] * pieces + [ON_CHIP],
        out_specs=[ANYWHERE] * pieces,
        out_shape=[jax.ShapeDtypeStruct((rows_each, sh.lanes), jnp.bfloat16)] * pieces,
        scratch_shapes=[
            pltpu.VMEM((sh.span, 3 * sh.lanes), jnp.bfloat16),
            pltpu.VMEM((sh.span, sh.lanes), jnp.bfloat16),
            pltpu.VMEM((sh.span, sh.columns), jnp.float32),
            pltpu.SemaphoreType.DMA((2 * pieces,)),
        ],
        compiler_params=pltpu.CompilerParams(vmem_limit_bytes=40 * MEGA),
        cost_estimate=attend_cost(sh, 2),
        name="attend_forward",
    )(used, member, idx, bidx, *packed, bias)


def attend_backward(sh, packed, tops, lists, unroll=2):
    pieces = len(packed)
    used, member, idx, bidx, bias = lists
    rows_each = sh.span // pieces
    return pl.pallas_call(
        functools.partial(backward_kernel, sh, pieces, unroll),
        in_specs=[SCALARS] * 4 + [ANYWHERE] * (2 * pieces) + [ON_CHIP],
        out_specs=[ANYWHERE] * pieces,
        out_shape=[jax.ShapeDtypeStruct((rows_each, 3 * sh.lanes), jnp.bfloat16)] * pieces,
        scratch_shapes=[
            pltpu.VMEM((sh.span, 3 * sh.lanes), jnp.bfloat16),
            pltpu.VMEM((sh.span, sh.lanes), jnp.bfloat16),
            pltpu.VMEM((sh.span, 3 * sh.lanes), jnp.bfloat16),
            pltpu.VMEM((sh.span, sh.lanes), jnp.float32),
            pltpu.VMEM((sh.span, sh.lanes), jnp.float32),
            pltpu.VMEM((sh.span, sh.columns), jnp.float32),
            pltpu.VMEM((sh.span, sh.columns), jnp.float32),
            pltpu.SemaphoreType.DMA((3 * pieces,)),
        ],
        compiler_params=pltpu.CompilerParams(vmem_limit_bytes=56 * MEGA),
        cost_estimate=attend_cost(sh, 5),
        name="attend_backward",
    )(used, member, idx, bidx, *packed, *tops, bias)


def low(values):
    return values.astype(jnp.bfloat16)


def full(values):
    return values.astype(jnp.float32)


def swap(values, bit):
    size = lax.axis_size("dp")
    return lax.ppermute(values, "dp", [(i, i ^ bit) for i in range(size)])


def halve(values, bit):
    half = values.shape[0] // 2
    upper = (lax.axis_index("dp") // bit) % 2
    mine = lax.dynamic_slice_in_dim(values, upper * half, half, 0)
    theirs = lax.dynamic_slice_in_dim(values, (1 - upper) * half, half, 0)
    return low(full(mine) + full(swap(theirs, bit)))


def double(values, bit):
    upper = (lax.axis_index("dp") // bit) % 2
    other = swap(values, bit)
    return jnp.where(
        upper == 0,
        jnp.concatenate([values, other], axis=0),
        jnp.concatenate([other, values], axis=0),
    )


def sum_groups(values):
    bits = [1 << i for i in range(lax.axis_size("dp").bit_length() - 1)]
    orders = [bits, bits[1:2] + bits[:1] + bits[2:]]
    part = values.shape[0] // len(orders)
    sums = []
    for i, order in enumerate(orders):
        total = low(values[i * part : (i + 1) * part])
        for bit in order:
            total = halve(total, bit)
        for bit in order[::-1]:
            total = double(total, bit)
        sums.append(total)
    return jnp.concatenate(sums, axis=0).astype(jnp.float32)


def per_device(
    inputs,
    query_weight,
    key_weight,
    value_weight,
    output_weight,
    inner_weight,
    inner_bias,
    outer_weight,
    outer_bias,
    first_gain,
    first_shift,
    second_gain,
    second_shift,
    item_lengths,
    key_mask,
    random_blocks,
    cotangent,
):
    tensor = lax.axis_size("tensor")
    items = item_lengths.shape[0]
    local_rows, model = inputs.shape
    span = local_rows * tensor // items
    members = tensor // items
    place = lax.axis_index("tensor")
    item, member = place // members, place % members
    heads, blocks = random_blocks.shape[1], random_blocks.shape[2]
    lanes = query_weight.shape[0]
    length = span // blocks
    sh = Shape(span, heads, lanes // heads, blocks, SHARED + random_blocks.shape[3])

    def from_item(values, step):
        if step % items == 0:
            return values
        pairs = [
            (t, (t // members - step) % items * members + t % members) for t in range(tensor)
        ]
        return lax.ppermute(values, "tensor", pairs)

    def from_member(values, step):
        if step % members == 0:
            return values
        pairs = [
            (t, t // members * members + (t % members - step) % members) for t in range(tensor)
        ]
        return lax.ppermute(values, "tensor", pairs)

    joint = jnp.concatenate([query_weight, key_weight, value_weight], axis=0)
    joint_item = [from_item(joint, s) for s in range(items)]
    out_item = [from_item(output_weight, s) for s in range(items)]
    inner_item = [from_item(inner_weight, s) for s in range(items)]
    outer_item = [from_item(outer_weight, s) for s in range(items)]
    order = [(s, r) for s in range(items) for r in range(members)]

    def gather(parts):
        return [from_member(parts[s], -r) for s, r in order]

    resid = inputs.astype(jnp.float32)
    grad_top = cotangent.astype(jnp.float32)
    first_own, first_unit, first_inverse = norm_rows(resid, first_gain, first_shift)
    first_all = [from_member(first_own, r) for r in range(members)]
    packed = [
        [low(contract_cols(first_all[r], joint_item[s])) for r in range(members)]
        for s in range(items)
    ]

    used = lax.dynamic_index_in_dim(item_lengths, item, 0, False) // length
    flags = lax.dynamic_index_in_dim(key_mask.reshape(items, span), item, 0, False)
    key_ok = (jnp.arange(span, dtype=jnp.int32) < used * length) & (flags == 1)
    bias = jnp.where(jnp.concatenate([key_ok, jnp.zeros((length,), bool)]), 0.0, MASKED)
    bias = jnp.broadcast_to(bias.astype(jnp.float32)[:, None], (span + length, 128))

    def lists_of(s):
        picks = from_item(
            lax.dynamic_index_in_dim(random_blocks, (item - s) % items, 0, False), s
        )
        chosen, usable = jax.vmap(lambda pick: block_lists(used, pick))(picks)
        marked = jnp.where(usable, chosen, blocks)
        return (used.reshape(1), member.reshape(1), chosen.reshape(-1), marked.reshape(-1), bias)

    lists = [lists_of(s) for s in range(items)]

    merged = []
    for s in range(items):
        outs = attend_forward(sh, packed[s], lists[s])
        merged += [from_member(outs[r], -r) for r in range(members)]
    merged = jnp.concatenate(merged, axis=1)

    out_full = jnp.concatenate(gather(out_item), axis=0)
    inner_full = jnp.concatenate(gather(inner_item), axis=1)
    outer_full = jnp.concatenate(gather(outer_item), axis=0)
    biases = lax.all_gather(inner_bias, "tensor", axis=0)
    spots = jnp.stack([(item + s) % items * members + (member - r) % members for s, r in order])
    bias_full = jnp.concatenate(
        [lax.dynamic_index_in_dim(biases, spots[i], 0, False) for i in range(tensor)]
    )

    middle = resid + matmul(merged, out_full)
    second_own, second_unit, second_inverse = norm_rows(middle, second_gain, second_shift)
    inner_pre = matmul(second_own, inner_full) + bias_full
    hidden_act = low(jax.nn.gelu(inner_pre, approximate=True))
    outputs = low(middle + matmul(hidden_act, outer_full) + outer_bias)

    outer_part = contract_rows(hidden_act, cotangent)
    hidden_grad = contract_cols(cotangent, outer_full)
    gelu_pull = jax.vjp(lambda pre_act: jax.nn.gelu(pre_act, approximate=True), inner_pre)[1]
    inner_grad = low(gelu_pull(hidden_grad)[0])
    inner_part = contract_rows(inner_grad, second_own)
    bias_part = jnp.sum(inner_grad.astype(jnp.float32), axis=0)
    second_grad = contract_cols(inner_grad, inner_full)
    second_resid, second_gain_grad, second_shift_grad = norm_back(
        second_grad, second_unit, second_inverse, second_gain
    )
    middle_grad = grad_top + second_resid
    branch = low(middle_grad)
    output_part = contract_rows(merged, branch)
    merged_grad = low(contract_cols(branch, out_full))

    tops = [[None] * members for _ in range(items)]
    for i, (s, r) in enumerate(order):
        tops[s][r] = from_member(merged_grad[:, i * lanes : (i + 1) * lanes], r)
    packed_grad = [None] * items
    for s in range(items - 1, -1, -1):
        packed_grad[s] = attend_backward(sh, packed[s], tops[s], lists[s])

    def collect(parts):
        totals = []
        for s in range(items):
            total = parts[s * members]
            for r in range(1, members):
                total = total + full(from_member(low(parts[s * members + r]), r))
            totals.append(total)
        return collect_items(totals)

    def collect_items(totals):
        total = totals[0]
        for s in range(1, items):
            total = total + full(from_item(low(totals[s]), -s))
        return total

    def split(values):
        return [values[i * lanes_of : (i + 1) * lanes_of] for i in range(tensor)]

    lanes_of = outer_weight.shape[0]
    outer_grad = sum_groups(collect(split(outer_part)))
    inner_grad_sum = sum_groups(collect(split(inner_part))).T
    lanes_of = lanes
    output_grad = collect(split(output_part))

    joint_parts = []
    for s in range(items):
        total = contract_rows(packed_grad[s][0], first_all[0])
        for r in range(1, members):
            total = total + contract_rows(packed_grad[s][r], first_all[r])
        joint_parts.append(total)
    joint_grad = collect_items(joint_parts)
    attention_grad = sum_groups(jnp.concatenate([joint_grad, output_grad], axis=0))

    back = [from_member(packed_grad[s][r], -r) for s, r in order]
    joint_full = jnp.concatenate(gather(joint_item), axis=0)
    first_grad = matmul(jnp.concatenate(back, axis=1), joint_full)
    first_resid, first_gain_grad, first_shift_grad = norm_back(
        first_grad, first_unit, first_inverse, first_gain
    )
    input_grad = middle_grad + first_resid

    bias_parts = bias_part.reshape(tensor, -1)
    bias_own = jnp.zeros_like(bias_parts)
    for i in range(tensor):
        bias_own = lax.dynamic_update_index_in_dim(bias_own, bias_parts[i], spots[i], 0)
    vectors = lax.psum(
        jnp.concatenate(
            [
                jnp.stack(
                    [
                        jnp.sum(grad_top, axis=0),
                        first_gain_grad,
                        first_shift_grad,
                        second_gain_grad,
                        second_shift_grad,
                    ]
                ).reshape(-1),
                bias_own.reshape(-1),
            ]
        ),
        ("dp", "tensor"),
    )
    small = vectors[: 5 * model].reshape(5, model)
    bias_sum = lax.dynamic_index_in_dim(vectors[5 * model :].reshape(tensor, -1), place, 0, False)
    return (
        outputs,
        input_grad,
        attention_grad[:lanes],
        attention_grad[lanes : 2 * lanes],
        attention_grad[2 * lanes : 3 * lanes],
        attention_grad[3 * lanes :],
        inner_grad_sum,
        bias_sum,
        outer_grad,
        small[0],
        small[1],
        small[2],
        small[3],
        small[4],
    )


def solution(mesh):
    placed = (
        P(("dp", "tensor"), None),
        P("tensor", None),
        P("tensor", None),
        P("tensor", None),
        P("tensor", None),
        P(None, "tensor"),
        P("tensor"),
        P("tensor", None),
        P(),
        P(),
        P(),
        P(),
        P(),
        P("dp"),
        P("dp"),
        P("dp", "tensor", None, None),
        P(("dp", "tensor"), None),
    )
    return jax.shard_map(
        per_device,
        mesh=mesh,
        in_specs=placed,
        out_specs=(
            P(("dp", "tensor"), None),
            P(("dp", "tensor"), None),
            P("tensor", None),
            P("tensor", None),
            P("tensor", None),
            P("tensor", None),
            P(None, "tensor"),
            P("tensor"),
            P("tensor", None),
            P(),
            P(),
            P(),
            P(),
            P(),
        ),
        check_vma=False,
    )
```

time: 4030 us -> 1010 us (0.25)
  waiting for transfers between devices: 1440 us -> 161 us
  matrix products: 1400 us -> 274 us
  local copies, waits for them, and re-layouts: 862 us -> 123 us
  starting transfers between devices: 0.55 us -> 195 us
  Pallas kernels: 0 us -> 108 us
  other arithmetic: 188 us -> 80.5 us
  loops' own time: 44.2 us -> 0 us
    dot_general x140 -> x4, matrix products: 1160 us -> 88.5 us  [matmul(): lax.dot_general(left, right, (((1,), (0,)), ((), ())), preferred_element_...]
    reduce_scatter x4 -> x0, waiting for transfers between devices: 695 us -> none  [the longest x2 340 us: sum_inputs(): return lax.psum_scatter(term, 'tensor', scatter_dimension=0, tiled=True)]
    reshape x132 -> x2, local copies, waits for them, and re-layouts: 581 us -> 0.03 us  [the longest x1 0.02 us: per_device(): key_mask.reshape(items, span)]
    all_gather x4 -> x0, waiting for transfers between devices: 393 us -> none  [the longest x2 207 us: gather_normed(): return lax.all_gather(normed, 'tensor', axis=0, tiled=True)]
    psum x1 -> x0, waiting for transfers between devices: 346 us -> none  [per_device(): lax.psum((query_part, key_part, value_part, output_part, inner_part, oute...]
    ppermute x0 -> x66, starting transfers between devices: none -> 195 us  [the longest x36 162 us: swap(): return lax.ppermute(values, 'dp', [(i, i ^ bit) for i in range(size)])]
    ppermute x0 -> x66, waiting for transfers between devices: none -> 161 us  [the longest x9 86.5 us: from_item(): return lax.ppermute(values, 'tensor', pairs)]
    pallas_call x0 -> x4, Pallas kernels: none -> 108 us  [the longest x2 72.7 us: attend_backward(): pl.pallas_call(functools.partial(backward_kernel, sh, pieces, unroll), in...]
  transfers between devices with their start and end apart: 9 -> 66, of which waited for: 9 -> 21; matrix products, arithmetic and copies ran while one was open for 4% -> 28% of each run, Pallas kernels for 0% -> 11%
where the time goes in v1:
time: 1010 us; the launch traced here: 994 us
  matrix products  274 us (27%)
  starting transfers between devices  195 us (19%)
  waiting for transfers between devices  161 us (16%)
  local copies, waits for them, and re-layouts  123 us (12%)
  Pallas kernels  108 us (11%)
  other arithmetic  80.5 us (8%)
  blocking collectives  47.5 us (5%)
    ppermute x36, starting transfers between devices, swap(): return lax.ppermute(values, 'dp', [(i, i ^ bit) for i in range(size)])  162 us
    dot_general x7, matrix products, contract_cols(): lax.dot_general(left, right, (((1,), (1,)), ((), ())), preferred_element_...  102 us
    dot_general x4, matrix products, matmul(): lax.dot_general(left, right, (((1,), (0,)), ((), ())), preferred_element_...  88.5 us
    ppermute x9, waiting for transfers between devices, from_item(): return lax.ppermute(values, 'tensor', pairs)  86.5 us
    dot_general x7, matrix products, contract_rows(): lax.dot_general(left, right, (((0,), (0,)), ((), ())), preferred_element_...  83.9 us
    unnamed x117, local copies, waits for them, and re-layouts  80.4 us
    ppermute x36, waiting for transfers between devices, swap(): return lax.ppermute(values, 'dp', [(i, i ^ bit) for i in range(size)])  72.7 us
    pallas_call x2, Pallas kernels, attend_backward(): pl.pallas_call(functools.partial(backward_kernel, sh, pieces, unroll), in...  72.7 us
  transfers between devices with their start and end apart: 66, of which 21 were waited for; matrix products, arithmetic and copies ran while one was open for 28% of the time, Pallas kernels for 11%

profile of v1, /device:TPU:18, one launch (start us, length us, event | category | flops | bytes accessed | tf_op | source)
XLA Modules:
  0.0 994.5 jit_solution(8962956978199631429)
XLA Ops:
  48.6 6.4 copy.95
  56.0 13.5 %collective-permute-done.6 = bf16[256,1024]{1,0:T(8,128)(2,1)} collective-permute-done((bf16[256,1024]{1,0:T(8,128)(2,1)}, bf16[256,1024]{1,0:T(8,128)(2,1)}, u32[]{:S(2)}, u32[]{:S(2)}) %collective-permute-start.6) | collective-permute-done | bytes 524320 | tf_op jit(solution)/shard_map/ppermute | solution.py:503
  92.2 28.4 %collective-permute-done.9 = bf16[1024,1024]{1,0:T(8,128)(2,1)} collective-permute-done((bf16[1024,1024]{1,0:T(8,128)(2,1)}, bf16[1024,1024]{1,0:T(8,128)(2,1)}, u32[]{:S(2)}, u32[]{:S(2)}) %collective-permute-start.9) | collective-permute-done | bytes 2097184 | tf_op jit(solution)/shard_map/ppermute | solution.py:503
  120.6 44.1 %collective-permute-done.12 = bf16[1024,1024]{1,0:T(8,128)(2,1)} collective-permute-done((bf16[1024,1024]{1,0:T(8,128)(2,1)}, bf16[1024,1024]{1,0:T(8,128)(2,1)}, u32[]{:S(2)}, u32[]{:S(2)}) %collective-permute-start.12) | collective-permute-done | bytes 2097184 | tf_op jit(solution)/shard_map/ppermute | solution.py:503
  185.4 17.7 %attend_forward.2 = (bf16[2048,256]{1,0:T(8,128)(2,1)S(1)}, bf16[2048,256]{1,0:T(8,128)(2,1)S(1)}) custom-call(s32[1]{0:T(128)} %bitcast.1.used, s32[1]{0:T(128)} %bitcast.2.member, s32[2048]{0:T(1024)S(1)} %min.18.idx, s32[2048]{0:T(1024)S(1)} %broadcast_select_fusion.1.bidx, bf16[2048,768]{1,0:T(8,128)(2,1)S(1)} %convolution_convert_fusion.4.refs_0_, ...), custom_call_target="tpu_custom_call" | custom-call | flops 10737418240 | bytes 16777216 | tf_op jit(solution)/shard_map/attend_forward/pallas_call | solution.py:378
  210.0 17.7 %attend_forward.3 = (bf16[2048,256]{1,0:T(8,128)(2,1)S(1)}, bf16[2048,256]{1,0:T(8,128)(2,1)S(1)}) custom-call(s32[1]{0:T(128)} %bitcast.1.used, s32[1]{0:T(128)} %bitcast.2.member, s32[2048]{0:T(1024)S(1)} %min.20.idx, s32[2048]{0:T(1024)S(1)} %broadcast_select_fusion.bidx, bf16[2048,768]{1,0:T(8,128)(2,1)S(1)} %convolution_convert_fusion.2.refs_0_, ...), custom_call_target="tpu_custom_call" | custom-call | flops 10737418240 | bytes 16777216 | tf_op jit(solution)/shard_map/attend_forward/pallas_call | solution.py:378
  242.2 38.4 %multiply_convert_fusion = (bf16[2048,4096]{1,0:T(8,128)(2,1)}, f32[2048,4096]{1,0:T(8,128)}) fusion(f32[4096]{0:T(1024)S(1)} %pad_maximum_fusion.1, bf16[1024,4096]{1,0:T(8,128)(2,1)} %constant_dynamic-update-slice_fusion.11, f32[2048,1024]{0,1:T(8,128)S(1)} %get-tuple-element.136, f32[1024]{0:T(1024)S(1)} %copy-done.41, f32[1024]{0:T(1024)S(1)} %copy-done.35, ...), kind=kOutput, calls=%fused_computation.15 | convolution fusion | flops 17274241024 | bytes 67149824 | tf_op jit(solution)/shard_map/dot_general | solution.py:31
  280.6 47.0 %convert_reduce_fusion = (f32[4096]{0:T(1024)}, bf16[2048,4096]{1,0:T(8,128)(2,1)}) fusion(f32[2048,4096]{1,0:T(8,128)} %get-tuple-element.138, f32[4096]{0:T(1024)S(1)} %pad_maximum_fusion.1, bf16[4096,1024]{1,0:T(8,128)(2,1)} %constant_dynamic-update-slice_fusion.15, bf16[2048,1024]{1,0:T(8,128)(2,1)S(1)} %copy-done.17), kind=kOutput, calls=%fused_computation.14 | convolution fusion | flops 17372803072 | bytes 62947328 | tf_op jit(solution)/shard_map/dot_general | solution.py:25
  327.6 25.0 %fusion.64 = (f32[1024]{0:T(1024)}, f32[2048,1024]{1,0:T(8,128)}) fusion(bf16[2048,4096]{1,0:T(8,128)(2,1)} %get-tuple-element.144, bf16[1024,4096]{1,0:T(8,128)(2,1)} %constant_dynamic-update-slice_fusion.11), kind=kOutput, calls=%fused_computation.219 | convolution fusion | flops 17181966336 | bytes 33558528 | tf_op jit(solution)/shard_map/dot_general | solution.py:25
  352.6 28.4 %fusion.62 = (bf16[4096,1024]{1,0:T(8,128)(2,1)}, f32[4096,1024]{1,0:T(8,128)}) fusion(bf16[2048,4096]{1,0:T(8,128)(2,1)} %get-tuple-element.144, f32[2048,1024]{0,1:T(8,128)} %copy-done.12, f32[1024]{0:T(1024)S(1)} %copy-done.41, f32[1024]{0:T(1024)S(1)} %copy-done.35, f32[2048]{0:T(1024)S(1)} %add_rsqrt_fusion, f32[2048]{0:T(1024)S(1)} %broadcast_multiply_fusion.4), kind=kOutput, calls=%fused_computation.217 | convolution fusion | flops 17194549248 | bytes 50356224 | tf_op jit(solution)/shard_map/dot_general | solution.py:19
  381.0 9.2 copy.96
  390.2 8.3 multiply_reduce_fusion
  399.6 6.7 convert_reduce_fusion.2
  426.3 23.2 %fusion.65 = (bf16[4096,1024]{1,0:T(8,128)(2,1)S(1)}, f32[4096,1024]{1,0:T(8,128)}) fusion(bf16[2048,4096]{1,0:T(8,128)(2,1)} %get-tuple-element.137, bf16[2048,1024]{1,0:T(8,128)(2,1)S(1)} %copy-done.18), kind=kOutput, calls=%fused_computation.220 | convolution fusion | flops 17184063488 | bytes 46137344 | tf_op jit(solution)/shard_map/dot_general | solution.py:19
  453.5 36.4 %attend_backward.3 = (bf16[2048,768]{1,0:T(8,128)(2,1)}, bf16[2048,768]{1,0:T(8,128)(2,1)}) custom-call(s32[1]{0:T(128)} %bitcast.1.used, s32[1]{0:T(128)} %bitcast.2.member, s32[2048]{0:T(1024)} %copy-done.1, s32[2048]{0:T(1024)} %copy-done.4, bf16[2048,768]{1,0:T(8,128)(2,1)} %copy-done.6, bf16[2048,768]{1,0:T(8,128)(2,1)} %copy-done.8, ...), custom_call_target="tpu_custom_call" | custom-call | flops 26843545600 | bytes 16777216 | tf_op jit(solution)/shard_map/attend_backward/pallas_call | solution.py:399
  490.2 6.6 fusion.68
  496.8 6.9 add_convert_fusion.3
  503.8 36.3 %attend_backward.2 = (bf16[2048,768]{1,0:T(8,128)(2,1)}, bf16[2048,768]{1,0:T(8,128)(2,1)}) custom-call(s32[1]{0:T(128)} %bitcast.1.used, s32[1]{0:T(128)} %bitcast.2.member, s32[2048]{0:T(1024)} %copy-done.2, s32[2048]{0:T(1024)} %copy-done.3, bf16[2048,768]{1,0:T(8,128)(2,1)} %copy-done.5, bf16[2048,768]{1,0:T(8,128)(2,1)} %copy-done.7, ...), custom_call_target="tpu_custom_call" | custom-call | flops 26843545600 | bytes 16777216 | tf_op jit(solution)/shard_map/attend_backward/pallas_call | solution.py:399
  540.1 6.4 fusion.66
  555.9 73.4 %collective-permute-start.30 = (bf16[256,1024]{1,0:T(8,128)(2,1)S(1)}, bf16[256,1024]{1,0:T(8,128)(2,1)S(1)}, u32[]{:S(2)}, u32[]{:S(2)}) collective-permute-start(bf16[256,1024]{1,0:T(8,128)(2,1)S(1)} %fusion.44), channel_id=1, source_target_pairs={{0,8},{4,12},{8,0},{12,4},{16,24},{20,28},{24,16},{28,20},{1,9},{5... | collective-permute-start | bytes 1572872 | tf_op jit(solution)/shard_map/ppermute | solution.py:430
  633.7 7.9 collective-permute-done.30
  643.7 7.4 collective-permute-done.31
  658.9 29.8 %collective-permute-start.32 = (bf16[64,1024]{1,0:T(8,128)(2,1)S(1)}, bf16[64,1024]{1,0:T(8,128)(2,1)S(1)}, u32[]{:S(2)}, u32[]{:S(2)}) collective-permute-start(bf16[64,1024]{1,0:T(8,128)(2,1)S(1)} %constant_dynamic-slice_fusion.13), channel_id=1, source_target_pairs={{0,16},{4,20},{8,24},{12,28},{16,0},{20,4},{24,8},{28,12},{1,17},{... | collective-permute-start | bytes 393224 | tf_op jit(solution)/shard_map/ppermute | solution.py:430
  704.5 18.2 %collective-permute-start.38 = (bf16[1024,1024]{1,0:T(8,128)(2,1)}, bf16[1024,1024]{1,0:T(8,128)(2,1)S(1)}, u32[]{:S(2)}, u32[]{:S(2)}) collective-permute-start(bf16[1024,1024]{1,0:T(8,128)(2,1)} %fusion.35), channel_id=1, source_target_pairs={{0,2},{1,3},{2,0},{3,1},{4,6},{5,7},{6,4},{7,5},{8,10},{9,11},{10,... | collective-permute-start | bytes 6291464 | tf_op jit(solution)/shard_map/ppermute | solution.py:503
  722.7 24.7 %add_convert_fusion = bf16[2048,1024]{0,1:T(8,128)(2,1)} fusion(f32[2048,1024]{0,1:T(8,128)} %copy-done.12, bf16[2048,4096]{1,0:T(8,128)(2,1)} %get-tuple-element.137, bf16[4096,1024]{1,0:T(8,128)(2,1)} %constant_dynamic-update-slice_fusion.15, f32[1024]{0:T(1024)S(1)} %copy-done.42), kind=kOutput, calls=%fused_computation.45 | convolution fusion | flops 17186160640 | bytes 37752832 | tf_op jit(solution)/shard_map/dot_general | solution.py:31
  785.0 20.5 %fusion.63 = (f32[1024]{0:T(1024)S(1)}, f32[2048,1024]{1,0:T(8,128)}) fusion(bf16[3072,1024]{1,0:T(8,128)(2,1)} %constant_dynamic-update-slice_fusion.19, bf16[2048,768]{1,0:T(8,128)(2,1)} %collective-permute-done.17, bf16[2048,768]{1,0:T(8,128)(2,1)} %get-tuple-element.28, bf16[2048,768]{1,0:T(8,128)(2,1)} %collective-permute-done.15, ...), kind=kOutput, calls=%fused_computation.218 | convolution fusion | flops 12937329664 | bytes 27267072 | tf_op jit(solution)/shard_map/dot_general | solution.py:31
  805.5 9.3 copy.97
  831.1 8.3 fusion.29
  841.0 41.9 %psum.7 = f32[9216]{0:T(1024)S(1)} all-reduce(f32[9216]{0:T(1024)S(1)} %pad_maximum_fusion), channel_id=1, replica_groups=mesh['dp'=8,'tensor'=4] {'dp','tensor'}, use_global_device_ids=true, to_apply=%region_16.17 | all-reduce | flops 9216 | bytes 73728 | tf_op jit(solution)/shard_map/psum | solution.py:636
  884.1 9.2 copy.101
  922.4 10.5 %collective-permute-done.47 = bf16[64,1024]{1,0:T(8,128)(2,1)S(1)} collective-permute-done((bf16[64,1024]{1,0:T(8,128)(2,1)S(1)}, bf16[64,1024]{1,0:T(8,128)(2,1)S(1)}, u32[]{:S(2)}, u32[]{:S(2)}) %collective-permute-start.47) | collective-permute-done | bytes 131104 | tf_op jit(solution)/shard_map/ppermute | solution.py:430
  972.5 9.6 collective-permute-done.50
  (390 shorter events, 312.2 us)
Async XLA Ops:
  7.1 65.2 %collective-permute-start.18 = (bf16[768,1024]{1,0:T(8,128)(2,1)}, bf16[768,1024]{1,0:T(8,128)(2,1)}, u32[]{:S(2)}, u32[]{:S(2)}) collective-permute-start(bf16[768,1024]{1,0:T(8,128)(2,1)} %get-tuple-element.115), channel_id=1, source_target_pairs={{0,1},{1,0},{2,3},{3,2},{4,5},{5,4},{6,7},{7,6},{8,9},{9,8},{10,11... | collective-permute-start | bytes 4718600 | tf_op jit(solution)/shard_map/ppermute | solution.py:511
  7.1 66.7 %collective-permute-start.3 = (bf16[768,1024]{1,0:T(8,128)(2,1)}, bf16[768,1024]{1,0:T(8,128)(2,1)}, u32[]{:S(2)}, u32[]{:S(2)}) collective-permute-start(bf16[768,1024]{1,0:T(8,128)(2,1)} %get-tuple-element.115), channel_id=1, source_target_pairs={{0,2},{1,3},{2,0},{3,1},{4,6},{5,7},{6,4},{7,5},{8,10},{9,11},{10,... | collective-permute-start | bytes 4718600 | tf_op jit(solution)/shard_map/ppermute | solution.py:503
  7.7 47.4 %collective-permute-start.2 = (s32[4,64,3]{1,2,0:T(4,128)S(1)}, s32[4,64,3]{1,2,0:T(4,128)S(1)}, u32[]{:S(2)}, u32[]{:S(2)}) collective-permute-start(s32[4,64,3]{1,2,0:T(4,128)S(1)} %bitcast.89), channel_id=1, source_target_pairs={{0,2},{1,3},{2,0},{3,1},{4,6},{5,7},{6,4},{7,5},{8,10},{9,11},{10,... | collective-permute-start | bytes 9224 | tf_op jit(solution)/shard_map/ppermute | solution.py:503
  9.2 46.4 %collective-permute-start.5 = (bf16[256,1024]{1,0:T(8,128)(2,1)}, bf16[256,1024]{1,0:T(8,128)(2,1)}, u32[]{:S(2)}, u32[]{:S(2)}) collective-permute-start(bf16[256,1024]{1,0:T(8,128)(2,1)} %param.21), channel_id=1, source_target_pairs={{0,1},{1,0},{2,3},{3,2},{4,5},{5,4},{6,7},{7,6},{8,9},{9,8},{10,11... | collective-permute-start | bytes 1572872 | tf_op jit(solution)/shard_map/ppermute | solution.py:511
  23.4 155.1 %collective-permute-start = (bf16[2048,1024]{0,1:T(8,128)(2,1)}, bf16[2048,1024]{0,1:T(8,128)(2,1)}, u32[]{:S(2)}, u32[]{:S(2)}) collective-permute-start(bf16[2048,1024]{0,1:T(8,128)(2,1)} %fusion.25), channel_id=1, source_target_pairs={{0,1},{1,0},{2,3},{3,2},{4,5},{5,4},{6,7},{7,6},{8,9},{9,8},{10,11... | collective-permute-start | bytes 12582920 | tf_op jit(solution)/shard_map/ppermute | solution.py:511
  55.6 27.1 %collective-permute-start.8 = (bf16[1024,1024]{1,0:T(8,128)(2,1)}, bf16[1024,1024]{1,0:T(8,128)(2,1)}, u32[]{:S(2)}, u32[]{:S(2)}) collective-permute-start(bf16[1024,1024]{1,0:T(8,128)(2,1)} %param.22), channel_id=1, source_target_pairs={{0,1},{1,0},{2,3},{3,2},{4,5},{5,4},{6,7},{7,6},{8,9},{9,8},{10,11... | collective-permute-start | bytes 6291464 | tf_op jit(solution)/shard_map/ppermute | solution.py:511
  71.8 48.8 %collective-permute-start.9 = (bf16[1024,1024]{1,0:T(8,128)(2,1)}, bf16[1024,1024]{1,0:T(8,128)(2,1)}, u32[]{:S(2)}, u32[]{:S(2)}) collective-permute-start(bf16[1024,1024]{1,0:T(8,128)(2,1)} %param.22), channel_id=1, source_target_pairs={{0,2},{1,3},{2,0},{3,1},{4,6},{5,7},{6,4},{7,5},{8,10},{9,11},{10,... | collective-permute-start | bytes 6291464 | tf_op jit(solution)/shard_map/ppermute | solution.py:503
  72.3 92.4 %collective-permute-start.12 = (bf16[1024,1024]{1,0:T(8,128)(2,1)}, bf16[1024,1024]{1,0:T(8,128)(2,1)}, u32[]{:S(2)}, u32[]{:S(2)}) collective-permute-start(bf16[1024,1024]{1,0:T(8,128)(2,1)} %param.24), channel_id=1, source_target_pairs={{0,2},{1,3},{2,0},{3,1},{4,6},{5,7},{6,4},{7,5},{8,10},{9,11},{10,... | collective-permute-start | bytes 6291464 | tf_op jit(solution)/shard_map/ppermute | solution.py:503
  73.8 97.2 %collective-permute-start.11 = (bf16[1024,1024]{1,0:T(8,128)(2,1)}, bf16[1024,1024]{1,0:T(8,128)(2,1)}, u32[]{:S(2)}, u32[]{:S(2)}) collective-permute-start(bf16[1024,1024]{1,0:T(8,128)(2,1)} %param.24), channel_id=1, source_target_pairs={{0,1},{1,0},{2,3},{3,2},{4,5},{5,4},{6,7},{7,6},{8,9},{9,8},{10,11... | collective-permute-start | bytes 6291464 | tf_op jit(solution)/shard_map/ppermute | solution.py:511
  82.7 94.5 %collective-permute-start.19 = (bf16[768,1024]{1,0:T(8,128)(2,1)}, bf16[768,1024]{1,0:T(8,128)(2,1)S(1)}, u32[]{:S(2)}, u32[]{:S(2)}) collective-permute-start(bf16[768,1024]{1,0:T(8,128)(2,1)} %collective-permute-done.3), channel_id=1, source_target_pairs={{0,1},{1,0},{2,3},{3,2},{4,5},{5,4},{6,7},{7,6},{8,9},{9,8},{10,11... | collective-permute-start | bytes 4718600 | tf_op jit(solution)/shard_map/ppermute | solution.py:511
  120.6 107.2 %collective-permute-start.10 = (bf16[1024,1024]{1,0:T(8,128)(2,1)}, bf16[1024,1024]{1,0:T(8,128)(2,1)S(1)}, u32[]{:S(2)}, u32[]{:S(2)}) collective-permute-start(bf16[1024,1024]{1,0:T(8,128)(2,1)} %collective-permute-done.9), channel_id=1, source_target_pairs={{0,1},{1,0},{2,3},{3,2},{4,5},{5,4},{6,7},{7,6},{8,9},{9,8},{10,11... | collective-permute-start | bytes 6291464 | tf_op jit(solution)/shard_map/ppermute | solution.py:511
  164.7 64.7 %collective-permute-start.13 = (bf16[1024,1024]{1,0:T(8,128)(2,1)}, bf16[1024,1024]{1,0:T(8,128)(2,1)S(1)}, u32[]{:S(2)}, u32[]{:S(2)}) collective-permute-start(bf16[1024,1024]{1,0:T(8,128)(2,1)} %collective-permute-done.12), channel_id=1, source_target_pairs={{0,1},{1,0},{2,3},{3,2},{4,5},{5,4},{6,7},{7,6},{8,9},{9,8},{10,11... | collective-permute-start | bytes 6291464 | tf_op jit(solution)/shard_map/ppermute | solution.py:511
  203.1 28.0 %collective-permute-start.1 = (bf16[2048,256]{1,0:T(8,128)(2,1)S(1)}, bf16[2048,256]{1,0:T(8,128)(2,1)S(1)}, u32[]{:S(2)}, u32[]{:S(2)}) collective-permute-start(bf16[2048,256]{1,0:T(8,128)(2,1)S(1)} %get-tuple-element.23), channel_id=1, source_target_pairs={{0,1},{1,0},{2,3},{3,2},{4,5},{5,4},{6,7},{7,6},{8,9},{9,8},{10,11... | collective-permute-start | bytes 3145736 | tf_op jit(solution)/shard_map/ppermute | solution.py:511
  421.2 82.6 %collective-permute-start.14 = (bf16[2048,256]{1,0:T(8,128)(2,1)}, bf16[2048,256]{1,0:T(8,128)(2,1)}, u32[]{:S(2)}, u32[]{:S(2)}) collective-permute-start(bf16[2048,256]{1,0:T(8,128)(2,1)} %get-tuple-element.104), channel_id=1, source_target_pairs={{0,1},{1,0},{2,3},{3,2},{4,5},{5,4},{6,7},{7,6},{8,9},{9,8},{10,11... | collective-permute-start | bytes 3145736 | tf_op jit(solution)/shard_map/ppermute | solution.py:511
  421.2 32.3 %collective-permute-start.16 = (bf16[2048,256]{1,0:T(8,128)(2,1)}, bf16[2048,256]{1,0:T(8,128)(2,1)}, u32[]{:S(2)}, u32[]{:S(2)}) collective-permute-start(bf16[2048,256]{1,0:T(8,128)(2,1)} %get-tuple-element.105), channel_id=1, source_target_pairs={{0,1},{1,0},{2,3},{3,2},{4,5},{5,4},{6,7},{7,6},{8,9},{9,8},{10,11... | collective-permute-start | bytes 3145736 | tf_op jit(solution)/shard_map/ppermute | solution.py:511
  421.7 29.6 %collective-permute-start.27 = (bf16[256,1024]{1,0:T(8,128)(2,1)}, bf16[256,1024]{1,0:T(8,128)(2,1)S(1)}, u32[]{:S(2)}, u32[]{:S(2)}) collective-permute-start(bf16[256,1024]{1,0:T(8,128)(2,1)} %get-tuple-element.112), channel_id=1, source_target_pairs={{0,1},{1,0},{2,3},{3,2},{4,5},{5,4},{6,7},{7,6},{8,9},{9,8},{10,11... | collective-permute-start | bytes 1572872 | tf_op jit(solution)/shard_map/ppermute | solution.py:511
  424.3 346.8 %collective-permute-start.36 = (bf16[1024,1024]{1,0:T(8,128)(2,1)}, bf16[1024,1024]{1,0:T(8,128)(2,1)}, u32[]{:S(2)}, u32[]{:S(2)}) collective-permute-start(bf16[1024,1024]{1,0:T(8,128)(2,1)} %get-tuple-element.96), channel_id=1, source_target_pairs={{0,1},{1,0},{2,3},{3,2},{4,5},{5,4},{6,7},{7,6},{8,9},{9,8},{10,11... | collective-permute-start | bytes 6291464 | tf_op jit(solution)/shard_map/ppermute | solution.py:511
  451.6 177.8 %collective-permute-start.37 = (bf16[1024,1024]{1,0:T(8,128)(2,1)S(1)}, bf16[1024,1024]{1,0:T(8,128)(2,1)S(1)}, u32[]{:S(2)}, u32[]{:S(2)}) collective-permute-start(bf16[1024,1024]{1,0:T(8,128)(2,1)S(1)} %copy-done.21), channel_id=1, source_target_pairs={{0,1},{1,0},{2,3},{3,2},{4,5},{5,4},{6,7},{7,6},{8,9},{9,8},{10,11... | collective-permute-start | bytes 6291464 | tf_op jit(solution)/shard_map/ppermute | solution.py:511
  451.7 252.7 %collective-permute-start.52 = (bf16[1024,1024]{1,0:T(8,128)(2,1)S(1)}, bf16[1024,1024]{1,0:T(8,128)(2,1)}, u32[]{:S(2)}, u32[]{:S(2)}) collective-permute-start(bf16[1024,1024]{1,0:T(8,128)(2,1)S(1)} %get-tuple-element.95), channel_id=1, source_target_pairs={{0,1},{1,0},{2,3},{3,2},{4,5},{5,4},{6,7},{7,6},{8,9},{9,8},{10,11... | collective-permute-start | bytes 6291464 | tf_op jit(solution)/shard_map/ppermute | solution.py:511
  490.0 293.0 %collective-permute-start.17 = (bf16[2048,768]{1,0:T(8,128)(2,1)}, bf16[2048,768]{1,0:T(8,128)(2,1)}, u32[]{:S(2)}, u32[]{:S(2)}) collective-permute-start(bf16[2048,768]{1,0:T(8,128)(2,1)} %get-tuple-element.29), channel_id=1, source_target_pairs={{0,1},{1,0},{2,3},{3,2},{4,5},{5,4},{6,7},{7,6},{8,9},{9,8},{10,11... | collective-permute-start | bytes 9437192 | tf_op jit(solution)/shard_map/ppermute | solution.py:511
  503.8 49.0 %collective-permute-start.20 = (bf16[768,1024]{1,0:T(8,128)(2,1)}, bf16[768,1024]{1,0:T(8,128)(2,1)}, u32[]{:S(2)}, u32[]{:S(2)}) collective-permute-start(bf16[768,1024]{1,0:T(8,128)(2,1)} %add_convert_fusion.3), channel_id=1, source_target_pairs={{0,2},{1,3},{2,0},{3,1},{4,6},{5,7},{6,4},{7,5},{8,10},{9,11},{10,... | collective-permute-start | bytes 4718600 | tf_op jit(solution)/shard_map/ppermute | solution.py:503
  555.9 85.7 %collective-permute-start.30 = (bf16[256,1024]{1,0:T(8,128)(2,1)S(1)}, bf16[256,1024]{1,0:T(8,128)(2,1)S(1)}, u32[]{:S(2)}, u32[]{:S(2)}) collective-permute-start(bf16[256,1024]{1,0:T(8,128)(2,1)S(1)} %fusion.44), channel_id=1, source_target_pairs={{0,8},{4,12},{8,0},{12,4},{16,24},{20,28},{24,16},{28,20},{1,9},{5... | collective-permute-start | bytes 1572872 | tf_op jit(solution)/shard_map/ppermute | solution.py:430
  641.6 142.7 %collective-permute-start.15 = (bf16[2048,768]{1,0:T(8,128)(2,1)}, bf16[2048,768]{1,0:T(8,128)(2,1)}, u32[]{:S(2)}, u32[]{:S(2)}) collective-permute-start(bf16[2048,768]{1,0:T(8,128)(2,1)} %get-tuple-element.27), channel_id=1, source_target_pairs={{0,1},{1,0},{2,3},{3,2},{4,5},{5,4},{6,7},{7,6},{8,9},{9,8},{10,11... | collective-permute-start | bytes 9437192 | tf_op jit(solution)/shard_map/ppermute | solution.py:511
  658.9 34.5 %collective-permute-start.32 = (bf16[64,1024]{1,0:T(8,128)(2,1)S(1)}, bf16[64,1024]{1,0:T(8,128)(2,1)S(1)}, u32[]{:S(2)}, u32[]{:S(2)}) collective-permute-start(bf16[64,1024]{1,0:T(8,128)(2,1)S(1)} %constant_dynamic-slice_fusion.13), channel_id=1, source_target_pairs={{0,16},{4,20},{8,24},{12,28},{16,0},{20,4},{24,8},{28,12},{1,17},{... | collective-permute-start | bytes 393224 | tf_op jit(solution)/shard_map/ppermute | solution.py:430
  704.5 72.7 %collective-permute-start.38 = (bf16[1024,1024]{1,0:T(8,128)(2,1)}, bf16[1024,1024]{1,0:T(8,128)(2,1)S(1)}, u32[]{:S(2)}, u32[]{:S(2)}) collective-permute-start(bf16[1024,1024]{1,0:T(8,128)(2,1)} %fusion.35), channel_id=1, source_target_pairs={{0,2},{1,3},{2,0},{3,1},{4,6},{5,7},{6,4},{7,5},{8,10},{9,11},{10,... | collective-permute-start | bytes 6291464 | tf_op jit(solution)/shard_map/ppermute | solution.py:503
  722.6 31.2 %collective-permute-start.24 = (bf16[64,1024]{1,0:T(8,128)(2,1)S(1)}, bf16[64,1024]{1,0:T(8,128)(2,1)S(1)}, u32[]{:S(2)}, u32[]{:S(2)}) collective-permute-start(bf16[64,1024]{1,0:T(8,128)(2,1)S(1)} %add_convert_fusion.21), channel_id=1, source_target_pairs={{0,16},{4,20},{8,24},{12,28},{16,0},{20,4},{24,8},{28,12},{1,17},{... | collective-permute-start | bytes 393224 | tf_op jit(solution)/shard_map/ppermute | solution.py:430
  770.2 51.8 %collective-permute-start.51 = (bf16[1024,1024]{1,0:T(8,128)(2,1)}, bf16[1024,1024]{1,0:T(8,128)(2,1)}, u32[]{:S(2)}, u32[]{:S(2)}) collective-permute-start(bf16[1024,1024]{1,0:T(8,128)(2,1)} %get-tuple-element.94), channel_id=1, source_target_pairs={{0,1},{1,0},{2,3},{3,2},{4,5},{5,4},{6,7},{7,6},{8,9},{9,8},{10,11... | collective-permute-start | bytes 6291464 | tf_op jit(solution)/shard_map/ppermute | solution.py:511
  771.1 52.7 %collective-permute-start.53 = (bf16[1024,1024]{1,0:T(8,128)(2,1)}, bf16[1024,1024]{1,0:T(8,128)(2,1)}, u32[]{:S(2)}, u32[]{:S(2)}) collective-permute-start(bf16[1024,1024]{1,0:T(8,128)(2,1)} %fusion.32), channel_id=1, source_target_pairs={{0,2},{1,3},{2,0},{3,1},{4,6},{5,7},{6,4},{7,5},{8,10},{9,11},{10,... | collective-permute-start | bytes 6291464 | tf_op jit(solution)/shard_map/ppermute | solution.py:503
  777.2 117.3 %collective-permute-start.26 = (bf16[256,1024]{1,0:T(8,128)(2,1)}, bf16[256,1024]{1,0:T(8,128)(2,1)}, u32[]{:S(2)}, u32[]{:S(2)}) collective-permute-start(bf16[256,1024]{1,0:T(8,128)(2,1)} %maximum_select_fusion.6), channel_id=1, source_target_pairs={{0,4},{4,0},{8,12},{12,8},{16,20},{20,16},{24,28},{28,24},{1,5},{5... | collective-permute-start | bytes 1572872 | tf_op jit(solution)/shard_map/ppermute | solution.py:430
  783.0 114.1 %collective-permute-start.35 = (bf16[256,1024]{1,0:T(8,128)(2,1)}, bf16[256,1024]{1,0:T(8,128)(2,1)}, u32[]{:S(2)}, u32[]{:S(2)}) collective-permute-start(bf16[256,1024]{1,0:T(8,128)(2,1)} %maximum_select_fusion.7), channel_id=1, source_target_pairs={{0,8},{4,12},{8,0},{12,4},{16,24},{20,28},{24,16},{28,20},{1,9},{5... | collective-permute-start | bytes 1572872 | tf_op jit(solution)/shard_map/ppermute | solution.py:430
  784.3 115.4 %collective-permute-start.45 = (bf16[256,1024]{1,0:T(8,128)(2,1)}, bf16[256,1024]{1,0:T(8,128)(2,1)}, u32[]{:S(2)}, u32[]{:S(2)}) collective-permute-start(bf16[256,1024]{1,0:T(8,128)(2,1)} %constant_dynamic-slice_fusion.9), channel_id=1, source_target_pairs={{0,8},{4,12},{8,0},{12,4},{16,24},{20,28},{24,16},{28,20},{1,9},{5... | collective-permute-start | bytes 1572872 | tf_op jit(solution)/shard_map/ppermute | solution.py:430
  822.0 80.3 %collective-permute-start.39 = (bf16[256,1024]{1,0:T(8,128)(2,1)}, bf16[256,1024]{1,0:T(8,128)(2,1)}, u32[]{:S(2)}, u32[]{:S(2)}) collective-permute-start(bf16[256,1024]{1,0:T(8,128)(2,1)} %constant_dynamic-slice_fusion.12), channel_id=1, source_target_pairs={{0,4},{4,0},{8,12},{12,8},{16,20},{20,16},{24,28},{28,24},{1,5},{5... | collective-permute-start | bytes 1572872 | tf_op jit(solution)/shard_map/ppermute | solution.py:430
  (81 other events, 1649.8 us)

commit v2 on v1

v2 whole, which is shorter than its diff:
```python
import functools

import jax
import jax.numpy as jnp
from jax import lax
from jax.experimental import pallas as pl
from jax.experimental.pallas import tpu as pltpu
from jax.sharding import PartitionSpec as P

EPSILON = 1e-05
MASKED = -1e30
LOG2E = 1.4426950408889634
SHARED = 5
KEY_CHUNK = 512
MEGA = 2**20
ROW_TILE = 256
LAST_PARTS = 2
BACK_PARTS = 2


def contract_rows(left, right):
    return lax.dot_general(
        left, right, (((0,), (0,)), ((), ())), preferred_element_type=jnp.float32
    )


def contract_cols(left, right):
    return lax.dot_general(
        left, right, (((1,), (1,)), ((), ())), preferred_element_type=jnp.float32
    )


def matmul(left, right):
    return lax.dot_general(
        left, right, (((1,), (0,)), ((), ())), preferred_element_type=jnp.float32
    )


def block_lists(blocks_used, random_pick):
    block_count = random_pick.shape[0]
    places = jnp.arange(block_count, dtype=jnp.int32)[:, None]
    fixed_cols = jnp.zeros_like(places)
    chosen = jnp.concatenate(
        [
            places - 1,
            places,
            places + 1,
            fixed_cols,
            fixed_cols + blocks_used - 1,
            random_pick % blocks_used,
        ],
        axis=1,
    )
    inside = (chosen >= 0) & (chosen < blocks_used)
    slot_count = chosen.shape[1]
    before = jnp.arange(slot_count)[:, None] < jnp.arange(slot_count)[None, :]
    repeated = jnp.any(
        (chosen[:, :, None] == chosen[:, None, :]) & inside[:, :, None] & before[None], axis=1
    )
    return (jnp.clip(chosen, 0, block_count - 1), inside & jnp.logical_not(repeated))


def low(values):
    return values.astype(jnp.bfloat16)


def full(values):
    return values.astype(jnp.float32)


class Shape:
    def __init__(self, span, heads, head_size, blocks, slots):
        self.span, self.heads, self.head_size, self.blocks, self.slots = (
            span,
            heads,
            head_size,
            blocks,
            slots,
        )
        self.length = span // blocks
        self.lanes = heads * head_size
        self.columns = heads * self.length
        self.wide = max(1, min(heads, 128 // head_size))
        self.tile = self.wide * head_size
        self.chunk = min(KEY_CHUNK, span)
        self.bias_lanes = min(128, self.columns)


def rows_of(index, length):
    return pl.ds(pl.multiple_of(index * length, length), length)


def spread_heads(block, sh):
    lane = lax.broadcasted_iota(jnp.int32, block.shape, 1) // sh.head_size
    zero = jnp.zeros_like(block)
    return jnp.concatenate([jnp.where(lane == h, block, zero) for h in range(sh.heads)], axis=0)


def pick_heads(stacked, sh):
    lane = lax.broadcasted_iota(jnp.int32, (sh.length, sh.lanes), 1) // sh.head_size
    out = stacked[: sh.length]
    for h in range(1, sh.heads):
        out = jnp.where(lane == h, stacked[h * sh.length : (h + 1) * sh.length], out)
    return out


def mixed_slot(load, idx, j, s, sh):
    cols = []
    for t in range(sh.heads // sh.wide):
        out = None
        for i in range(sh.wide):
            at = idx[((t * sh.wide + i) * sh.blocks + j) * sh.slots + s]
            piece = load(rows_of(at, sh.length), t)
            if i == 0:
                out = piece
            else:
                lane = lax.broadcasted_iota(jnp.int32, piece.shape, 1) // sh.head_size
                out = jnp.where(lane == i, piece, out)
        cols.append(out)
    return cols[0] if len(cols) == 1 else jnp.concatenate(cols, axis=1)


def gather_rows(ref, first, idx, j, sh):
    parts = [
        ref[rows_of(idx[j * sh.slots + s], sh.length), first : first + sh.lanes]
        for s in range(SHARED)
    ]

    def load(rows, t):
        return ref[rows, first + t * sh.tile : first + (t + 1) * sh.tile]

    for s in range(SHARED, sh.slots):
        parts.append(mixed_slot(load, idx, j, s, sh))
    return jnp.concatenate(parts, axis=0)


def widen(bias, sh):
    reps = sh.columns // sh.bias_lanes
    return bias if reps == 1 else jnp.concatenate([bias] * reps, axis=1)


def gather_bias(ref, idx, j, sh):
    parts = [
        widen(ref[rows_of(idx[j * sh.slots + s], sh.length), : sh.bias_lanes], sh)
        for s in range(SHARED)
    ]

    def load(rows, t):
        return ref[rows, : sh.bias_lanes]

    for s in range(SHARED, sh.slots):
        parts.append(mixed_slot(load, idx, j, s, sh))
    return jnp.concatenate(parts, axis=0)


def split_rows(dot, left, right, cuts):
    edges = [0, *cuts, left.shape[0]]
    return jnp.concatenate([dot(left[a:b], right) for a, b in zip(edges, edges[1:])], axis=0)


def each_block(first, count, unroll, blocks_from):
    def many(i, carry):
        blocks_from(first + i * unroll, unroll)
        return carry

    lax.fori_loop(0, count // unroll, many, 0)

    def one(j, carry):
        blocks_from(j, 1)
        return carry

    lax.fori_loop(first + count // unroll * unroll, first + count, one, 0)


def forward_kernel(sh, pieces, unroll, used, member, idx, bidx, *refs):
    packed, bias_ref = refs[:pieces], refs[pieces]
    outs, log_ref = refs[pieces + 1 : 2 * pieces + 1], refs[2 * pieces + 1]
    rows, o_scr, s_scr, sems = refs[2 * pieces + 2 :]
    c = used[0]
    scale = sh.head_size ** (-0.5) * LOG2E
    rows_each = sh.span // pieces
    query, key, value = 0, sh.lanes, 2 * sh.lanes

    def place(r):
        return rows_of(lax.rem(member[0] + r, pieces), rows_each)

    loads = [pltpu.make_async_copy(packed[r], rows.at[place(r)], sems.at[r]) for r in range(pieces)]
    for copy in loads:
        copy.start()
    o_scr[...] = jnp.zeros_like(o_scr)
    log_ref[...] = jnp.zeros_like(log_ref)
    for copy in loads:
        copy.wait()

    def block(j):
        at = rows_of(j, sh.length)
        q_all = spread_heads(rows[at, query : query + sh.lanes], sh)
        scores = contract_cols(gather_rows(rows, key, idx, j, sh), q_all) * scale
        scores = scores + gather_bias(bias_ref, bidx, j, sh)
        top = jnp.max(scores, axis=0, keepdims=True)
        shifted = jnp.exp2(scores - top)
        total = jnp.sum(shifted, axis=0, keepdims=True)
        log_ref[pl.ds(j, 1), :] = top + jnp.log2(total)
        probs = low(shifted * (1.0 / total))
        out = pick_heads(contract_rows(probs, gather_rows(rows, value, idx, j, sh)), sh)
        o_scr[at, :] = low(out)

    def blocks_from(j, count):
        for u in range(count):
            block(j + u)

    each_block(1, c - 2, unroll, blocks_from)

    chunks = pl.cdiv(c * sh.length, sh.chunk)
    row = (1, sh.columns)
    for j in (0, c - 1):
        at = rows_of(j, sh.length)
        q_all = spread_heads(rows[at, query : query + sh.lanes], sh)

        def first(i, top):
            keys = rows_of(i, sh.chunk)
            scores = contract_cols(rows[keys, key : key + sh.lanes], q_all) * scale
            scores = scores + widen(bias_ref[keys, : sh.bias_lanes], sh)
            s_scr[keys, :] = scores
            return jnp.maximum(top, jnp.max(scores, axis=0, keepdims=True))

        top = lax.fori_loop(0, chunks, first, jnp.full(row, MASKED, jnp.float32))

        def second(i, total):
            keys = rows_of(i, sh.chunk)
            shifted = jnp.exp2(s_scr[keys, :] - top)
            s_scr[keys, :] = shifted
            return total + jnp.sum(shifted, axis=0, keepdims=True)

        total = lax.fori_loop(0, chunks, second, jnp.zeros(row, jnp.float32))
        log_ref[pl.ds(j, 1), :] = top + jnp.log2(total)
        inverse = 1.0 / total

        def third(i, out):
            keys = rows_of(i, sh.chunk)
            probs = low(s_scr[keys, :] * inverse)
            return out + contract_rows(probs, rows[keys, value : value + sh.lanes])

        out = lax.fori_loop(0, chunks, third, jnp.zeros((sh.columns, sh.lanes), jnp.float32))
        o_scr[at, :] = low(pick_heads(out, sh))

    stores = [
        pltpu.make_async_copy(o_scr.at[place(r)], outs[r], sems.at[pieces + r])
        for r in range(pieces)
    ]
    for copy in stores:
        copy.start()
    for copy in stores:
        copy.wait()


def backward_kernel(sh, pieces, unroll, part, used, member, idx, bidx, *refs):
    part, parts = part
    packed, tops, made = refs[:pieces], refs[pieces : 2 * pieces], refs[2 * pieces : 3 * pieces]
    refs = refs[3 * pieces :]
    (bias_ref, log_ref), refs = refs[:2], refs[2:]
    carried, refs = refs[: pieces * (part > 0)], refs[pieces * (part > 0) :]
    outs, refs = refs[:pieces], refs[pieces:]
    rows, grads, merged, d_scr, ka_scr, va_scr, sems = refs
    c = used[0]
    factor = sh.head_size ** (-0.5)
    scale = factor * LOG2E
    rows_each = sh.span // pieces
    query, key, value = 0, sh.lanes, 2 * sh.lanes
    length, slots = sh.length, sh.slots
    keys_each = slots * length

    def place(r):
        return rows_of(lax.rem(member[0] + r, pieces), rows_each)

    loads = []
    for n, (sources, target) in enumerate(((packed, rows), (tops, grads), (made, merged))):
        for r in range(pieces):
            copy = pltpu.make_async_copy(
                sources[r], target.at[place(r)], sems.at[n * pieces + r]
            )
            loads.append(copy)
            copy.start()
    for r in range(pieces if part else 0):
        copy = pltpu.make_async_copy(
            carried[r], d_scr.at[place(r)], sems.at[4 * pieces + r]
        )
        loads.append(copy)
        copy.start()
    if not part:
        d_scr[:, : sh.lanes] = jnp.zeros((sh.span, sh.lanes), d_scr.dtype)
        ka_scr[...] = jnp.zeros_like(ka_scr)
        va_scr[...] = jnp.zeros_like(va_scr)
    for copy in loads:
        copy.wait()
    if part:
        ka_scr[...] = full(d_scr[:, key : key + sh.lanes]) * (1.0 / factor)
        va_scr[...] = full(d_scr[:, value : value + sh.lanes])

    def equal_rows(products):
        row = lax.broadcasted_iota(jnp.int32, products.shape, 0)
        column = lax.broadcasted_iota(jnp.int32, products.shape, 1)
        return jnp.sum(
            jnp.where(column % length == row, products, 0.0), axis=0, keepdims=True
        )

    def block(j):
        at = rows_of(j, length)
        q_all = spread_heads(rows[at, query : query + sh.lanes], sh)
        g_all = spread_heads(grads[at, :], sh)
        k_all = gather_rows(rows, key, idx, j, sh)
        v_all = jnp.concatenate([gather_rows(rows, value, idx, j, sh), merged[at, :]], axis=0)
        cuts = [keys_each // 2]
        scores = split_rows(contract_cols, k_all, q_all, cuts) * scale
        prob_grad = split_rows(contract_cols, v_all, g_all, cuts)
        delta = equal_rows(prob_grad[keys_each:])
        scores = scores + gather_bias(bias_ref, bidx, j, sh)
        probs = jnp.exp2(scores - log_ref[pl.ds(j, 1), :])
        score_grad = low(probs * (prob_grad[:keys_each] - delta))
        query_grad = pick_heads(contract_rows(score_grad, k_all), sh) * factor
        d_scr[at, : sh.lanes] = low(query_grad)
        return (
            split_rows(matmul, score_grad, q_all, cuts),
            split_rows(matmul, low(probs), g_all, cuts),
        )

    def random_add(ref, j, value):
        tile = sh.tile
        for s in range(SHARED, slots):
            for h in range(sh.heads):
                t, i = h // sh.wide, h % sh.wide
                at = rows_of(idx[(h * sh.blocks + j) * slots + s], length)
                piece = value[s * length : (s + 1) * length, t * tile : (t + 1) * tile]
                if sh.wide > 1:
                    lane = lax.broadcasted_iota(jnp.int32, piece.shape, 1) // sh.head_size
                    piece = jnp.where(lane == i, piece, 0.0)
                ref[at, t * tile : (t + 1) * tile] += piece

    def blocks_from(j, count):
        gained = [block(j + u) for u in range(count)]
        for which, ref in ((0, ka_scr), (1, va_scr)):

            def slot(u, s):
                return gained[u][which][s * length : (s + 1) * length]

            for n in range(count + 2):
                total = None
                for u in range(count):
                    if 0 <= n - u <= 2:
                        total = slot(u, n - u) if total is None else total + slot(u, n - u)
                ref[rows_of(j - 1 + n, length), :] += total
            for s, target in ((3, 0), (4, c - 1)):
                total = slot(0, s)
                for u in range(1, count):
                    total = total + slot(u, s)
                ref[rows_of(target, length), :] += total
            for u in range(count):
                random_add(ref, j + u, gained[u][which])

    steps = (c - 2) // unroll
    begin, end = steps * part // parts * unroll, steps * (part + 1) // parts * unroll
    if part == parts - 1:
        end = c - 2
    each_block(1 + begin, end - begin, unroll, blocks_from)

    chunks = pl.cdiv(c * length, sh.chunk)
    for j in (0, c - 1)[2 * part // parts : 2 * (part + 1) // parts]:
        at = rows_of(j, length)
        q_all = spread_heads(rows[at, query : query + sh.lanes], sh)
        g_all = spread_heads(grads[at, :], sh)
        delta = equal_rows(contract_cols(merged[at, :], g_all))
        log_row = log_ref[pl.ds(j, 1), :]

        def chunk(i, total):
            keys = rows_of(i, sh.chunk)
            k_all = rows[keys, key : key + sh.lanes]
            scores = contract_cols(k_all, q_all) * scale
            scores = scores + widen(bias_ref[keys, : sh.bias_lanes], sh)
            probs = jnp.exp2(scores - log_row)
            prob_grad = contract_cols(rows[keys, value : value + sh.lanes], g_all)
            score_grad = low(probs * (prob_grad - delta))
            ka_scr[keys, :] += matmul(score_grad, q_all)
            va_scr[keys, :] += matmul(low(probs), g_all)
            return total + contract_rows(score_grad, k_all)

        total = lax.fori_loop(0, chunks, chunk, jnp.zeros((sh.columns, sh.lanes), jnp.float32))
        d_scr[at, : sh.lanes] = low(pick_heads(total, sh) * factor)

    d_scr[:, key : key + sh.lanes] = low(ka_scr[...] * factor)
    d_scr[:, value : value + sh.lanes] = low(va_scr[...])
    stores = [
        pltpu.make_async_copy(d_scr.at[place(r)], outs[r], sems.at[3 * pieces + r])
        for r in range(pieces)
    ]
    for copy in stores:
        copy.start()
    for copy in stores:
        copy.wait()


ANYWHERE = pl.BlockSpec(memory_space=pl.ANY)
ON_CHIP = pl.BlockSpec(memory_space=pltpu.VMEM)
SCALARS = pl.BlockSpec(memory_space=pltpu.SMEM)


def cost(flops, accessed=10**6):
    return pl.CostEstimate(flops=int(flops), bytes_accessed=int(accessed), transcendentals=0)


def attend_cost(sh, weight):
    return cost(weight * sh.blocks * sh.slots * sh.length * sh.columns * sh.lanes)


def attend_forward(sh, packed, lists, weight=16, unroll=6):
    pieces = len(packed)
    used, member, idx, bidx, bias = lists
    rows_each = sh.span // pieces
    outs = pl.pallas_call(
        functools.partial(forward_kernel, sh, pieces, unroll),
        in_specs=[SCALARS] * 4 + [ANYWHERE] * pieces + [ON_CHIP],
        out_specs=[ANYWHERE] * pieces + [ON_CHIP],
        out_shape=[jax.ShapeDtypeStruct((rows_each, sh.lanes), jnp.bfloat16)] * pieces
        + [jax.ShapeDtypeStruct((sh.blocks, sh.columns), jnp.float32)],
        scratch_shapes=[
            pltpu.VMEM((sh.span, 3 * sh.lanes), jnp.bfloat16),
            pltpu.VMEM((sh.span, sh.lanes), jnp.bfloat16),
            pltpu.VMEM((sh.span, sh.columns), jnp.float32),
            pltpu.SemaphoreType.DMA((2 * pieces,)),
        ],
        compiler_params=pltpu.CompilerParams(vmem_limit_bytes=40 * MEGA),
        cost_estimate=attend_cost(sh, weight),
        name="attend_forward",
    )(used, member, idx, bidx, *packed, bias)
    return outs[:pieces], outs[pieces]


def attend_backward(sh, packed, tops, made, log_rows, lists, part=(0, 1), carried=(), unroll=2):
    pieces = len(packed)
    used, member, idx, bidx, bias = lists
    rows_each = sh.span // pieces
    return pl.pallas_call(
        functools.partial(backward_kernel, sh, pieces, unroll, part),
        in_specs=[SCALARS] * 4
        + [ANYWHERE] * (3 * pieces)
        + [ON_CHIP] * 2
        + [ANYWHERE] * len(carried),
        out_specs=[ANYWHERE] * pieces,
        out_shape=[jax.ShapeDtypeStruct((rows_each, 3 * sh.lanes), jnp.bfloat16)] * pieces,
        scratch_shapes=[
            pltpu.VMEM((sh.span, 3 * sh.lanes), jnp.bfloat16),
            pltpu.VMEM((sh.span, sh.lanes), jnp.bfloat16),
            pltpu.VMEM((sh.span, sh.lanes), jnp.bfloat16),
            pltpu.VMEM((sh.span, 3 * sh.lanes), jnp.bfloat16),
            pltpu.VMEM((sh.span, sh.lanes), jnp.float32),
            pltpu.VMEM((sh.span, sh.lanes), jnp.float32),
            pltpu.SemaphoreType.DMA((5 * pieces,)),
        ],
        compiler_params=pltpu.CompilerParams(vmem_limit_bytes=36 * MEGA),
        cost_estimate=attend_cost(sh, 32 // part[1]),
        name="attend_backward",
    )(used, member, idx, bidx, *packed, *tops, *made, bias, log_rows, *carried)


GELU_A = (2 / 3.141592653589793) ** 0.5
GELU_B = GELU_A * 0.044715
ONES = 16


def gelu_both(pre):
    square = pre * pre
    turn = jnp.tanh(pre * (GELU_A + GELU_B * square))
    half = 0.5 + 0.5 * turn
    act = pre * half
    slope = half + act * (1.0 - turn) * (GELU_A + 3.0 * GELU_B * square)
    return act, slope


def unit_of(rows):
    center = jnp.mean(rows, axis=1, keepdims=True)
    deviation = rows - center
    inverse = lax.rsqrt(jnp.mean(deviation * deviation, axis=1, keepdims=True) + EPSILON)
    return deviation * inverse, inverse


def norm_grad(grad_normed, unit, inverse, gain):
    scaled = grad_normed * gain
    plain_mean = jnp.mean(scaled, axis=1, keepdims=True)
    cross_mean = jnp.mean(scaled * unit, axis=1, keepdims=True)
    return inverse * (scaled - plain_mean - unit * cross_mean)


def column_sum(values):
    return jnp.sum(values, axis=0, keepdims=True)


def take(refs, count):
    return refs[:count], refs[count:]


def tiled(tile, cols, first=0):
    return pl.BlockSpec((tile, cols), lambda i: (first + i, 0))


def line(cols):
    return pl.BlockSpec((1, cols), lambda i: (0, 0))


def line_out(cols):
    return jax.ShapeDtypeStruct((1, cols), jnp.float32)


def rows_out(rows, cols, dtype=jnp.bfloat16):
    return jax.ShapeDtypeStruct((rows, cols), dtype)


def middle_kernel(count, outs_count, head, tail, offsets, *refs):
    (cot_ref, bias_ref), refs = take(refs, 2)
    if head:
        (resid_ref, outer_bias_ref, gain_ref, shift_ref), refs = take(refs, 4)
        merged, refs = take(refs, outs_count)
    else:
        (second_in, total_in, back_in), refs = take(refs, 3)
    if tail:
        (middle_in, gain_in), refs = take(refs, 2)
    out_w, refs = take(refs, outs_count if head or tail else 0)
    inner_w, refs = take(refs, count)
    outer_w, refs = take(refs, count)
    if head:
        (second_ref, middle_ref), refs = take(refs, 2)
    if tail:
        (outputs_ref, grad_ref, branch_ref, gain_sum, shift_sum, cot_sum), refs = take(refs, 6)
        tops, refs = take(refs, outs_count)
    else:
        (total_ref, back_ref), refs = take(refs, 2)
    acts, refs = take(refs, count)
    inner_grads, refs = take(refs, count)
    out_scr, inner_scr, outer_scr, total_scr, back_scr, sems = refs
    step = pl.program_id(0)
    model, width = inner_scr.shape[1:]
    out_copies = []
    for i, ref in enumerate(out_w):
        lanes = out_scr.shape[0] // outs_count
        out_copies.append(
            pltpu.make_async_copy(
                ref.at[pl.ds(offsets[0][i], lanes)], out_scr.at[pl.ds(i * lanes, lanes)], sems.at[i]
            )
        )
    copies = []
    for i in range(count):
        n = outs_count + 2 * i
        inner = inner_w[i].at[pl.ds(offsets[1][i], model)]
        outer = outer_w[i].at[pl.ds(offsets[2][i], width)]
        copies.append(
            [
                pltpu.make_async_copy(inner, inner_scr.at[i], sems.at[n]),
                pltpu.make_async_copy(outer, outer_scr.at[i], sems.at[n + 1]),
            ]
        )

    @pl.when(step == 0)
    def _():
        for copy in out_copies if head else []:
            copy.start()
        for pair in copies:
            for copy in pair:
                copy.start()
        for copy in [] if head else out_copies:
            copy.start()
        if tail:
            for ref in (gain_sum, shift_sum, cot_sum):
                ref[...] = jnp.zeros_like(ref)

    def body(first_step):
        def ready(group):
            if first_step:
                for copy in group:
                    copy.wait()

        cot = cot_ref[...]
        if head:
            ready(out_copies)
            joined = jnp.concatenate([ref[...] for ref in merged], axis=1)
            middle = full(resid_ref[...]) + matmul(joined, out_scr[...])
            middle_ref[...] = middle
            unit, _ = unit_of(middle)
            second = low(unit * gain_ref[...] + shift_ref[...])
            second_ref[:, :model] = second
            second_ref[:, model:] = jnp.ones((second.shape[0], ONES), jnp.bfloat16)
            total_scr[...] = middle + outer_bias_ref[...]
        else:
            second = second_in[:, :model]
            total_scr[...] = total_in[...]
            back_scr[...] = back_in[...]
        for i in range(count):
            ready(copies[i])
            pre = matmul(second, inner_scr[i]) + bias_ref[:, i * width : (i + 1) * width]
            grad = contract_cols(cot, outer_scr[i])
            act, slope = gelu_both(pre)
            act = low(act)
            acts[i][...] = act
            grad = low(grad * slope)
            inner_grads[i][...] = grad
            total_scr[...] += matmul(act, outer_scr[i])
            back = contract_cols(grad, inner_scr[i])
            if head and i == 0:
                back_scr[...] = back
            else:
                back_scr[...] += back
        if not tail:
            total_ref[...] = total_scr[...]
            back_ref[...] = back_scr[...]
            return
        outputs_ref[...] = low(total_scr[...])
        second_grad = back_scr[...]
        unit, inverse = unit_of(middle_in[...])
        cot_wide = full(cot)
        middle_grad = cot_wide + norm_grad(second_grad, unit, inverse, gain_in[...])
        gain_sum[...] += column_sum(second_grad * unit)
        shift_sum[...] += column_sum(second_grad)
        cot_sum[...] += column_sum(cot_wide)
        grad_ref[...] = middle_grad
        branch = low(middle_grad)
        branch_ref[...] = branch
        ready([] if head else out_copies)
        top = low(contract_cols(branch, out_scr[...]))
        at = 0
        for ref in tops:
            ref[...] = top[:, at : at + ref.shape[1]]
            at += ref.shape[1]

    @pl.when(step == 0)
    def _():
        body(True)

    @pl.when(step > 0)
    def _():
        body(False)


def run_middle(cot, bias, inner_w, outer_w, out_w, head=None, carried=None, tail=None):
    rows, model = cot.shape
    count, outs_count = len(inner_w), len(out_w)
    tile = min(ROW_TILE, rows)
    width = bias.shape[1] // count
    lanes = model // outs_count
    args, in_specs = [cot, bias], [tiled(tile, model), line(count * width)]
    if head is not None:
        resid, lines, merged = head
        args += [resid, *lines, *merged]
        in_specs += [tiled(tile, model)] + [line(model)] * 3 + [tiled(tile, lanes)] * outs_count
    else:
        args += carried
        in_specs += [tiled(tile, model + ONES)] + [tiled(tile, model)] * 2
    if tail is not None:
        args += tail
        in_specs += [tiled(tile, model), line(model)]
    used_out = out_w if head is not None or tail is not None else []
    weights = [*used_out, *inner_w, *outer_w]
    args += [array for array, _ in weights]
    in_specs += [ANYWHERE] * len(weights)
    offsets = [[first for _, first in group] for group in (used_out, inner_w, outer_w)]
    out_specs, out_shape = [], []

    def result(cols, dtype=jnp.bfloat16):
        out_specs.append(tiled(tile, cols))
        out_shape.append(rows_out(rows, cols, dtype))

    if head is not None:
        result(model + ONES)
        result(model, jnp.float32)
    if tail is not None:
        result(model)
        result(model, jnp.float32)
        result(model)
        for _ in range(3):
            out_specs.append(line(model))
            out_shape.append(line_out(model))
        for _ in range(outs_count):
            result(lanes)
    else:
        result(model, jnp.float32)
        result(model, jnp.float32)
    for _ in range(2 * count):
        result(width)
    outs = pl.pallas_call(
        functools.partial(
            middle_kernel, count, outs_count, head is not None, tail is not None, offsets
        ),
        grid=(rows // tile,),
        in_specs=in_specs,
        out_specs=out_specs,
        out_shape=out_shape,
        scratch_shapes=[
            pltpu.VMEM((model, model), jnp.bfloat16),
            pltpu.VMEM((count, model, width), jnp.bfloat16),
            pltpu.VMEM((count, width, model), jnp.bfloat16),
            pltpu.VMEM((tile, model), jnp.float32),
            pltpu.VMEM((tile, model), jnp.float32),
            pltpu.SemaphoreType.DMA((outs_count + 2 * count,)),
        ],
        compiler_params=pltpu.CompilerParams(vmem_limit_bytes=58 * MEGA),
        cost_estimate=cost(rows * model),
        name="middle",
    )(*args)
    plain = outs[: -2 * count]
    return plain, outs[-2 * count : -count], outs[-count:]


def bundle_kernel(count, *refs):
    sources, target, (held, sems) = refs[:count], refs[count], refs[count + 1 :]
    loads, stores, at = [], [], 0
    for i, source in enumerate(sources):
        rows = pl.ds(at, source.shape[0])
        at += source.shape[0]
        loads.append(pltpu.make_async_copy(source, held.at[rows], sems.at[i]))
        stores.append(pltpu.make_async_copy(held.at[rows], target.at[rows], sems.at[count + i]))
    for copy in loads:
        copy.start()
    for load, store in zip(loads, stores):
        load.wait()
        store.start()
    for copy in stores:
        copy.wait()


def run_bundle(arrays):
    rows, cols = sum(array.shape[0] for array in arrays), arrays[0].shape[1]
    return pl.pallas_call(
        functools.partial(bundle_kernel, len(arrays)),
        in_specs=[ANYWHERE] * len(arrays),
        out_specs=ANYWHERE,
        out_shape=rows_out(rows, cols),
        scratch_shapes=[
            pltpu.VMEM((rows, cols), jnp.bfloat16),
            pltpu.SemaphoreType.DMA((2 * len(arrays),)),
        ],
        compiler_params=pltpu.CompilerParams(vmem_limit_bytes=58 * MEGA),
        cost_estimate=cost(rows * cols),
        name="bundle",
    )(*arrays)


def add_kernel(count, tall, *refs):
    firsts, seconds, (out_ref, row_ref) = refs[:count], refs[count : 2 * count], refs[2 * count :]

    def total(arrays, rows):
        value = full(arrays[0][rows, :])
        for ref in arrays[1:]:
            value = value + full(ref[rows, :])
        return value

    rest = total(firsts, slice(tall, firsts[0].shape[0]))
    row_ref[...] = rest[:1]
    out_ref[:tall, :] = low(total(firsts, slice(0, tall)))
    out_ref[tall:, :] = low(total(seconds, slice(0, seconds[0].shape[0])))


def run_add(firsts, seconds, tall):
    count, cols = len(firsts), firsts[0].shape[1]
    return pl.pallas_call(
        functools.partial(add_kernel, count, tall),
        in_specs=[ON_CHIP] * (2 * count),
        out_specs=[ON_CHIP] * 2,
        out_shape=[rows_out(tall + seconds[0].shape[0], cols), line_out(cols)],
        compiler_params=pltpu.CompilerParams(vmem_limit_bytes=32 * MEGA),
        cost_estimate=cost(10**6, 8 * firsts[0].shape[0] * cols),
        name="add",
    )(*firsts, *seconds)


def first_kernel(resid_ref, gain_ref, shift_ref, weight_ref, normed_ref, packed_ref):
    unit, _ = unit_of(full(resid_ref[...]))
    normed = low(unit * gain_ref[...] + shift_ref[...])
    normed_ref[...] = normed
    packed_ref[...] = low(contract_cols(normed, weight_ref[...]))


def run_first(resid, gain, shift, weight):
    rows, model = resid.shape
    tile = min(ROW_TILE, rows)
    cols = weight.shape[0]
    return pl.pallas_call(
        first_kernel,
        grid=(rows // tile,),
        in_specs=[
            tiled(tile, model),
            line(model),
            line(model),
            pl.BlockSpec((cols, model), lambda i: (0, 0), pipeline_mode=pl.Buffered(1)),
        ],
        out_specs=[tiled(tile, model), tiled(tile, cols)],
        out_shape=[rows_out(rows, model), rows_out(rows, cols)],
        compiler_params=pltpu.CompilerParams(vmem_limit_bytes=32 * MEGA),
        cost_estimate=cost(rows * model),
        name="first",
    )(resid, gain, shift, weight)


def project_kernel(rows_ref, weight_ref, packed_ref):
    packed_ref[...] = low(contract_cols(rows_ref[...], weight_ref[...]))


def run_project(rows_in, weight):
    rows, model = rows_in.shape
    tile = min(2 * ROW_TILE, rows)
    cols = weight.shape[0]
    return pl.pallas_call(
        project_kernel,
        grid=(rows // tile,),
        in_specs=[
            tiled(tile, model),
            pl.BlockSpec((cols, model), lambda i: (0, 0), pipeline_mode=pl.Buffered(1)),
        ],
        out_specs=tiled(tile, cols),
        out_shape=rows_out(rows, cols),
        compiler_params=pltpu.CompilerParams(vmem_limit_bytes=32 * MEGA),
        cost_estimate=cost(rows * model),
        name="project",
    )(rows_in, weight)


def last_kernel(parts, *refs):
    (resid_ref, grad_ref, gain_ref), refs = take(refs, 3)
    packed, refs = take(refs, parts)
    joint_w, refs = take(refs, parts)
    out_ref, gain_sum, shift_sum, joint_scr, sems = refs[-5:]
    step = pl.program_id(0)
    copies = [
        pltpu.make_async_copy(joint_w[i], joint_scr.at[i], sems.at[i]) for i in range(parts)
    ]

    @pl.when(step == 0)
    def _():
        for copy in copies:
            copy.start()
        gain_sum[...] = jnp.zeros_like(gain_sum)
        shift_sum[...] = jnp.zeros_like(shift_sum)
        for copy in copies:
            copy.wait()

    unit, inverse = unit_of(full(resid_ref[...]))
    joined = jnp.concatenate([ref[...] for ref in packed], axis=1)
    first_grad = matmul(joined, joint_scr[...].reshape(joined.shape[1], joint_scr.shape[2]))
    out_ref[...] = grad_ref[...] + norm_grad(first_grad, unit, inverse, gain_ref[...])
    gain_sum[...] += column_sum(first_grad * unit)
    shift_sum[...] += column_sum(first_grad)


def run_last(part, part_rows, resid, middle_grad, gain, packed, joint_w, made):
    parts = len(packed)
    rows, model = resid.shape
    tile = min(ROW_TILE, part_rows)
    depth = packed[0].shape[1]
    first = part * part_rows // tile
    return pl.pallas_call(
        functools.partial(last_kernel, parts),
        grid=(part_rows // tile,),
        in_specs=[tiled(tile, model, first)] * 2
        + [line(model)]
        + [tiled(tile, depth, first)] * parts
        + [ANYWHERE] * parts
        + [ANYWHERE] * (made is not None),
        out_specs=[tiled(tile, model, first)] + [line(model)] * 2,
        out_shape=[rows_out(rows, model, jnp.float32)] + [line_out(model)] * 2,
        scratch_shapes=[
            pltpu.VMEM((parts, depth, model), jnp.bfloat16),
            pltpu.SemaphoreType.DMA((parts,)),
        ],
        input_output_aliases={} if made is None else {3 + 2 * parts: 0},
        compiler_params=pltpu.CompilerParams(vmem_limit_bytes=40 * MEGA),
        cost_estimate=cost(2 * part_rows * model * parts * depth, part_rows * model * 20),
        name="last",
    )(resid, middle_grad, gain, *packed, *joint_w, *([] if made is None else [made]))


def swap(values, axis, bit):
    size = lax.axis_size(axis)
    return lax.ppermute(values, axis, [(i, i ^ bit) for i in range(size)])


def after(values, *earlier):
    return lax.optimization_barrier((values, earlier))[0]


def put_halves(upper, mine, other):
    return jnp.where(
        upper == 0,
        jnp.concatenate([mine, other], axis=0),
        jnp.concatenate([other, mine], axis=0),
    )


def half(values, upper):
    rows = values.shape[0] // 2
    return lax.dynamic_slice_in_dim(values, upper * rows, rows, 0)


class GroupSum:
    def __init__(self, values, which=(0, 1)):
        bits = [1 << i for i in range(lax.axis_size("dp").bit_length() - 1)]
        orders = []
        for order in (bits, bits[1:2] + bits[:1] + bits[2:]):
            odd = len(order) % 2
            groups = [order[:odd]] + [order[i : i + 2] for i in range(odd, len(order), 2)]
            orders.append([tuple(group) for group in groups if group])
        orders = [orders[n] for n in which]
        part = values.shape[0] // len(orders)
        self.parts = [values[n * part : (n + 1) * part] for n in range(len(orders))]
        self.steps = [
            [(True, group) for group in order] + [(False, group) for group in order[::-1]]
            for order in orders
        ]
        self.pending = None

    def start(self):
        self.pending, sent = [], []
        if not self.steps[0]:
            return tuple(self.parts)
        for values, steps in zip(self.parts, self.steps):
            halving, group = steps.pop(0)
            uppers = [(lax.axis_index("dp") // bit) % 2 for bit in group]
            others = []
            for k in range(1, 1 << len(group)):
                flips = [k >> i & 1 for i in range(len(group))]
                leaving = values
                if halving:
                    for upper, flip in zip(uppers[::-1], flips[::-1]):
                        leaving = half(leaving, 1 - upper if flip else upper)
                sent.append(leaving)
                bit = sum(bit for bit, flip in zip(group, flips) if flip)
                others.append(swap(leaving, "dp", bit))
            if halving:
                for upper in uppers[::-1]:
                    values = half(values, upper)
            self.pending.append((halving, uppers, values, others))
        return tuple(sent)

    def finish(self, *earlier):
        if not self.pending:
            return
        self.parts = []
        for halving, uppers, mine, others in self.pending:
            if earlier:
                others = after(others, *earlier)
            if halving:
                total = full(mine)
                for other in others:
                    total = total + full(other)
                self.parts.append(low(total))
            else:
                pieces = [mine, *others]
                for upper in uppers:
                    pieces = [
                        put_halves(upper, pieces[n], pieces[n + 1])
                        for n in range(0, len(pieces), 2)
                    ]
                self.parts += pieces
        self.pending = None

    def step(self, *earlier):
        self.finish(*earlier)
        return self.start()

    def result(self):
        while self.steps[0] or self.pending:
            self.step()
        return full(jnp.concatenate(self.parts, axis=0))


def sum_all(values):
    for axis in ("tensor", "dp"):
        size, bit = lax.axis_size(axis), 1
        while bit < size:
            if 2 * bit < size:
                others = [swap(values, axis, bit * n) for n in (1, 2, 3)]
                values = (values + others[0]) + (others[1] + others[2])
                bit *= 4
            else:
                values = values + swap(values, axis, bit)
                bit *= 2
    return values


def split_exact(values):
    terms = []
    for _ in range(3):
        term = lax.reduce_precision(values, 8, 7)
        terms.append(low(term))
        values = values - term
    return terms


def per_device(
    inputs,
    query_weight,
    key_weight,
    value_weight,
    output_weight,
    inner_weight,
    inner_bias,
    outer_weight,
    outer_bias,
    first_gain,
    first_shift,
    second_gain,
    second_shift,
    item_lengths,
    key_mask,
    random_blocks,
    cotangent,
):
    tensor = lax.axis_size("tensor")
    items = item_lengths.shape[0]
    local_rows, model = inputs.shape
    span = local_rows * tensor // items
    members = tensor // items
    place = lax.axis_index("tensor")
    item, member = place // members, place % members
    heads, blocks = random_blocks.shape[1], random_blocks.shape[2]
    lanes = query_weight.shape[0]
    length = span // blocks
    sh = Shape(span, heads, lanes // heads, blocks, SHARED + random_blocks.shape[3])

    def from_item(values, step):
        if step % items == 0:
            return values
        pairs = [
            (t, (t // members - step) % items * members + t % members) for t in range(tensor)
        ]
        return lax.ppermute(values, "tensor", pairs)

    def from_member(values, step):
        if step % members == 0:
            return values
        pairs = [
            (t, t // members * members + (t % members - step) % members) for t in range(tensor)
        ]
        return lax.ppermute(values, "tensor", pairs)

    order = [(s, r) for s in range(items) for r in range(members)]
    away = range(1, items)
    joint = run_bundle([query_weight, key_weight, value_weight])
    upper = lax.axis_index("dp") % 2
    joint_halves = [from_item(half(joint, upper), s) for s in away]

    lines = (first_gain.reshape(1, -1), first_shift.reshape(1, -1))
    firsts = [run_first(from_member(inputs, r), *lines, joint) for r in range(members)]
    first_all = [normed for normed, _ in firsts]

    width = inner_weight.shape[1]
    bias_rows = jnp.stack(split_exact(inner_bias))
    bias_rows = jnp.concatenate([bias_rows, jnp.zeros((13, width), jnp.bfloat16)], axis=0)
    own_weights = [output_weight, inner_weight, outer_weight, bias_rows]
    if width == model:
        sent = [run_bundle([output_weight, outer_weight, bias_rows]), inner_weight]
        views = [(0, 0), (1, 0), (0, lanes), (0, lanes + width)]
    else:
        sent = own_weights
        views = [(n, 0) for n in range(len(own_weights))]

    used = lax.dynamic_index_in_dim(item_lengths, item, 0, False) // length
    flags = lax.dynamic_index_in_dim(key_mask.reshape(items, span), item, 0, False)
    key_ok = (jnp.arange(span, dtype=jnp.int32) < used * length) & (flags == 1)
    bias = jnp.where(jnp.concatenate([key_ok, jnp.zeros((length,), bool)]), 0.0, MASKED)
    bias = jnp.broadcast_to(full(bias)[:, None], (span + length, 128))
    def lists_of(s):
        picks = lax.dynamic_index_in_dim(random_blocks, (item - s) % items, 0, False)
        if s:
            picks = from_item(after(picks, joint_halves), s)
        chosen, usable = jax.vmap(lambda pick: block_lists(used, pick))(picks)
        marked = jnp.where(usable, chosen, blocks)
        return (used.reshape(1), member.reshape(1), chosen.reshape(-1), marked.reshape(-1), bias)

    lists = [lists_of(s) for s in range(items)]

    packed, made, merged, logs, joint_item = [], [], [], [], [joint]
    rows_in = first_all
    for s in range(items):
        if s == 0:
            group = [packed_rows for _, packed_rows in firsts]
            sent = after(sent, joint_halves)
            joint_others = [swap(rows, "dp", 1) for rows in joint_halves]
            own_sent = after(sent, group[-1])
            own_parts = {
                r: [from_member(array, -r) for array in own_sent] for r in range(1, members)
            }
            item_sent = [own_sent] + [[from_item(array, t) for array in sent] for t in away]
        else:
            halves = after((joint_halves[s - 1], joint_others[s - 1]), made[s - 1][0])
            weight = put_halves(upper, *halves)
            joint_item.append(weight)
            group = [run_project(rows, weight) for rows in rows_in]
        packed.append(group)
        outs, log_rows = attend_forward(sh, after(group, sent, joint_halves), lists[s], 0 if s else 64)
        made.append(outs)
        logs.append(log_rows)
        merged += [from_member(outs[r], -r) for r in range(members)]
        rows_in = after(first_all, outs[0], [arrays[0] for arrays in own_parts.values()])

    part_weights = {}
    for s, r in order:
        if (s, r) == (0, 0):
            part_weights[s, r] = [(array, 0) for array in own_weights]
        else:
            arrays = own_parts[r] if s == 0 else None
            if s:
                early = item_sent[s][:1] if width == model else item_sent[s]
                arrays = [from_member(array, -r) for array in after(early, packed[s])]
                arrays += item_sent[s][len(early) :]
            part_weights[s, r] = [(arrays[n], row) for n, row in views]

    def part_bias(part):
        if part == (0, 0):
            return inner_bias.reshape(1, -1)
        array, row = part_weights[part][3]
        terms = full(array[row : row + 3])
        return (terms[0] + terms[1] + terms[2]).reshape(1, -1)

    groups = [
        [(0, 0)],
        [part for part in order if part[0] > 0],
        [(0, r) for r in range(1, members)],
    ]
    groups = [group for group in groups if group]
    out_full = [part_weights[part][0] for part in order]
    acts, inner_grads = {}, {}

    def outer_product(part):
        return contract_rows(acts[part], cotangent)

    def inner_product(part):
        return contract_rows(second_own, inner_grads[part])

    def output_product(part):
        return contract_rows(merged[order.index(part)], branch)

    def send_members(product, s):
        return [from_member(low(product((s, r))), r) for r in range(members - 1, 0, -1)]

    def add_members(product, s, others):
        total = product((s, 0))
        for other in others:
            total = total + full(other)
        return low(total)

    totals = {}
    carried, waits = None, ()
    for n, group in enumerate(groups):
        head = tail = None
        if n == 0:
            lines = [row.reshape(1, -1) for row in (outer_bias, second_gain, second_shift)]
            head = (inputs, lines, merged)
        if n == len(groups) - 1:
            tail = [middle, second_gain.reshape(1, -1)]
        inner_parts = [part_weights[part][1] for part in group]
        if n == 1 and width == model:
            late = after([item_sent[s][1] for s in range(items)], acts[0, 0])
            inner_parts = [(from_member(late[s], -r), 0) for s, r in group]
        plain, group_acts, group_grads = run_middle(
            cotangent,
            jnp.concatenate([part_bias(part) for part in group], axis=1),
            inner_parts,
            [part_weights[part][2] for part in group],
            out_full,
            head,
            after(carried, waits) if carried else None,
            tail,
        )
        for part, act, grad in zip(group, group_acts, group_grads):
            acts[part], inner_grads[part] = act, grad
        if n == 0:
            second_own, middle = plain[:2]
            plain = plain[2:]
        if n < len(groups) - 1:
            carried = [second_own, *plain]
        waits = []
        for s in sorted({s for s, _ in group if s > 0}, reverse=True):
            for name, product in (("outer", outer_product), ("inner", inner_product)):
                totals[name, s] = add_members(product, s, send_members(product, s))
                waits.append(totals[name, s])
    outputs, middle_grad, branch, second_gain_sum, second_shift_sum, cot_sum = plain[:6]
    tops = plain[6:]

    top_rows = [[None] * members for _ in range(items)]
    for i, (s, r) in enumerate(order):
        top_rows[s][r] = from_member(tops[i], r)
    products = {"outer": outer_product, "inner": inner_product, "output": output_product}
    item_sent = {
        name: [from_item(totals[name, s], -s) for s in away] for name in ("outer", "inner")
    }
    member_sent = {name: send_members(product, 0) for name, product in products.items()}
    totals["outer", 0] = add_members(outer_product, 0, member_sent["outer"])
    for s in range(items - 1, -1, -1):
        others = send_members(output_product, s) if s else member_sent["output"]
        totals["output", s] = add_members(output_product, s, others)
    item_sent["output"] = [from_item(totals["output", s], -s) for s in away]

    def add_items(total, others):
        total = full(total)
        for other in others:
            total = total + full(other)
        return low(total)

    packed_grad, joint_totals = [None] * items, [None] * items
    outer_sum = GroupSum(
        add_items(totals["outer", 0], after(item_sent["outer"], branch)), (0,)
    )
    waits = (outer_sum.start(), member_sent, totals["output", 0])
    inner_sum = None
    back, joint_sent = {}, []
    for s in range(items - 1, -1, -1):
        grads = ()
        for part in range(BACK_PARTS):
            if part:
                waits = outer_sum.step(grads[0])
                if inner_sum is None:
                    others, second_own = after((item_sent, second_own), grads[0], waits)
                    totals["inner", 0] = add_members(inner_product, 0, member_sent["inner"])
                    inner_terms = [totals["inner", 0], *others["inner"]]
                    output_terms = [totals["output", 0], *others["output"]]
                    if width == model:
                        inner_total, bias_total = run_add(inner_terms, output_terms, model)
                    else:
                        inner_total = add_items(inner_terms[0], inner_terms[1:])
                        bias_total = full(inner_total[model : model + 1])
                        inner_total = inner_total[:model]
                        output_sum = GroupSum(add_items(output_terms[0], output_terms[1:]), (0,))
                    inner_sum = GroupSum(inner_total, (1,))
                    waits = (waits, inner_sum.start(), outer_sum.step(inner_total))
                else:
                    waits = (waits, inner_sum.step(grads[0]), joint_sent)
            grads = attend_backward(
                sh,
                packed[s],
                after(top_rows[s], waits),
                made[s],
                logs[s],
                lists[s],
                (part, BACK_PARTS),
                grads,
            )
        packed_grad[s] = grads
        waits = inner_sum.step(grads[0])
        rows = after(grads, waits, outer_sum.step(grads[0]) if s else ())
        total = contract_rows(rows[0], first_all[0])
        for r in range(1, members):
            total = total + contract_rows(rows[r], first_all[r])
        joint_totals[s] = low(total) if s else total
        grads = after(grads, waits)
        waits = joint_totals[s]
        if s:
            grads = after(grads, waits)
            joint_sent.append(from_item(joint_totals[s], -s))
        for r in range(members):
            back[s, r] = from_member(grads[r], -r)

    back = [back[part] for part in order]
    joint_full = [from_member(joint_item[s], -r) for s, r in order]
    end_sum = GroupSum(add_items(joint_totals[0], joint_sent), (0,))
    waits = end_sum.start()
    pieces = []
    cut = local_rows // LAST_PARTS
    for n in range(LAST_PARTS):
        outs = run_last(
            n,
            cut,
            inputs,
            middle_grad,
            first_gain.reshape(1, -1),
            after(back, waits),
            joint_full,
            pieces[-1][0] if pieces else None,
        )
        pieces.append(outs)
        if n == 0:
            waits = end_sum.step(outs[1])
    input_grad = pieces[-1][0]
    vectors = [
        sum(piece[1] for piece in pieces),
        sum(piece[2] for piece in pieces),
        second_gain_sum,
        second_shift_sum,
        cot_sum,
        lax.dynamic_update_slice(jnp.zeros((tensor, width), jnp.float32), bias_total, (place, 0)),
    ]
    vectors = after(vectors, end_sum.step(), inner_sum.step(pieces[-1][1]))
    small = sum_all(jnp.concatenate([vector.reshape(-1) for vector in vectors]))
    bias_grad = lax.dynamic_slice_in_dim(small, 5 * model + place * width, width, 0)
    small = small[: 5 * model].reshape(5, model)
    end_grad = end_sum.result()
    outer_grad, inner_grad = outer_sum.result(), inner_sum.result()
    if width == model:
        inner_grad, output_grad = inner_grad[:model], inner_grad[model:]
    else:
        output_grad = output_sum.result()
    return (
        outputs,
        input_grad,
        end_grad[:lanes],
        end_grad[lanes : 2 * lanes],
        end_grad[2 * lanes :],
        output_grad,
        inner_grad,
        bias_grad,
        outer_grad,
        small[4],
        small[0],
        small[1],
        small[2],
        small[3],
    )


def solution(mesh):
    placed = (
        P(("dp", "tensor"), None),
        P("tensor", None),
        P("tensor", None),
        P("tensor", None),
        P("tensor", None),
        P(None, "tensor"),
        P("tensor"),
        P("tensor", None),
        P(),
        P(),
        P(),
        P(),
        P(),
        P("dp"),
        P("dp"),
        P("dp", "tensor", None, None),
        P(("dp", "tensor"), None),
    )
    return jax.shard_map(
        per_device,
        mesh=mesh,
        in_specs=placed,
        out_specs=(
            P(("dp", "tensor"), None),
            P(("dp", "tensor"), None),
            P("tensor", None),
            P("tensor", None),
            P("tensor", None),
            P("tensor", None),
            P(None, "tensor"),
            P("tensor"),
            P("tensor", None),
            P(),
            P(),
            P(),
            P(),
            P(),
        ),
        check_vma=False,
    )
```

time: 1010 us -> 669 us (0.66)
  Pallas kernels: 108 us -> 383 us
  matrix products: 274 us -> 88.5 us
  starting transfers between devices: 195 us -> 42 us
  waiting for transfers between devices: 161 us -> 69.4 us
  local copies, waits for them, and re-layouts: 123 us -> 39.8 us
  other arithmetic: 80.5 us -> 28.4 us
  blocking collectives: 47.5 us -> 0 us
    pallas_call x2 -> x16, Pallas kernels: 72.7 us -> 316 us  [the longest x4 139 us: attend_backward(): pl.pallas_call(functools.partial(backward_kernel, sh, pieces, unroll, par...]
    dot_general x11 -> x0, matrix products: 190 us -> none  [the longest x7 102 us: contract_cols(): lax.dot_general(left, right, (((1,), (1,)), ((), ())), preferred_element_...]
    ppermute x36 -> x32, starting transfers between devices: 162 us -> 30.1 us  [swap(): return lax.ppermute(values, axis, [(i, i ^ bit) for i in range(size)])]
    ppermute x9 -> x8, waiting for transfers between devices: 86.5 us -> 26.9 us  [from_item(): return lax.ppermute(values, 'tensor', pairs)]
    unnamed x117 -> x159, local copies, waits for them, and re-layouts: 80.4 us -> 24.6 us
    psum x1 -> x0, blocking collectives: 41.9 us -> none  [per_device(): lax.psum(jnp.concatenate([jnp.stack([jnp.sum(grad_top, axis=0), first_gai...]
    ppermute x36 -> x32, waiting for transfers between devices: 72.7 us -> 39.2 us  [swap(): return lax.ppermute(values, axis, [(i, i ^ bit) for i in range(size)])]
    pallas_call x2, Pallas kernels: 35.3 us -> 67.5 us  [attend_forward(): pl.pallas_call(functools.partial(forward_kernel, sh, pieces, unroll), in_...]
  transfers between devices with their start and end apart: 66 -> 59, of which waited for: 21 -> 12; matrix products, arithmetic and copies ran while one was open for 28% -> 18% of each run, Pallas kernels for 11% -> 51%
where the time goes in v2:
time: 669 us; the launch traced here: 657 us
  Pallas kernels  383 us (57%)
  matrix products  88.5 us (13%)
  waiting for transfers between devices  69.4 us (10%)
  starting transfers between devices  42 us (6%)
  local copies, waits for them, and re-layouts  39.8 us (6%)
  other arithmetic  28.4 us (4%)
    pallas_call x4, Pallas kernels, attend_backward(): pl.pallas_call(functools.partial(backward_kernel, sh, pieces, unroll, par...  139 us
    pallas_call x3, Pallas kernels, run_middle(): pl.pallas_call(functools.partial(middle_kernel, count, outs_count, head i...  118 us
    dot_general x16, matrix products, contract_rows(): lax.dot_general(left, right, (((0,), (0,)), ((), ())), preferred_element_...  88.5 us
    pallas_call x2, Pallas kernels, attend_forward(): pl.pallas_call(functools.partial(forward_kernel, sh, pieces, unroll), in_...  67.5 us
    ppermute x32, waiting for transfers between devices, swap(): return lax.ppermute(values, axis, [(i, i ^ bit) for i in range(size)])  39.2 us
    ppermute x32, starting transfers between devices, swap(): return lax.ppermute(values, axis, [(i, i ^ bit) for i in range(size)])  30.1 us
    pallas_call x2, Pallas kernels, run_last(): pl.pallas_call(functools.partial(last_kernel, parts), grid=(part_rows //...  28.2 us
    ppermute x8, waiting for transfers between devices, from_item(): return lax.ppermute(values, 'tensor', pairs)  26.9 us
  transfers between devices with their start and end apart: 59, of which 12 were waited for; matrix products, arithmetic and copies ran while one was open for 18% of the time, Pallas kernels for 51%

profile of v2, /device:TPU:18, one launch (start us, length us, event | category | flops | bytes accessed | tf_op | source)
XLA Modules:
  0.0 656.6 jit_solution(4557148514721586722)
XLA Ops:
  9.4 14.9 %collective-permute-done = bf16[384,1024]{1,0:T(8,128)(2,1)} collective-permute-done((bf16[384,1024]{1,0:T(8,128)(2,1)S(1)}, bf16[384,1024]{1,0:T(8,128)(2,1)}, u32[]{:S(2)}, u32[]{:S(2)}) %collective-permute-start) | collective-permute-done | bytes 786464 | tf_op jit(solution)/shard_map/ppermute | solution.py:1030
  29.1 7.1 %first.3 = (bf16[2048,1024]{1,0:T(8,128)(2,1)S(1)}, bf16[2048,768]{1,0:T(8,128)(2,1)S(1)}) custom-call(bf16[2048,1024]{1,0:T(8,128)(2,1)S(1)} %copy-done, f32[1,1024]{1,0:T(1,128)S(1)} %bitcast.56, f32[1,1024]{1,0:T(1,128)S(1)} %bitcast.60, bf16[768,1024]{1,0:T(8,128)(2,1)S(1)} %copy-done.1), custom_call_target="tpu_custom_call" | custom-call | flops 2097152 | bytes 1000000 | tf_op jit(solution)/shard_map/first/pallas_call | solution.py:782
  44.1 8.9 %first.2 = (bf16[2048,1024]{1,0:T(8,128)(2,1)S(1)}, bf16[2048,768]{1,0:T(8,128)(2,1)S(1)}) custom-call(bf16[2048,1024]{1,0:T(8,128)(2,1)} %collective-permute-done.1.resid_ref, f32[1,1024]{1,0:T(1,128)S(1)} %bitcast.57, f32[1,1024]{1,0:T(1,128)S(1)} %bitcast.61, bf16[768,1024]{1,0:T(8,128)(2,1)S(1)} %copy-done.1), custom_call_target="tpu_custom_call" | custom-call | flops 2097152 | bytes 1000000 | tf_op jit(solution)/shard_map/first/pallas_call | solution.py:782
  53.7 33.6 %attend_forward.2 = (bf16[2048,256]{1,0:T(8,128)(2,1)S(1)}, bf16[2048,256]{1,0:T(8,128)(2,1)S(1)}, f32[64,256]{1,0:T(8,128)S(1)}) custom-call(s32[1]{0:T(128)} %bitcast.7.used, s32[1]{0:T(128)} %bitcast.8.member, s32[2048]{0:T(1024)S(1)} %min.18.idx, s32[2048]{0:T(1024)S(1)} %broadcast_select_fusion.1.bidx, bf16[2048,768]{1,0:T(8,128)(2,1)S(1)} %copy-done.31, ...), custom_call_target="tpu_custom_call" | custom-call | flops 137438953472 | bytes 1000000 | tf_op jit(solution)/shard_map/attend_forward/pallas_call | solution.py:418
  90.5 4.1 project.3.refs_1_
  108.5 33.8 %attend_forward.3 = (bf16[2048,256]{1,0:T(8,128)(2,1)S(1)}, bf16[2048,256]{1,0:T(8,128)(2,1)S(1)}, f32[64,256]{1,0:T(8,128)S(1)}) custom-call(s32[1]{0:T(128)} %bitcast.7.used, s32[1]{0:T(128)} %bitcast.8.member, s32[2048]{0:T(1024)S(1)} %min.20.idx, s32[2048]{0:T(1024)S(1)} %broadcast_select_fusion.bidx, bf16[2048,768]{1,0:T(8,128)(2,1)S(1)} %copy-done.13, ...), custom_call_target="tpu_custom_call" | custom-call | bytes 1000000 | tf_op jit(solution)/shard_map/attend_forward/pallas_call | solution.py:418
  147.1 34.5 %middle.3 = (bf16[2048,1040]{1,0:T(8,128)(2,1)}, f32[2048,1024]{1,0:T(8,128)}, f32[2048,1024]{1,0:T(8,128)}, f32[2048,1024]{1,0:T(8,128)}, bf16[2048,1024]{1,0:T(8,128)(2,1)}, /*index=5*/bf16[2048,1024]{1,0:T(8,128)(2,1)}) custom-call(bf16[2048,1024]{1,0:T(8,128)(2,1)} %refs_0_.11, f32[1,1024]{1,0:T(1,128)} %bitcast.69, bf16[2048,1024]{1,0:T(8,128)(2,1)} %refs_0_.13, ...), custom_call_target="tpu_custom_call" | custom-call | flops 2097152 | bytes 1000000 | tf_op jit(solution)/shard_map/middle/pallas_call | solution.py:685
  187.3 46.5 %middle.4 = (f32[2048,1024]{1,0:T(8,128)}, f32[2048,1024]{1,0:T(8,128)}, bf16[2048,1024]{1,0:T(8,128)(2,1)}, bf16[2048,1024]{1,0:T(8,128)(2,1)}, bf16[2048,1024]{1,0:T(8,128)(2,1)}, /*index=5*/bf16[2048,1024]{1,0:T(8,128)(2,1)}) custom-call(bf16[2048,1024]{1,0:T(8,128)(2,1)} %refs_0_.11, f32[1,2048]{1,0:T(1,128)} %pad_maximum_fusion.refs_1_, ...), custom_call_target="tpu_custom_call" | custom-call | flops 2097152 | bytes 1000000 | tf_op jit(solution)/shard_map/middle/pallas_call | solution.py:685
  233.9 9.5 %convolution_convert_fusion.3 = bf16[1024,1024]{1,0:T(8,128)(2,1)} fusion(bf16[2048,1024]{1,0:T(8,128)(2,1)} %get-tuple-element.169, bf16[2048,1024]{1,0:T(8,128)(2,1)} %refs_0_.11), kind=kOutput, calls=%fused_computation.16 | convolution fusion | flops 4296015872 | bytes 10485760 | tf_op jit(solution)/shard_map/dot_general | solution.py:22
  243.7 5.8 convolution_convert_fusion.1
  251.4 10.1 %add_convert_fusion.2 = bf16[1024,1024]{1,0:T(8,128)(2,1)} fusion(bf16[1024,1024]{1,0:T(8,128)(2,1)} %collective-permute-done.11, bf16[2048,1024]{1,0:T(8,128)(2,1)} %get-tuple-element.168, bf16[2048,1024]{1,0:T(8,128)(2,1)} %refs_0_.11), kind=kOutput, calls=%fused_computation.4 | convolution fusion | flops 4298113024 | bytes 12582912 | tf_op jit(solution)/shard_map/dot_general | solution.py:22
  261.6 8.8 %fusion = bf16[1040,1024]{1,0:T(8,128)(2,1)} fusion(bf16[1040,1024]{1,0:T(8,128)(2,1)} %collective-permute-done.12, bf16[2048,1040]{1,0:T(8,128)(2,1)} %get-tuple-element.191.refs_2_, bf16[2048,1024]{1,0:T(8,128)(2,1)S(1)} %copy-done.65), kind=kOutput, calls=%fused_computation.5 | convolution fusion | flops 4365271040 | bytes 12713984 | tf_op jit(solution)/shard_map/dot_general | solution.py:22
  270.3 37.2 %middle.5 = (bf16[2048,1024]{1,0:T(8,128)(2,1)}, f32[2048,1024]{1,0:T(8,128)}, bf16[2048,1024]{1,0:T(8,128)(2,1)}, f32[1,1024]{1,0:T(1,128)}, f32[1,1024]{1,0:T(...) custom-call(bf16[2048,1024]{1,0:T(8,128)(2,1)} %refs_0_.11, ...), custom_call_target="tpu_custom_call" | custom-call | flops 2097152 | bytes 1000000 | tf_op jit(solution)/shard_map/middle/pallas_call | solution.py:685
  314.2 5.2 convolution_convert_fusion.2
  319.6 5.8 convolution_convert_fusion
  325.8 4.6 fusion.12
  344.5 31.9 %attend_backward.4 = (bf16[2048,768]{1,0:T(8,128)(2,1)S(1)}, bf16[2048,768]{1,0:T(8,128)(2,1)S(1)}) custom-call(s32[1]{0:T(128)} %bitcast.7.used, s32[1]{0:T(128)} %bitcast.8.member, s32[2048]{0:T(1024)S(1)} %min.20.idx, s32[2048]{0:T(1024)S(1)} %broadcast_select_fusion.bidx, bf16[2048,768]{1,0:T(8,128)(2,1)S(1)} %copy-done.14, ...), custom_call_target="tpu_custom_call" | custom-call | flops 34359738368 | bytes 1000000 | tf_op jit(solution)/shard_map/attend_backward/pallas_call | solution.py:441
  379.4 12.0 %collective-permute-done.26.refs_3_ = bf16[256,1024]{1,0:T(8,128)(2,1)S(1)} collective-permute-done((bf16[256,1024]{1,0:T(8,128)(2,1)S(1)}, bf16[256,1024]{1,0:T(8,128)(2,1)S(1)}, u32[]{:S(2)}, u32[]{:S(2)}) %collective-permute-start.26) | collective-permute-done | bytes 524320 | tf_op jit(solution)/shard_map/ppermute | solution.py:1030
  391.4 8.3 %fusion.1.refs_0_ = bf16[1040,1024]{1,0:T(8,128)(2,1)S(1)} fusion(bf16[1040,1024]{1,0:T(8,128)(2,1)S(1)} %copy-done.72, bf16[2048,1040]{1,0:T(8,128)(2,1)} %get-tuple-element.191.refs_2_, bf16[2048,1024]{1,0:T(8,128)(2,1)} %get-tuple-element.192), kind=kOutput, calls=%fused_computation.6 | convolution fusion | flops 4365271040 | bytes 12713984 | tf_op jit(solution)/shard_map/dot_general | solution.py:22
  408.6 37.9 %attend_backward.5 = (bf16[2048,768]{1,0:T(8,128)(2,1)S(1)}, bf16[2048,768]{1,0:T(8,128)(2,1)}) custom-call(s32[1]{0:T(128)} %bitcast.7.used, s32[1]{0:T(128)} %bitcast.8.member, s32[2048]{0:T(1024)S(1)} %min.20.idx, s32[2048]{0:T(1024)S(1)} %broadcast_select_fusion.bidx, bf16[2048,768]{1,0:T(8,128)(2,1)S(1)} %copy-done.14, bf16[2048,768]{1,0:T(8,128)(2,1)} %copy-done.10, ...), custom_call_target="tpu_custom_call" | custom-call | flops 34359738368 | bytes 1000000 | tf_op jit(solution)/shard_map/attend_backward/pallas_call | solution.py:441
  451.6 4.6 collective-permute-start.33
  459.8 5.5 add_convert_fusion.4
  466.9 32.1 %attend_backward.6 = (bf16[2048,768]{1,0:T(8,128)(2,1)S(1)}, bf16[2048,768]{1,0:T(8,128)(2,1)S(1)}) custom-call(s32[1]{0:T(128)} %bitcast.7.used, s32[1]{0:T(128)} %bitcast.8.member, s32[2048]{0:T(1024)S(1)} %min.18.idx, s32[2048]{0:T(1024)S(1)} %copy-done.29, bf16[2048,768]{1,0:T(8,128)(2,1)S(1)} %copy-done.32, bf16[2048,768]{1,0:T(8,128)(2,1)} %copy-done.33, ...), custom_call_target="tpu_custom_call" | custom-call | flops 34359738368 | bytes 1000000 | tf_op jit(solution)/shard_map/attend_backward/pallas_call | solution.py:441
  503.4 4.3 collective-permute-start.38
  507.7 37.4 %attend_backward.7 = (bf16[2048,768]{1,0:T(8,128)(2,1)S(1)}, bf16[2048,768]{1,0:T(8,128)(2,1)}) custom-call(s32[1]{0:T(128)} %bitcast.7.used, s32[1]{0:T(128)} %bitcast.8.member, s32[2048]{0:T(1024)S(1)} %min.18.idx, s32[2048]{0:T(1024)S(1)} %copy-done.29, bf16[2048,768]{1,0:T(8,128)(2,1)S(1)} %copy-done.32, bf16[2048,768]{1,0:T(8,128)(2,1)} %copy-done.33, ...), custom_call_target="tpu_custom_call" | custom-call | flops 34359738368 | bytes 1000000 | tf_op jit(solution)/shard_map/attend_backward/pallas_call | solution.py:441
  548.0 6.3 fusion.14
  554.4 5.4 add_convert_fusion.3
  564.2 14.1 %last.2 = (f32[2048,1024]{1,0:T(8,128)}, f32[1,1024]{1,0:T(1,128)S(1)}, f32[1,1024]{1,0:T(1,128)S(1)}) custom-call(bf16[2048,1024]{1,0:T(8,128)(2,1)} %refs_0_.13, f32[2048,1024]{1,0:T(8,128)} %get-tuple-element.177.refs_1_, f32[1,1024]{1,0:T(1,128)S(1)} %bitcast.58, bf16[2048,768]{1,0:T(8,128)(2,1)S(1)} %copy-done.9, ...), custom_call_target="tpu_custom_call" | custom-call | flops 6442450944 | bytes 20971520 | tf_op jit(solution)/shard_map/last/pallas_call | solution.py:855
  587.4 14.1 %last.3 = (f32[2048,1024]{1,0:T(8,128)}, f32[1,1024]{1,0:T(1,128)S(1)}, f32[1,1024]{1,0:T(1,128)S(1)}) custom-call(bf16[2048,1024]{1,0:T(8,128)(2,1)} %refs_0_.13, f32[2048,1024]{1,0:T(8,128)} %get-tuple-element.177.refs_1_, f32[1,1024]{1,0:T(1,128)S(1)} %bitcast.59, bf16[2048,768]{1,0:T(8,128)(2,1)S(1)} %copy-done.9, ...), custom_call_target="tpu_custom_call", output_to_operand_aliasing={{0}: (11, {})} | custom-call | flops 6442450944 | bytes 20971520 | tf_op jit(solution)/shard_map/last/pallas_call | solution.py:855
  609.7 4.9 collective-permute-done.47
  614.7 8.0 %collective-permute-done.48 = bf16[96,1024]{1,0:T(8,128)(2,1)S(1)} collective-permute-done((bf16[96,1024]{1,0:T(8,128)(2,1)S(1)}, bf16[96,1024]{1,0:T(8,128)(2,1)S(1)}, u32[]{:S(2)}, u32[]{:S(2)}) %collective-permute-start.48) | collective-permute-done | bytes 196640 | tf_op jit(solution)/shard_map/ppermute | solution.py:878
  632.2 14.9 %collective-permute-done.55 = f32[9216]{0:T(1024)S(1)} collective-permute-done((f32[9216]{0:T(1024)S(1)}, f32[9216]{0:T(1024)S(1)}, u32[]{:S(2)}, u32[]{:S(2)}) %collective-permute-start.55) | collective-permute-done | bytes 36896 | tf_op jit(solution)/shard_map/ppermute | solution.py:878
  (370 shorter events, 139.2 us)
Async XLA Ops:
  0.7 43.4 %collective-permute-start.1 = (bf16[2048,1024]{1,0:T(8,128)(2,1)}, bf16[2048,1024]{1,0:T(8,128)(2,1)}, u32[]{:S(2)}, u32[]{:S(2)}) collective-permute-start(bf16[2048,1024]{1,0:T(8,128)(2,1)} %refs_0_.13), channel_id=1, source_target_pairs={{0,1},{1,0},{2,3},{3,2},{4,5},{5,4},{6,7},{7,6},{8,9},{9,8},{10,11... | collective-permute-start | bytes 12582920 | tf_op jit(solution)/shard_map/ppermute | solution.py:1038
  39.8 62.2 %collective-permute-start.7 = (bf16[1296,1024]{1,0:T(8,128)(2,1)}, bf16[1296,1024]{1,0:T(8,128)(2,1)}, u32[]{:S(2)}, u32[]{:S(2)}) collective-permute-start(bf16[1296,1024]{1,0:T(8,128)(2,1)} %bundle.2), channel_id=1, source_target_pairs={{0,2},{1,3},{2,0},{3,1},{4,6},{5,7},{6,4},{7,5},{8,10},{9,11},{10,... | collective-permute-start | bytes 7962632 | tf_op jit(solution)/shard_map/ppermute | solution.py:1030
  41.3 46.1 %collective-permute-start.5 = (bf16[384,1024]{1,0:T(8,128)(2,1)}, bf16[384,1024]{1,0:T(8,128)(2,1)}, u32[]{:S(2)}, u32[]{:S(2)}) collective-permute-start(bf16[384,1024]{1,0:T(8,128)(2,1)} %collective-permute-done), channel_id=1, source_target_pairs={{0,4},{4,0},{8,12},{12,8},{16,20},{20,16},{24,28},{28,24},{1,5},{5... | collective-permute-start | bytes 2359304 | tf_op jit(solution)/shard_map/ppermute | solution.py:878
  53.0 37.4 %collective-permute-start.2 = (bf16[1296,1024]{1,0:T(8,128)(2,1)}, bf16[1296,1024]{1,0:T(8,128)(2,1)S(1)}, u32[]{:S(2)}, u32[]{:S(2)}) collective-permute-start(bf16[1296,1024]{1,0:T(8,128)(2,1)} %bundle.2), channel_id=1, source_target_pairs={{0,1},{1,0},{2,3},{3,2},{4,5},{5,4},{6,7},{7,6},{8,9},{9,8},{10,11... | collective-permute-start | bytes 7962632 | tf_op jit(solution)/shard_map/ppermute | solution.py:1038
  102.1 44.1 %collective-permute-start.8 = (bf16[1296,1024]{1,0:T(8,128)(2,1)}, bf16[1296,1024]{1,0:T(8,128)(2,1)}, u32[]{:S(2)}, u32[]{:S(2)}) collective-permute-start(bf16[1296,1024]{1,0:T(8,128)(2,1)} %collective-permute-done.7.refs_12_.refs_7_.refs_9_), channel_id=1, source_target_pairs={{0,1},{1,0},{2,3},{3,2},{4,5},{5,4},{6,7},{7,6},{8,9},{9,8},{10,11... | collective-permute-start | bytes 7962632 | tf_op jit(solution)/shard_map/ppermute | solution.py:1038
  102.6 79.0 %collective-permute-start.9 = (bf16[1024,1024]{1,0:T(8,128)(2,1)}, bf16[1024,1024]{1,0:T(8,128)(2,1)}, u32[]{:S(2)}, u32[]{:S(2)}) collective-permute-start(bf16[1024,1024]{1,0:T(8,128)(2,1)} %refs_14_.1), channel_id=1, source_target_pairs={{0,2},{1,3},{2,0},{3,1},{4,6},{5,7},{6,4},{7,5},{8,10},{9,11},{10,... | collective-permute-start | bytes 6291464 | tf_op jit(solution)/shard_map/ppermute | solution.py:1030
  103.1 41.8 %collective-permute-start.3 = (bf16[2048,256]{1,0:T(8,128)(2,1)S(1)}, bf16[2048,256]{1,0:T(8,128)(2,1)S(1)}, u32[]{:S(2)}, u32[]{:S(2)}) collective-permute-start(bf16[2048,256]{1,0:T(8,128)(2,1)S(1)} %get-tuple-element.144.refs_5_), channel_id=1, source_target_pairs={{0,1},{1,0},{2,3},{3,2},{4,5},{5,4},{6,7},{7,6},{8,9},{9,8},{10,11... | collective-permute-start | bytes 3145736 | tf_op jit(solution)/shard_map/ppermute | solution.py:1038
  249.7 20.6 %collective-permute-start.13 = (bf16[1024,1024]{1,0:T(8,128)(2,1)}, bf16[1024,1024]{1,0:T(8,128)(2,1)}, u32[]{:S(2)}, u32[]{:S(2)}) collective-permute-start(bf16[1024,1024]{1,0:T(8,128)(2,1)} %refs_14_.1), channel_id=1, source_target_pairs={{0,1},{1,0},{2,3},{3,2},{4,5},{5,4},{6,7},{7,6},{8,9},{9,8},{10,11... | collective-permute-start | bytes 6291464 | tf_op jit(solution)/shard_map/ppermute | solution.py:1038
  261.5 75.6 %collective-permute-start.16 = (bf16[1024,1024]{1,0:T(8,128)(2,1)}, bf16[1024,1024]{1,0:T(8,128)(2,1)S(1)}, u32[]{:S(2)}, u32[]{:S(2)}) collective-permute-start(bf16[1024,1024]{1,0:T(8,128)(2,1)} %add_convert_fusion.2), channel_id=1, source_target_pairs={{0,2},{1,3},{2,0},{3,1},{4,6},{5,7},{6,4},{7,5},{8,10},{9,11},{10,... | collective-permute-start | bytes 6291464 | tf_op jit(solution)/shard_map/ppermute | solution.py:1030
  313.8 22.0 %collective-permute-start.20 = (bf16[256,1024]{1,0:T(8,128)(2,1)}, bf16[256,1024]{1,0:T(8,128)(2,1)S(1)}, u32[]{:S(2)}, u32[]{:S(2)}) collective-permute-start(bf16[256,1024]{1,0:T(8,128)(2,1)} %convolution_convert_fusion.5), channel_id=1, source_target_pairs={{0,1},{1,0},{2,3},{3,2},{4,5},{5,4},{6,7},{7,6},{8,9},{9,8},{10,11... | collective-permute-start | bytes 1572872 | tf_op jit(solution)/shard_map/ppermute | solution.py:1038
  331.2 60.2 %collective-permute-start.24 = (bf16[1040,1024]{1,0:T(8,128)(2,1)}, bf16[1040,1024]{1,0:T(8,128)(2,1)S(1)}, u32[]{:S(2)}, u32[]{:S(2)}) collective-permute-start(bf16[1040,1024]{1,0:T(8,128)(2,1)} %fusion), channel_id=1, source_target_pairs={{0,2},{1,3},{2,0},{3,1},{4,6},{5,7},{6,4},{7,5},{8,10},{9,11},{10,... | collective-permute-start | bytes 6389768 | tf_op jit(solution)/shard_map/ppermute | solution.py:1030
  338.5 126.9 %collective-permute-start.14 = (bf16[2048,256]{1,0:T(8,128)(2,1)}, bf16[2048,256]{1,0:T(8,128)(2,1)S(1)}, u32[]{:S(2)}, u32[]{:S(2)}) collective-permute-start(bf16[2048,256]{1,0:T(8,128)(2,1)} %get-tuple-element.179), channel_id=1, source_target_pairs={{0,1},{1,0},{2,3},{3,2},{4,5},{5,4},{6,7},{7,6},{8,9},{9,8},{10,11... | collective-permute-start | bytes 3145736 | tf_op jit(solution)/shard_map/ppermute | solution.py:1038
  339.1 52.4 %collective-permute-start.26 = (bf16[256,1024]{1,0:T(8,128)(2,1)S(1)}, bf16[256,1024]{1,0:T(8,128)(2,1)S(1)}, u32[]{:S(2)}, u32[]{:S(2)}) collective-permute-start(bf16[256,1024]{1,0:T(8,128)(2,1)S(1)} %fusion.4), channel_id=1, source_target_pairs={{0,2},{1,3},{2,0},{3,1},{4,6},{5,7},{6,4},{7,5},{8,10},{9,11},{10,... | collective-permute-start | bytes 1572872 | tf_op jit(solution)/shard_map/ppermute | solution.py:1030
  343.0 33.4 %collective-permute-start.17 = (bf16[512,1024]{1,0:T(8,128)(2,1)S(1)}, bf16[512,1024]{1,0:T(8,128)(2,1)}, u32[]{:S(2)}, u32[]{:S(2)}) collective-permute-start(bf16[512,1024]{1,0:T(8,128)(2,1)S(1)} %constant_dynamic-slice_fusion.11), channel_id=1, source_target_pairs={{0,4},{4,0},{8,12},{12,8},{16,20},{20,16},{24,28},{28,24},{1,5},{5... | collective-permute-start | bytes 3145736 | tf_op jit(solution)/shard_map/ppermute | solution.py:878
  379.2 22.3 %collective-permute-start.21 = (bf16[128,1024]{1,0:T(8,128)(2,1)S(1)}, bf16[128,1024]{1,0:T(8,128)(2,1)S(1)}, u32[]{:S(2)}, u32[]{:S(2)}) collective-permute-start(bf16[128,1024]{1,0:T(8,128)(2,1)S(1)} %get-tuple-element.270), channel_id=1, source_target_pairs={{0,8},{4,12},{8,0},{12,4},{16,24},{20,28},{24,16},{28,20},{1,9},{5... | collective-permute-start | bytes 786440 | tf_op jit(solution)/shard_map/ppermute | solution.py:878
  379.3 22.3 %collective-permute-start.22 = (bf16[128,1024]{1,0:T(8,128)(2,1)S(1)}, bf16[128,1024]{1,0:T(8,128)(2,1)S(1)}, u32[]{:S(2)}, u32[]{:S(2)}) collective-permute-start(bf16[128,1024]{1,0:T(8,128)(2,1)S(1)} %get-tuple-element.269), channel_id=1, source_target_pairs={{0,16},{4,20},{8,24},{12,28},{16,0},{20,4},{24,8},{28,12},{1,17},{... | collective-permute-start | bytes 786440 | tf_op jit(solution)/shard_map/ppermute | solution.py:878
  401.6 45.8 %collective-permute-start.31 = (bf16[640,1024]{1,0:T(8,128)(2,1)}, bf16[640,1024]{1,0:T(8,128)(2,1)}, u32[]{:S(2)}, u32[]{:S(2)}) collective-permute-start(bf16[640,1024]{1,0:T(8,128)(2,1)} %constant_dynamic-slice_fusion.7), channel_id=1, source_target_pairs={{0,8},{4,12},{8,0},{12,4},{16,24},{20,28},{24,16},{28,20},{1,9},{5... | collective-permute-start | bytes 3932168 | tf_op jit(solution)/shard_map/ppermute | solution.py:878
  405.1 41.4 %collective-permute-start.27 = (bf16[128,1024]{1,0:T(8,128)(2,1)S(1)}, bf16[128,1024]{1,0:T(8,128)(2,1)S(1)}, u32[]{:S(2)}, u32[]{:S(2)}) collective-permute-start(bf16[128,1024]{1,0:T(8,128)(2,1)S(1)} %add_convert_fusion.9), channel_id=1, source_target_pairs={{0,8},{4,12},{8,0},{12,4},{16,24},{20,28},{24,16},{28,20},{1,9},{5... | collective-permute-start | bytes 786440 | tf_op jit(solution)/shard_map/ppermute | solution.py:878
  405.2 41.4 %collective-permute-start.28 = (bf16[128,1024]{1,0:T(8,128)(2,1)S(1)}, bf16[128,1024]{1,0:T(8,128)(2,1)S(1)}, u32[]{:S(2)}, u32[]{:S(2)}) collective-permute-start(bf16[128,1024]{1,0:T(8,128)(2,1)S(1)} %add_convert_fusion.9), channel_id=1, source_target_pairs={{0,16},{4,20},{8,24},{12,28},{16,0},{20,4},{24,8},{28,12},{1,17},{... | collective-permute-start | bytes 786440 | tf_op jit(solution)/shard_map/ppermute | solution.py:878
  407.1 39.4 %collective-permute-start.29 = (bf16[128,1024]{1,0:T(8,128)(2,1)S(1)}, bf16[128,1024]{1,0:T(8,128)(2,1)S(1)}, u32[]{:S(2)}, u32[]{:S(2)}) collective-permute-start(bf16[128,1024]{1,0:T(8,128)(2,1)S(1)} %add_convert_fusion.9), channel_id=1, source_target_pairs={{0,24},{4,28},{8,16},{12,20},{16,8},{20,12},{24,0},{28,4},{1,25},{... | collective-permute-start | bytes 786440 | tf_op jit(solution)/shard_map/ppermute | solution.py:878
  447.3 51.7 %collective-permute-start.30 = (bf16[512,1024]{1,0:T(8,128)(2,1)S(1)}, bf16[512,1024]{1,0:T(8,128)(2,1)S(1)}, u32[]{:S(2)}, u32[]{:S(2)}) collective-permute-start(bf16[512,1024]{1,0:T(8,128)(2,1)S(1)} %maximum_select_fusion.5), channel_id=1, source_target_pairs={{0,4},{4,0},{8,12},{12,8},{16,20},{20,16},{24,28},{28,24},{1,5},{5... | collective-permute-start | bytes 3145736 | tf_op jit(solution)/shard_map/ppermute | solution.py:878
  449.9 53.1 %collective-permute-start.32 = (bf16[160,1024]{1,0:T(8,128)(2,1)S(1)}, bf16[160,1024]{1,0:T(8,128)(2,1)S(1)}, u32[]{:S(2)}, u32[]{:S(2)}) collective-permute-start(bf16[160,1024]{1,0:T(8,128)(2,1)S(1)} %get-tuple-element.267), channel_id=1, source_target_pairs={{0,4},{4,0},{8,12},{12,8},{16,20},{20,16},{24,28},{28,24},{1,5},{5... | collective-permute-start | bytes 983048 | tf_op jit(solution)/shard_map/ppermute | solution.py:878
  451.6 51.4 %collective-permute-start.33 = (bf16[160,1024]{1,0:T(8,128)(2,1)S(1)}, bf16[160,1024]{1,0:T(8,128)(2,1)S(1)}, u32[]{:S(2)}, u32[]{:S(2)}) collective-permute-start(bf16[160,1024]{1,0:T(8,128)(2,1)S(1)} %get-tuple-element.266), channel_id=1, source_target_pairs={{0,16},{4,20},{8,24},{12,28},{16,0},{20,4},{24,8},{28,12},{1,17},{... | collective-permute-start | bytes 983048 | tf_op jit(solution)/shard_map/ppermute | solution.py:878
  456.2 46.7 %collective-permute-start.34 = (bf16[160,1024]{1,0:T(8,128)(2,1)S(1)}, bf16[160,1024]{1,0:T(8,128)(2,1)S(1)}, u32[]{:S(2)}, u32[]{:S(2)}) collective-permute-start(bf16[160,1024]{1,0:T(8,128)(2,1)S(1)} %get-tuple-element.265), channel_id=1, source_target_pairs={{0,20},{4,16},{8,28},{12,24},{16,4},{20,0},{24,12},{28,8},{1,21},{... | collective-permute-start | bytes 983048 | tf_op jit(solution)/shard_map/ppermute | solution.py:878
  465.4 42.3 %collective-permute-start.35 = (bf16[768,1024]{1,0:T(8,128)(2,1)S(1)}, bf16[768,1024]{1,0:T(8,128)(2,1)S(1)}, u32[]{:S(2)}, u32[]{:S(2)}) collective-permute-start(bf16[768,1024]{1,0:T(8,128)(2,1)S(1)} %add_convert_fusion.4), channel_id=1, source_target_pairs={{0,2},{1,3},{2,0},{3,1},{4,6},{5,7},{6,4},{7,5},{8,10},{9,11},{10,... | collective-permute-start | bytes 4718600 | tf_op jit(solution)/shard_map/ppermute | solution.py:1030
  499.0 63.2 %collective-permute-start.40 = (bf16[2048,768]{1,0:T(8,128)(2,1)}, bf16[2048,768]{1,0:T(8,128)(2,1)}, u32[]{:S(2)}, u32[]{:S(2)}) collective-permute-start(bf16[2048,768]{1,0:T(8,128)(2,1)} %get-tuple-element.231), channel_id=1, source_target_pairs={{0,1},{1,0},{2,3},{3,2},{4,5},{5,4},{6,7},{7,6},{8,9},{9,8},{10,11... | collective-permute-start | bytes 9437192 | tf_op jit(solution)/shard_map/ppermute | solution.py:1038
  503.2 41.9 %collective-permute-start.36 = (bf16[160,1024]{1,0:T(8,128)(2,1)S(1)}, bf16[160,1024]{1,0:T(8,128)(2,1)S(1)}, u32[]{:S(2)}, u32[]{:S(2)}) collective-permute-start(bf16[160,1024]{1,0:T(8,128)(2,1)S(1)} %add_convert_fusion.8), channel_id=1, source_target_pairs={{0,4},{4,0},{8,12},{12,8},{16,20},{20,16},{24,28},{28,24},{1,5},{5... | collective-permute-start | bytes 983048 | tf_op jit(solution)/shard_map/ppermute | solution.py:878
  503.3 41.8 %collective-permute-start.37 = (bf16[160,1024]{1,0:T(8,128)(2,1)S(1)}, bf16[160,1024]{1,0:T(8,128)(2,1)S(1)}, u32[]{:S(2)}, u32[]{:S(2)}) collective-permute-start(bf16[160,1024]{1,0:T(8,128)(2,1)S(1)} %add_convert_fusion.8), channel_id=1, source_target_pairs={{0,16},{4,20},{8,24},{12,28},{16,0},{20,4},{24,8},{28,12},{1,17},{... | collective-permute-start | bytes 983048 | tf_op jit(solution)/shard_map/ppermute | solution.py:878
  503.4 41.7 %collective-permute-start.38 = (bf16[160,1024]{1,0:T(8,128)(2,1)S(1)}, bf16[160,1024]{1,0:T(8,128)(2,1)S(1)}, u32[]{:S(2)}, u32[]{:S(2)}) collective-permute-start(bf16[160,1024]{1,0:T(8,128)(2,1)S(1)} %add_convert_fusion.8), channel_id=1, source_target_pairs={{0,20},{4,16},{8,28},{12,24},{16,4},{20,0},{24,12},{28,8},{1,21},{... | collective-permute-start | bytes 983048 | tf_op jit(solution)/shard_map/ppermute | solution.py:878
  562.2 39.3 %collective-permute-start.51 = (bf16[640,1024]{1,0:T(8,128)(2,1)}, bf16[640,1024]{1,0:T(8,128)(2,1)S(1)}, u32[]{:S(2)}, u32[]{:S(2)}) collective-permute-start(bf16[640,1024]{1,0:T(8,128)(2,1)} %maximum_select_fusion.4), channel_id=1, source_target_pairs={{0,8},{4,12},{8,0},{12,4},{16,24},{20,28},{24,16},{28,20},{1,9},{5... | collective-permute-start | bytes 3932168 | tf_op jit(solution)/shard_map/ppermute | solution.py:878
  583.8 20.3 %collective-permute-start.44 = (bf16[96,1024]{1,0:T(8,128)(2,1)S(1)}, bf16[96,1024]{1,0:T(8,128)(2,1)S(1)}, u32[]{:S(2)}, u32[]{:S(2)}) collective-permute-start(bf16[96,1024]{1,0:T(8,128)(2,1)S(1)} %get-tuple-element.273), channel_id=1, source_target_pairs={{0,8},{4,12},{8,0},{12,4},{16,24},{20,28},{24,16},{28,20},{1,9},{5... | collective-permute-start | bytes 589832 | tf_op jit(solution)/shard_map/ppermute | solution.py:878
  627.1 27.0 %collective-permute-start.50 = (bf16[384,1024]{1,0:T(8,128)(2,1)S(1)}, bf16[384,1024]{1,0:T(8,128)(2,1)S(1)}, u32[]{:S(2)}, u32[]{:S(2)}) collective-permute-start(bf16[384,1024]{1,0:T(8,128)(2,1)S(1)} %maximum_select_fusion.6), channel_id=1, source_target_pairs={{0,4},{4,0},{8,12},{12,8},{16,20},{20,16},{24,28},{28,24},{1,5},{5... | collective-permute-start | bytes 2359304 | tf_op jit(solution)/shard_map/ppermute | solution.py:878
  (104 other events, 1047.9 us)

commit v3 on v2

--- a/solution.py
+++ b/solution.py
@@ -261,7 +261,7 @@
     (bias_ref, log_ref), refs = refs[:2], refs[2:]
     carried, refs = refs[: pieces * (part > 0)], refs[pieces * (part > 0) :]
     outs, refs = refs[:pieces], refs[pieces:]
-    rows, grads, merged, d_scr, ka_scr, va_scr, sems = refs
+    rows, grads, merged, d_scr, ka_scr, va_scr, sems = refs[:7]
     c = used[0]
     factor = sh.head_size ** (-0.5)
     scale = factor * LOG2E
@@ -281,21 +281,16 @@
             )
             loads.append(copy)
             copy.start()
+    carries = []
     for r in range(pieces if part else 0):
-        copy = pltpu.make_async_copy(
-            carried[r], d_scr.at[place(r)], sems.at[4 * pieces + r]
-        )
-        loads.append(copy)
+        copy = pltpu.make_async_copy(carried[r], refs[7].at[place(r)], sems.at[4 * pieces + r])
+        carries.append(copy)
         copy.start()
-    if not part:
-        d_scr[:, : sh.lanes] = jnp.zeros((sh.span, sh.lanes), d_scr.dtype)
-        ka_scr[...] = jnp.zeros_like(ka_scr)
-        va_scr[...] = jnp.zeros_like(va_scr)
+    d_scr[:, : sh.lanes] = jnp.zeros((sh.span, sh.lanes), d_scr.dtype)
+    ka_scr[...] = jnp.zeros_like(ka_scr)
+    va_scr[...] = jnp.zeros_like(va_scr)
     for copy in loads:
         copy.wait()
-    if part:
-        ka_scr[...] = full(d_scr[:, key : key + sh.lanes]) * (1.0 / factor)
-        va_scr[...] = full(d_scr[:, value : value + sh.lanes])
 
     def equal_rows(products):
         row = lax.broadcasted_iota(jnp.int32, products.shape, 0)
@@ -386,8 +381,16 @@
         total = lax.fori_loop(0, chunks, chunk, jnp.zeros((sh.columns, sh.lanes), jnp.float32))
         d_scr[at, : sh.lanes] = low(pick_heads(total, sh) * factor)
 
-    d_scr[:, key : key + sh.lanes] = low(ka_scr[...] * factor)
-    d_scr[:, value : value + sh.lanes] = low(va_scr[...])
+    for copy in carries:
+        copy.wait()
+
+    def with_carried(first, values):
+        return values + full(refs[7][:, first : first + sh.lanes]) if part else values
+
+    if part:
+        d_scr[:, : sh.lanes] = d_scr[:, : sh.lanes] + refs[7][:, : sh.lanes]
+    d_scr[:, key : key + sh.lanes] = low(with_carried(key, ka_scr[...] * factor))
+    d_scr[:, value : value + sh.lanes] = low(with_carried(value, va_scr[...]))
     stores = [
         pltpu.make_async_copy(d_scr.at[place(r)], outs[r], sems.at[3 * pieces + r])
         for r in range(pieces)
@@ -427,14 +430,14 @@
             pltpu.VMEM((sh.span, sh.columns), jnp.float32),
             pltpu.SemaphoreType.DMA((2 * pieces,)),
         ],
-        compiler_params=pltpu.CompilerParams(vmem_limit_bytes=40 * MEGA),
+        compiler_params=pltpu.CompilerParams(vmem_limit_bytes=34 * MEGA),
         cost_estimate=attend_cost(sh, weight),
         name="attend_forward",
     )(used, member, idx, bidx, *packed, bias)
     return outs[:pieces], outs[pieces]
 
 
-def attend_backward(sh, packed, tops, made, log_rows, lists, part=(0, 1), carried=(), unroll=2):
+def attend_backward(sh, packed, tops, made, log_rows, lists, part=(0, 1), carried=(), weight=32, unroll=2):
     pieces = len(packed)
     used, member, idx, bidx, bias = lists
     rows_each = sh.span // pieces
@@ -454,16 +457,18 @@
             pltpu.VMEM((sh.span, sh.lanes), jnp.float32),
             pltpu.VMEM((sh.span, sh.lanes), jnp.float32),
             pltpu.SemaphoreType.DMA((5 * pieces,)),
-        ],
-        compiler_params=pltpu.CompilerParams(vmem_limit_bytes=36 * MEGA),
-        cost_estimate=attend_cost(sh, 32 // part[1]),
+        ]
+        + [pltpu.VMEM((sh.span, 3 * sh.lanes), jnp.bfloat16)] * (len(carried) > 0),
+        compiler_params=pltpu.CompilerParams(
+            vmem_limit_bytes=(40 if carried else 34) * MEGA
+        ),
+        cost_estimate=attend_cost(sh, weight // part[1]),
         name="attend_backward",
     )(used, member, idx, bidx, *packed, *tops, *made, bias, log_rows, *carried)
 
 
 GELU_A = (2 / 3.141592653589793) ** 0.5
 GELU_B = GELU_A * 0.044715
-ONES = 16
 
 
 def gelu_both(pre):
@@ -526,12 +531,13 @@
     inner_w, refs = take(refs, count)
     outer_w, refs = take(refs, count)
     if head:
-        (second_ref, middle_ref), refs = take(refs, 2)
+        (second_ref, middle_ref, joined_ref), refs = take(refs, 3)
     if tail:
         (outputs_ref, grad_ref, branch_ref, gain_sum, shift_sum, cot_sum), refs = take(refs, 6)
         tops, refs = take(refs, outs_count)
     else:
         (total_ref, back_ref), refs = take(refs, 2)
+    (bias_sum,), refs = take(refs, 1)
     acts, refs = take(refs, count)
     inner_grads, refs = take(refs, count)
     out_scr, inner_scr, outer_scr, total_scr, back_scr, sems = refs
@@ -566,9 +572,8 @@
                 copy.start()
         for copy in [] if head else out_copies:
             copy.start()
-        if tail:
-            for ref in (gain_sum, shift_sum, cot_sum):
-                ref[...] = jnp.zeros_like(ref)
+        for ref in (bias_sum, gain_sum, shift_sum, cot_sum) if tail else (bias_sum,):
+            ref[...] = jnp.zeros_like(ref)
 
     def body(first_step):
         def ready(group):
@@ -580,15 +585,15 @@
         if head:
             ready(out_copies)
             joined = jnp.concatenate([ref[...] for ref in merged], axis=1)
+            joined_ref[...] = joined
             middle = full(resid_ref[...]) + matmul(joined, out_scr[...])
             middle_ref[...] = middle
             unit, _ = unit_of(middle)
             second = low(unit * gain_ref[...] + shift_ref[...])
-            second_ref[:, :model] = second
-            second_ref[:, model:] = jnp.ones((second.shape[0], ONES), jnp.bfloat16)
+            second_ref[...] = second
             total_scr[...] = middle + outer_bias_ref[...]
         else:
-            second = second_in[:, :model]
+            second = second_in[...]
             total_scr[...] = total_in[...]
             back_scr[...] = back_in[...]
         for i in range(count):
@@ -598,7 +603,9 @@
             act, slope = gelu_both(pre)
             act = low(act)
             acts[i][...] = act
-            grad = low(grad * slope)
+            grad = grad * slope
+            bias_sum[:, i * width : (i + 1) * width] += column_sum(grad)
+            grad = low(grad)
             inner_grads[i][...] = grad
             total_scr[...] += matmul(act, outer_scr[i])
             back = contract_cols(grad, inner_scr[i])
@@ -650,7 +657,7 @@
         in_specs += [tiled(tile, model)] + [line(model)] * 3 + [tiled(tile, lanes)] * outs_count
     else:
         args += carried
-        in_specs += [tiled(tile, model + ONES)] + [tiled(tile, model)] * 2
+        in_specs += [tiled(tile, model)] * 3
     if tail is not None:
         args += tail
         in_specs += [tiled(tile, model), line(model)]
@@ -666,8 +673,9 @@
         out_shape.append(rows_out(rows, cols, dtype))
 
     if head is not None:
-        result(model + ONES)
+        result(model)
         result(model, jnp.float32)
+        result(model)
     if tail is not None:
         result(model)
         result(model, jnp.float32)
@@ -680,6 +688,8 @@
     else:
         result(model, jnp.float32)
         result(model, jnp.float32)
+    out_specs.append(line(count * width))
+    out_shape.append(line_out(count * width))
     for _ in range(2 * count):
         result(width)
     outs = pl.pallas_call(
@@ -698,12 +708,12 @@
             pltpu.VMEM((tile, model), jnp.float32),
             pltpu.SemaphoreType.DMA((outs_count + 2 * count,)),
         ],
-        compiler_params=pltpu.CompilerParams(vmem_limit_bytes=58 * MEGA),
+        compiler_params=pltpu.CompilerParams(vmem_limit_bytes=31 * MEGA),
         cost_estimate=cost(rows * model),
         name="middle",
     )(*args)
-    plain = outs[: -2 * count]
-    return plain, outs[-2 * count : -count], outs[-count:]
+    plain, bias_sums = outs[: -2 * count - 1], outs[-2 * count - 1]
+    return plain, bias_sums, outs[-2 * count : -count], outs[-count:]
 
 
 def bundle_kernel(count, *refs):
@@ -740,29 +750,24 @@
     )(*arrays)
 
 
-def add_kernel(count, tall, *refs):
-    firsts, seconds, (out_ref, row_ref) = refs[:count], refs[count : 2 * count], refs[2 * count :]
-
-    def total(arrays, rows):
-        value = full(arrays[0][rows, :])
-        for ref in arrays[1:]:
-            value = value + full(ref[rows, :])
-        return value
-
-    rest = total(firsts, slice(tall, firsts[0].shape[0]))
-    row_ref[...] = rest[:1]
-    out_ref[:tall, :] = low(total(firsts, slice(0, tall)))
-    out_ref[tall:, :] = low(total(seconds, slice(0, seconds[0].shape[0])))
-
-
-def run_add(firsts, seconds, tall):
+def add_kernel(count, *refs):
+    at = 0
+    for group in (refs[:count], refs[count : 2 * count]):
+        total = full(group[0][...])
+        for ref in group[1:]:
+            total = total + full(ref[...])
+        refs[-1][at : at + total.shape[0], :] = low(total)
+        at += total.shape[0]
+
+
+def run_add(firsts, seconds):
     count, cols = len(firsts), firsts[0].shape[1]
     return pl.pallas_call(
-        functools.partial(add_kernel, count, tall),
+        functools.partial(add_kernel, count),
         in_specs=[ON_CHIP] * (2 * count),
-        out_specs=[ON_CHIP] * 2,
-        out_shape=[rows_out(tall + seconds[0].shape[0], cols), line_out(cols)],
-        compiler_params=pltpu.CompilerParams(vmem_limit_bytes=32 * MEGA),
+        out_specs=ON_CHIP,
+        out_shape=rows_out(firsts[0].shape[0] + seconds[0].shape[0], cols),
+        compiler_params=pltpu.CompilerParams(vmem_limit_bytes=14 * MEGA),
         cost_estimate=cost(10**6, 8 * firsts[0].shape[0] * cols),
         name="add",
     )(*firsts, *seconds)
@@ -790,7 +795,7 @@
         ],
         out_specs=[tiled(tile, model), tiled(tile, cols)],
         out_shape=[rows_out(rows, model), rows_out(rows, cols)],
-        compiler_params=pltpu.CompilerParams(vmem_limit_bytes=32 * MEGA),
+        compiler_params=pltpu.CompilerParams(vmem_limit_bytes=14 * MEGA),
         cost_estimate=cost(rows * model),
         name="first",
     )(resid, gain, shift, weight)
@@ -813,7 +818,7 @@
         ],
         out_specs=tiled(tile, cols),
         out_shape=rows_out(rows, cols),
-        compiler_params=pltpu.CompilerParams(vmem_limit_bytes=32 * MEGA),
+        compiler_params=pltpu.CompilerParams(vmem_limit_bytes=12 * MEGA),
         cost_estimate=cost(rows * model),
         name="project",
     )(rows_in, weight)
@@ -867,7 +872,7 @@
             pltpu.SemaphoreType.DMA((parts,)),
         ],
         input_output_aliases={} if made is None else {3 + 2 * parts: 0},
-        compiler_params=pltpu.CompilerParams(vmem_limit_bytes=40 * MEGA),
+        compiler_params=pltpu.CompilerParams(vmem_limit_bytes=20 * MEGA),
         cost_estimate=cost(2 * part_rows * model * parts * depth, part_rows * model * 20),
         name="last",
     )(resid, middle_grad, gain, *packed, *joint_w, *([] if made is None else [made]))
@@ -896,10 +901,13 @@
 
 
 class GroupSum:
-    def __init__(self, values, which=(0, 1)):
+    def __init__(self, values, which=(0, 1), pairs=True):
         bits = [1 << i for i in range(lax.axis_size("dp").bit_length() - 1)]
         orders = []
         for order in (bits, bits[1:2] + bits[:1] + bits[2:]):
+            if not pairs:
+                orders.append([(bit,) for bit in order])
+                continue
             odd = len(order) % 2
             groups = [order[:odd]] + [order[i : i + 2] for i in range(odd, len(order), 2)]
             orders.append([tuple(group) for group in groups if group])
@@ -961,23 +969,43 @@
         self.finish(*earlier)
         return self.start()
 
-    def result(self):
-        while self.steps[0] or self.pending:
+    def result(self, cuts=()):
+        while self.steps[0] or (self.pending and not cuts):
             self.step()
-        return full(jnp.concatenate(self.parts, axis=0))
+        if not cuts:
+            return full(jnp.concatenate(self.parts, axis=0))
+        ((_, uppers, mine, others),) = self.pending
+        if len(uppers) > 1:
+            self.finish()
+            halves = self.parts
+        else:
+            halves = [
+                jnp.where(uppers[0] == 0, mine, others[0]),
+                jnp.where(uppers[0] == 0, others[0], mine),
+            ]
+        edges, outs = [0, *cuts, sum(half.shape[0] for half in halves)], []
+        for low_at, high_at in zip(edges, edges[1:]):
+            pieces, first = [], 0
+            for rows in halves:
+                a, b = max(low_at - first, 0), min(high_at - first, rows.shape[0])
+                if a < b:
+                    pieces.append(rows[a:b])
+                first += rows.shape[0]
+            outs.append(full(jnp.concatenate(pieces, axis=0)))
+        return outs
 
 
 def sum_all(values):
     for axis in ("tensor", "dp"):
-        size, bit = lax.axis_size(axis), 1
-        while bit < size:
-            if 2 * bit < size:
-                others = [swap(values, axis, bit * n) for n in (1, 2, 3)]
-                values = (values + others[0]) + (others[1] + others[2])
-                bit *= 4
-            else:
-                values = values + swap(values, axis, bit)
-                bit *= 2
+        bits = [1 << i for i in range(lax.axis_size(axis).bit_length() - 1)]
+        bits = bits[len(bits) % 2 :] + bits[: len(bits) % 2]
+        for i in range(0, len(bits) - 1, 2):
+            others = [
+                swap(values, axis, bit) for bit in (bits[i], bits[i + 1], bits[i] ^ bits[i + 1])
+            ]
+            values = (values + others[0]) + (others[1] + others[2])
+        if len(bits) % 2:
+            values = values + swap(values, axis, bits[-1])
     return values
 
 
@@ -1063,15 +1091,16 @@
     key_ok = (jnp.arange(span, dtype=jnp.int32) < used * length) & (flags == 1)
     bias = jnp.where(jnp.concatenate([key_ok, jnp.zeros((length,), bool)]), 0.0, MASKED)
     bias = jnp.broadcast_to(full(bias)[:, None], (span + length, 128))
-    def lists_of(s):
-        picks = lax.dynamic_index_in_dim(random_blocks, (item - s) % items, 0, False)
-        if s:
-            picks = from_item(after(picks, joint_halves), s)
-        chosen, usable = jax.vmap(lambda pick: block_lists(used, pick))(picks)
-        marked = jnp.where(usable, chosen, blocks)
-        return (used.reshape(1), member.reshape(1), chosen.reshape(-1), marked.reshape(-1), bias)
-
-    lists = [lists_of(s) for s in range(items)]
+    picks = [
+        from_item(lax.dynamic_index_in_dim(random_blocks, (item - s) % items, 0, False), s)
+        for s in range(items)
+    ]
+    chosen, usable = jax.vmap(lambda pick: block_lists(used, pick))(jnp.concatenate(picks))
+    marked = jnp.where(usable, chosen, blocks)
+    chosen, marked = chosen.reshape(items, -1), marked.reshape(items, -1)
+    lists = [
+        (used.reshape(1), member.reshape(1), chosen[s], marked[s], bias) for s in range(items)
+    ]
 
     packed, made, merged, logs, joint_item = [], [], [], [], [joint]
     rows_in = first_all
@@ -1123,7 +1152,7 @@
     ]
     groups = [group for group in groups if group]
     out_full = [part_weights[part][0] for part in order]
-    acts, inner_grads = {}, {}
+    acts, inner_grads, bias_sums = {}, {}, {}
 
     def outer_product(part):
         return contract_rows(acts[part], cotangent)
@@ -1132,7 +1161,8 @@
         return contract_rows(second_own, inner_grads[part])
 
     def output_product(part):
-        return contract_rows(merged[order.index(part)], branch)
+        at = order.index(part) * lanes
+        return output_grads[at : at + lanes]
 
     def send_members(product, s):
         return [from_member(low(product((s, r))), r) for r in range(members - 1, 0, -1)]
@@ -1156,7 +1186,7 @@
         if n == 1 and width == model:
             late = after([item_sent[s][1] for s in range(items)], acts[0, 0])
             inner_parts = [(from_member(late[s], -r), 0) for s, r in group]
-        plain, group_acts, group_grads = run_middle(
+        plain, group_bias, group_acts, group_grads = run_middle(
             cotangent,
             jnp.concatenate([part_bias(part) for part in group], axis=1),
             inner_parts,
@@ -1166,11 +1196,12 @@
             after(carried, waits) if carried else None,
             tail,
         )
-        for part, act, grad in zip(group, group_acts, group_grads):
-            acts[part], inner_grads[part] = act, grad
+        for i, part in enumerate(group):
+            acts[part], inner_grads[part] = group_acts[i], group_grads[i]
+            bias_sums[part] = group_bias[:, i * width : (i + 1) * width]
         if n == 0:
-            second_own, middle = plain[:2]
-            plain = plain[2:]
+            second_own, middle, joined = plain[:3]
+            plain = plain[3:]
         if n < len(groups) - 1:
             carried = [second_own, *plain]
         waits = []
@@ -1180,6 +1211,7 @@
                 waits.append(totals[name, s])
     outputs, middle_grad, branch, second_gain_sum, second_shift_sum, cot_sum = plain[:6]
     tops = plain[6:]
+    output_grads = contract_rows(joined, branch)
 
     top_rows = [[None] * members for _ in range(items)]
     for i, (s, r) in enumerate(order):
@@ -1203,7 +1235,7 @@
 
     packed_grad, joint_totals = [None] * items, [None] * items
     outer_sum = GroupSum(
-        add_items(totals["outer", 0], after(item_sent["outer"], branch)), (0,)
+        add_items(totals["outer", 0], after(item_sent["outer"], branch)), (0,), False
     )
     waits = (outer_sum.start(), member_sent, totals["output", 0])
     inner_sum = None
@@ -1219,11 +1251,9 @@
                     inner_terms = [totals["inner", 0], *others["inner"]]
                     output_terms = [totals["output", 0], *others["output"]]
                     if width == model:
-                        inner_total, bias_total = run_add(inner_terms, output_terms, model)
+                        inner_total = run_add(inner_terms, output_terms)
                     else:
                         inner_total = add_items(inner_terms[0], inner_terms[1:])
-                        bias_total = full(inner_total[model : model + 1])
-                        inner_total = inner_total[:model]
                         output_sum = GroupSum(add_items(output_terms[0], output_terms[1:]), (0,))
                     inner_sum = GroupSum(inner_total, (1,))
                     waits = (waits, inner_sum.start(), outer_sum.step(inner_total))
@@ -1238,19 +1268,23 @@
                 lists[s],
                 (part, BACK_PARTS),
                 grads,
+                0 if s == items - 1 and part == 0 else 32,
             )
         packed_grad[s] = grads
-        waits = inner_sum.step(grads[0])
-        rows = after(grads, waits, outer_sum.step(grads[0]) if s else ())
+        if s:
+            rows = after(grads, outer_sum.step(grads[0]))
+        else:
+            rows = after(grads, inner_sum.step(grads[0]), outer_sum.step(grads[0]))
         total = contract_rows(rows[0], first_all[0])
         for r in range(1, members):
             total = total + contract_rows(rows[r], first_all[r])
         joint_totals[s] = low(total) if s else total
-        grads = after(grads, waits)
         waits = joint_totals[s]
         if s:
-            grads = after(grads, waits)
+            waits = (waits, outer_sum.step(total), inner_sum.step(total))
+            rows = after(grads, waits)
             joint_sent.append(from_item(joint_totals[s], -s))
+        grads = rows
         for r in range(members):
             back[s, r] = from_member(grads[r], -r)
 
@@ -1281,13 +1315,17 @@
         second_gain_sum,
         second_shift_sum,
         cot_sum,
-        lax.dynamic_update_slice(jnp.zeros((tensor, width), jnp.float32), bias_total, (place, 0)),
     ]
+    bias_rows = jnp.zeros((tensor, width), jnp.float32)
+    for s, r in order:
+        spot = (item + s) % items * members + (member - r) % members
+        bias_rows = lax.dynamic_update_slice(bias_rows, bias_sums[s, r], (spot, 0))
+    vectors.append(bias_rows)
     vectors = after(vectors, end_sum.step(), inner_sum.step(pieces[-1][1]))
     small = sum_all(jnp.concatenate([vector.reshape(-1) for vector in vectors]))
     bias_grad = lax.dynamic_slice_in_dim(small, 5 * model + place * width, width, 0)
     small = small[: 5 * model].reshape(5, model)
-    end_grad = end_sum.result()
+    end_grad = end_sum.result((lanes, 2 * lanes))
     outer_grad, inner_grad = outer_sum.result(), inner_sum.result()
     if width == model:
         inner_grad, output_grad = inner_grad[:model], inner_grad[model:]
@@ -1296,9 +1334,7 @@
     return (
         outputs,
         input_grad,
-        end_grad[:lanes],
-        end_grad[lanes : 2 * lanes],
-        end_grad[2 * lanes :],
+        *end_grad,
         output_grad,
         inner_grad,
         bias_grad,

time: 669 us -> 620 us (0.927)
  Pallas kernels: 383 us -> 308 us
  starting transfers between devices: 42 us -> 88.9 us
  waiting for transfers between devices: 69.4 us -> 53.2 us
  local copies, waits for them, and re-layouts: 39.8 us -> 51.4 us
  matrix products: 88.5 us -> 78.3 us
    ppermute x32 -> x30, starting transfers between devices: 30.1 us -> 79.7 us  [swap(): return lax.ppermute(values, axis, [(i, i ^ bit) for i in range(size)])]
    pallas_call x4, Pallas kernels: 139 us -> 89.7 us  [attend_backward(): pl.pallas_call(functools.partial(backward_kernel, sh, pieces, unroll, par...]
    pallas_call x2, Pallas kernels: 67.5 us -> 44.7 us  [attend_forward(): pl.pallas_call(functools.partial(forward_kernel, sh, pieces, unroll), in_...]
    ppermute x8, waiting for transfers between devices: 26.9 us -> 11.3 us  [from_item(): return lax.ppermute(values, 'tensor', pairs)]
    unnamed x159 -> x171, local copies, waits for them, and re-layouts: 24.6 us -> 35.4 us
    dot_general x16 -> x13, matrix products: 88.5 us -> 78.3 us  [contract_rows(): lax.dot_general(left, right, (((0,), (0,)), ((), ())), preferred_element_...]
    ppermute x32 -> x30, waiting for transfers between devices: 39.2 us -> 36.1 us  [swap(): return lax.ppermute(values, axis, [(i, i ^ bit) for i in range(size)])]
  transfers between devices with their start and end apart: 59 -> 57, of which waited for: 12 -> 15; matrix products, arithmetic and copies ran while one was open for 18% -> 19% of each run, Pallas kernels for 51% -> 50%
where the time goes in v3:
time: 620 us; the launch traced here: 612 us
  Pallas kernels  308 us (50%)
  starting transfers between devices  88.9 us (14%)
  matrix products  78.3 us (13%)
  waiting for transfers between devices  53.2 us (9%)
  local copies, waits for them, and re-layouts  51.4 us (8%)
  other arithmetic  26.8 us (4%)
    pallas_call x3, Pallas kernels, run_middle(): pl.pallas_call(functools.partial(middle_kernel, count, outs_count, head i...  115 us
    pallas_call x4, Pallas kernels, attend_backward(): pl.pallas_call(functools.partial(backward_kernel, sh, pieces, unroll, par...  89.7 us
    ppermute x30, starting transfers between devices, swap(): return lax.ppermute(values, axis, [(i, i ^ bit) for i in range(size)])  79.7 us
    dot_general x13, matrix products, contract_rows(): lax.dot_general(left, right, (((0,), (0,)), ((), ())), preferred_element_...  78.3 us
    pallas_call x2, Pallas kernels, attend_forward(): pl.pallas_call(functools.partial(forward_kernel, sh, pieces, unroll), in_...  44.7 us
    ppermute x30, waiting for transfers between devices, swap(): return lax.ppermute(values, axis, [(i, i ^ bit) for i in range(size)])  36.1 us
    unnamed x171, local copies, waits for them, and re-layouts  35.4 us
    pallas_call x2, Pallas kernels, run_last(): pl.pallas_call(functools.partial(last_kernel, parts), grid=(part_rows //...  26.7 us
  transfers between devices with their start and end apart: 57, of which 15 were waited for; matrix products, arithmetic and copies ran while one was open for 19% of the time, Pallas kernels for 50%

profile of v3, /device:TPU:18, one launch (start us, length us, event | category | flops | bytes accessed | tf_op | source)
XLA Modules:
  0.0 611.6 jit_solution(6674830828212204327)
XLA Ops:
  15.5 7.1 %first.3 = (bf16[2048,1024]{1,0:T(8,128)(2,1)S(1)}, bf16[2048,768]{1,0:T(8,128)(2,1)S(1)}) custom-call(bf16[2048,1024]{1,0:T(8,128)(2,1)S(1)} %copy-done, f32[1,1024]{1,0:T(1,128)S(1)} %bitcast.47, f32[1,1024]{1,0:T(1,128)S(1)} %bitcast.51, bf16[768,1024]{1,0:T(8,128)(2,1)S(1)} %copy-done.2), custom_call_target="tpu_custom_call" | custom-call | flops 2097152 | bytes 1000000 | tf_op jit(solution)/shard_map/first/pallas_call | solution.py:787
  30.1 8.7 %first.2 = (bf16[2048,1024]{1,0:T(8,128)(2,1)S(1)}, bf16[2048,768]{1,0:T(8,128)(2,1)S(1)}) custom-call(bf16[2048,1024]{1,0:T(8,128)(2,1)} %collective-permute-done.1.resid_ref, f32[1,1024]{1,0:T(1,128)S(1)} %bitcast.48, f32[1,1024]{1,0:T(1,128)S(1)} %bitcast.52, bf16[768,1024]{1,0:T(8,128)(2,1)S(1)} %copy-done.2), custom_call_target="tpu_custom_call" | custom-call | flops 2097152 | bytes 1000000 | tf_op jit(solution)/shard_map/first/pallas_call | solution.py:787
  39.5 22.7 %attend_forward.2 = (bf16[2048,256]{1,0:T(8,128)(2,1)S(1)}, bf16[2048,256]{1,0:T(8,128)(2,1)}, f32[64,256]{1,0:T(8,128)S(1)}) custom-call(s32[1]{0:T(128)} %bitcast.7.used, s32[1]{0:T(128)} %bitcast.8.member, s32[2048]{0:T(1024)S(1)} %squeeze.42.idx, s32[2048]{0:T(1024)S(1)} %squeeze.43.bidx, bf16[2048,768]{1,0:T(8,128)(2,1)S(1)} %copy-done.54, ...), custom_call_target="tpu_custom_call" | custom-call | flops 137438953472 | bytes 1000000 | tf_op jit(solution)/shard_map/attend_forward/pallas_call | solution.py:421
  76.4 11.3 %collective-permute-done.7.refs_12_.refs_7_.refs_9_ = bf16[1296,1024]{1,0:T(8,128)(2,1)} collective-permute-done((bf16[1296,1024]{1,0:T(8,128)(2,1)}, bf16[1296,1024]{1,0:T(8,128)(2,1)}, u32[]{:S(2)}, u32[]{:S(2)}) %collective-permute-start.7) | collective-permute-done | bytes 2654240 | tf_op jit(solution)/shard_map/ppermute | solution.py:1058
  94.4 22.0 %attend_forward.3 = (bf16[2048,256]{1,0:T(8,128)(2,1)S(1)}, bf16[2048,256]{1,0:T(8,128)(2,1)S(1)}, f32[64,256]{1,0:T(8,128)S(1)}) custom-call(s32[1]{0:T(128)} %bitcast.7.used, s32[1]{0:T(128)} %bitcast.8.member, s32[2048]{0:T(1024)S(1)} %squeeze.44.idx, s32[2048]{0:T(1024)S(1)} %squeeze.45.bidx, bf16[2048,768]{1,0:T(8,128)(2,1)S(1)} %copy-done.10, ...), custom_call_target="tpu_custom_call" | custom-call | bytes 1000000 | tf_op jit(solution)/shard_map/attend_forward/pallas_call | solution.py:421
  119.2 33.5 %middle.3 = (bf16[2048,1024]{1,0:T(8,128)(2,1)S(1)}, f32[2048,1024]{1,0:T(8,128)}, bf16[2048,1024]{1,0:T(8,128)(2,1)}, f32[2048,1024]{1,0:T(8,128)}, f32[2048,10...) custom-call(bf16[2048,1024]{1,0:T(8,128)(2,1)} %refs_0_.11, ...), custom_call_target="tpu_custom_call" | custom-call | flops 2097152 | bytes 1000000 | tf_op jit(solution)/shard_map/middle/pallas_call | solution.py:695
  160.0 46.5 %middle.4 = (f32[2048,1024]{1,0:T(8,128)}, f32[2048,1024]{1,0:T(8,128)}, f32[1,2048]{1,0:T(1,128)S(1)}, bf16[2048,1024]{1,0:T(8,128)(2,1)S(1)}, bf16[2048,1024]{...) custom-call(bf16[2048,1024]{1,0:T(8,128)(2,1)} %refs_0_.11, ...), custom_call_target="tpu_custom_call" | custom-call | flops 2097152 | bytes 1000000 | tf_op jit(solution)/shard_map/middle/pallas_call | solution.py:695
  206.5 8.1 %convolution_convert_fusion.3 = bf16[1024,1024]{1,0:T(8,128)(2,1)} fusion(bf16[2048,1024]{1,0:T(8,128)(2,1)S(1)} %get-tuple-element.165, bf16[2048,1024]{1,0:T(8,128)(2,1)} %refs_0_.11), kind=kOutput, calls=%fused_computation.13 | convolution fusion | flops 4296015872 | bytes 10485760 | tf_op jit(solution)/shard_map/dot_general | solution.py:22
  215.0 5.2 convolution_convert_fusion.2
  220.4 6.1 %fusion.12 = f32[1024,1024]{1,0:T(8,128)} fusion(bf16[2048,1024]{1,0:T(8,128)(2,1)S(1)} %copy-done.80, bf16[2048,1024]{1,0:T(8,128)(2,1)S(1)} %copy-done.65), kind=kOutput, calls=%fused_computation.97 | convolution fusion | flops 4294967296 | bytes 12582912 | tf_op jit(solution)/shard_map/dot_general | solution.py:22
  226.5 7.1 %add_convert_fusion.4 = bf16[1024,1024]{1,0:T(8,128)(2,1)} fusion(bf16[1024,1024]{1,0:T(8,128)(2,1)} %collective-permute-done.11, bf16[2048,1024]{1,0:T(8,128)(2,1)S(1)} %get-tuple-element.164, bf16[2048,1024]{1,0:T(8,128)(2,1)S(1)} %copy-done.65), kind=kOutput, calls=%fused_computation.4 | convolution fusion | flops 4298113024 | bytes 12582912 | tf_op jit(solution)/shard_map/dot_general | solution.py:22
  233.6 5.8 add_convert_fusion.3
  241.4 34.7 %middle.5 = (bf16[2048,1024]{1,0:T(8,128)(2,1)}, f32[2048,1024]{1,0:T(8,128)}, bf16[2048,1024]{1,0:T(8,128)(2,1)S(1)}, f32[1,1024]{1,0:T(1,128)S(1)}, f32[1,1024...) custom-call(bf16[2048,1024]{1,0:T(8,128)(2,1)} %refs_0_.11, ...), custom_call_target="tpu_custom_call" | custom-call | flops 2097152 | bytes 1000000 | tf_op jit(solution)/shard_map/middle/pallas_call | solution.py:695
  276.2 4.8 convolution_convert_fusion.1
  281.2 8.3 %convolution_convert_fusion = bf16[1024,1024]{1,0:T(8,128)(2,1)} fusion(bf16[2048,1024]{1,0:T(8,128)(2,1)S(1)} %copy-done.20, bf16[2048,1024]{1,0:T(8,128)(2,1)} %get-tuple-element.181), kind=kOutput, calls=%fused_computation.10 | convolution fusion | flops 4296015872 | bytes 10485760 | tf_op jit(solution)/shard_map/dot_general | solution.py:22
  290.0 4.6 fusion.11
  308.7 19.5 %attend_backward.4 = (bf16[2048,768]{1,0:T(8,128)(2,1)S(1)}, bf16[2048,768]{1,0:T(8,128)(2,1)S(1)}) custom-call(s32[1]{0:T(128)} %bitcast.7.used, s32[1]{0:T(128)} %bitcast.8.member, s32[2048]{0:T(1024)S(1)} %squeeze.44.idx, s32[2048]{0:T(1024)S(1)} %squeeze.45.bidx, bf16[2048,768]{1,0:T(8,128)(2,1)S(1)} %copy-done.11, bf16[2048,768]{1,0:T(8,128)(2,1)S(1)} %copy-done.8, ...), custom_call_target="tpu_custom_call" | custom-call | bytes 1000000 | tf_op jit(solution)/shard_map/attend_backward/pallas_call | solution.py:444
  331.0 27.0 %collective-permute-start.21 = (bf16[256,1024]{1,0:T(8,128)(2,1)S(1)}, bf16[256,1024]{1,0:T(8,128)(2,1)S(1)}, u32[]{:S(2)}, u32[]{:S(2)}) collective-permute-start(bf16[256,1024]{1,0:T(8,128)(2,1)S(1)} %constant_dynamic-slice_fusion.9), channel_id=1, source_target_pairs={{0,8},{4,12},{8,0},{12,4},{16,24},{20,28},{24,16},{28,20},{1,9},{5... | collective-permute-start | bytes 1572872 | tf_op jit(solution)/shard_map/ppermute | solution.py:883
  358.0 7.3 %add_convert_fusion.refs_0_ = bf16[1024,1024]{1,0:T(8,128)(2,1)S(1)} fusion(bf16[1024,1024]{1,0:T(8,128)(2,1)} %collective-permute-done.19, bf16[2048,1024]{1,0:T(8,128)(2,1)S(1)} %copy-done.21, bf16[2048,1024]{1,0:T(8,128)(2,1)} %get-tuple-element.189), kind=kOutput, calls=%fused_computation | convolution fusion | flops 4298113024 | bytes 12582912 | tf_op jit(solution)/shard_map/dot_general | solution.py:22
  371.1 25.4 %attend_backward.5 = (bf16[2048,768]{1,0:T(8,128)(2,1)S(1)}, bf16[2048,768]{1,0:T(8,128)(2,1)}) custom-call(s32[1]{0:T(128)} %bitcast.7.used, s32[1]{0:T(128)} %bitcast.8.member, s32[2048]{0:T(1024)S(1)} %squeeze.44.idx, s32[2048]{0:T(1024)S(1)} %squeeze.45.bidx, bf16[2048,768]{1,0:T(8,128)(2,1)} %copy-done.9, bf16[2048,768]{1,0:T(8,128)(2,1)} %copy-done.6, ...), custom_call_target="tpu_custom_call" | custom-call | flops 34359738368 | bytes 1000000 | tf_op jit(solution)/shard_map/attend_backward/pallas_call | solution.py:444
  400.3 5.5 convolution_add_fusion
  408.6 10.6 %collective-permute-start.27 = (bf16[256,1024]{1,0:T(8,128)(2,1)S(1)}, bf16[256,1024]{1,0:T(8,128)(2,1)S(1)}, u32[]{:S(2)}, u32[]{:S(2)}) collective-permute-start(bf16[256,1024]{1,0:T(8,128)(2,1)S(1)} %maximum_select_fusion.8), channel_id=1, source_target_pairs={{0,8},{4,12},{8,0},{12,4},{16,24},{20,28},{24,16},{28,20},{1,9},{5... | collective-permute-start | bytes 1572872 | tf_op jit(solution)/shard_map/ppermute | solution.py:883
  425.8 19.7 %attend_backward.6 = (bf16[2048,768]{1,0:T(8,128)(2,1)S(1)}, bf16[2048,768]{1,0:T(8,128)(2,1)S(1)}) custom-call(s32[1]{0:T(128)} %bitcast.7.used, s32[1]{0:T(128)} %bitcast.8.member, s32[2048]{0:T(1024)S(1)} %copy-done.48, s32[2048]{0:T(1024)S(1)} %copy-done.50, bf16[2048,768]{1,0:T(8,128)(2,1)S(1)} %copy-done.55, bf16[2048,768]{1,0:T(8,128)(2,1)S(1)} %copy-done.57, ...), custom_call_target="tpu_custom_call" | custom-call | flops 34359738368 | bytes 1000000 | tf_op jit(solution)/shard_map/attend_backward/pallas_call | solution.py:444
  458.0 25.1 %attend_backward.7 = (bf16[2048,768]{1,0:T(8,128)(2,1)S(1)}, bf16[2048,768]{1,0:T(8,128)(2,1)}) custom-call(s32[1]{0:T(128)} %bitcast.7.used, s32[1]{0:T(128)} %bitcast.8.member, s32[2048]{0:T(1024)S(1)} %copy-done.48, s32[2048]{0:T(1024)S(1)} %copy-done.50, bf16[2048,768]{1,0:T(8,128)(2,1)} %copy-done.53, bf16[2048,768]{1,0:T(8,128)(2,1)} %copy-done.56, ...), custom_call_target="tpu_custom_call" | custom-call | flops 34359738368 | bytes 1000000 | tf_op jit(solution)/shard_map/attend_backward/pallas_call | solution.py:444
  493.0 6.6 %fusion.14 = f32[768,1024]{1,0:T(8,128)S(1)} fusion(bf16[2048,768]{1,0:T(8,128)(2,1)} %copy-done.27, bf16[2048,1024]{1,0:T(8,128)(2,1)} %copy-done.31), kind=kOutput, calls=%fused_computation.99 | convolution fusion | flops 3221225472 | bytes 10485760 | tf_op jit(solution)/shard_map/dot_general | solution.py:22
  499.6 5.4 add_convert_fusion.5
  506.7 14.8 %collective-permute-start.49 = (bf16[640,1024]{1,0:T(8,128)(2,1)}, bf16[640,1024]{1,0:T(8,128)(2,1)S(1)}, u32[]{:S(2)}, u32[]{:S(2)}) collective-permute-start(bf16[640,1024]{1,0:T(8,128)(2,1)} %maximum_select_fusion.3), channel_id=1, source_target_pairs={{0,8},{4,12},{8,0},{12,4},{16,24},{20,28},{24,16},{28,20},{1,9},{5... | collective-permute-start | bytes 3932168 | tf_op jit(solution)/shard_map/ppermute | solution.py:883
  530.9 13.3 %last.2 = (f32[2048,1024]{1,0:T(8,128)}, f32[1,1024]{1,0:T(1,128)S(1)}, f32[1,1024]{1,0:T(1,128)S(1)}) custom-call(bf16[2048,1024]{1,0:T(8,128)(2,1)S(1)} %copy-done.1, f32[2048,1024]{1,0:T(8,128)S(1)} %copy-done.5, f32[1,1024]{1,0:T(1,128)S(1)} %bitcast.49, bf16[2048,768]{1,0:T(8,128)(2,1)S(1)} %copy-done.28, ...), custom_call_target="tpu_custom_call" | custom-call | flops 6442450944 | bytes 20971520 | tf_op jit(solution)/shard_map/last/pallas_call | solution.py:860
  549.4 13.3 %last.3 = (f32[2048,1024]{1,0:T(8,128)}, f32[1,1024]{1,0:T(1,128)S(1)}, f32[1,1024]{1,0:T(1,128)S(1)}) custom-call(bf16[2048,1024]{1,0:T(8,128)(2,1)S(1)} %copy-done.1, f32[2048,1024]{1,0:T(8,128)S(1)} %copy-done.5, f32[1,1024]{1,0:T(1,128)S(1)} %bitcast.50, bf16[2048,768]{1,0:T(8,128)(2,1)S(1)} %copy-done.28, ...), custom_call_target="tpu_custom_call", output_to_operand_aliasing={{0}: (11, {})} | custom-call | flops 6442450944 | bytes 20971520 | tf_op jit(solution)/shard_map/last/pallas_call | solution.py:860
  574.7 6.8 %collective-permute-done.46 = bf16[96,1024]{1,0:T(8,128)(2,1)S(1)} collective-permute-done((bf16[96,1024]{1,0:T(8,128)(2,1)S(1)}, bf16[96,1024]{1,0:T(8,128)(2,1)S(1)}, u32[]{:S(2)}, u32[]{:S(2)}) %collective-permute-start.46) | collective-permute-done | bytes 196640 | tf_op jit(solution)/shard_map/ppermute | solution.py:883
  581.4 6.1 collective-permute-done.47
  602.2 5.0 collective-permute-done.56
  (379 shorter events, 158.4 us)
Async XLA Ops:
  0.7 29.4 %collective-permute-start.1 = (bf16[2048,1024]{1,0:T(8,128)(2,1)}, bf16[2048,1024]{1,0:T(8,128)(2,1)}, u32[]{:S(2)}, u32[]{:S(2)}) collective-permute-start(bf16[2048,1024]{1,0:T(8,128)(2,1)} %refs_0_.13), channel_id=1, source_target_pairs={{0,1},{1,0},{2,3},{3,2},{4,5},{5,4},{6,7},{7,6},{8,9},{9,8},{10,11... | collective-permute-start | bytes 12582920 | tf_op jit(solution)/shard_map/ppermute | solution.py:1066
  5.2 22.7 %collective-permute-start = (bf16[384,1024]{1,0:T(8,128)(2,1)}, bf16[384,1024]{1,0:T(8,128)(2,1)}, u32[]{:S(2)}, u32[]{:S(2)}) collective-permute-start(bf16[384,1024]{1,0:T(8,128)(2,1)} %constant_dynamic-slice_fusion.11), channel_id=1, source_target_pairs={{0,2},{1,3},{2,0},{3,1},{4,6},{5,7},{6,4},{7,5},{8,10},{9,11},{10,... | collective-permute-start | bytes 2359304 | tf_op jit(solution)/shard_map/ppermute | solution.py:1058
  28.0 59.8 %collective-permute-start.7 = (bf16[1296,1024]{1,0:T(8,128)(2,1)}, bf16[1296,1024]{1,0:T(8,128)(2,1)}, u32[]{:S(2)}, u32[]{:S(2)}) collective-permute-start(bf16[1296,1024]{1,0:T(8,128)(2,1)} %bundle.2), channel_id=1, source_target_pairs={{0,2},{1,3},{2,0},{3,1},{4,6},{5,7},{6,4},{7,5},{8,10},{9,11},{10,... | collective-permute-start | bytes 7962632 | tf_op jit(solution)/shard_map/ppermute | solution.py:1058
  28.6 33.8 %collective-permute-start.5 = (bf16[384,1024]{1,0:T(8,128)(2,1)}, bf16[384,1024]{1,0:T(8,128)(2,1)S(1)}, u32[]{:S(2)}, u32[]{:S(2)}) collective-permute-start(bf16[384,1024]{1,0:T(8,128)(2,1)} %collective-permute-done), channel_id=1, source_target_pairs={{0,4},{4,0},{8,12},{12,8},{16,20},{20,16},{24,28},{28,24},{1,5},{5... | collective-permute-start | bytes 2359304 | tf_op jit(solution)/shard_map/ppermute | solution.py:883
  38.8 25.9 %collective-permute-start.2 = (bf16[1296,1024]{1,0:T(8,128)(2,1)}, bf16[1296,1024]{1,0:T(8,128)(2,1)S(1)}, u32[]{:S(2)}, u32[]{:S(2)}) collective-permute-start(bf16[1296,1024]{1,0:T(8,128)(2,1)} %bundle.2), channel_id=1, source_target_pairs={{0,1},{1,0},{2,3},{3,2},{4,5},{5,4},{6,7},{7,6},{8,9},{9,8},{10,11... | collective-permute-start | bytes 7962632 | tf_op jit(solution)/shard_map/ppermute | solution.py:1066
  87.7 31.4 %collective-permute-start.8 = (bf16[1296,1024]{1,0:T(8,128)(2,1)}, bf16[1296,1024]{1,0:T(8,128)(2,1)}, u32[]{:S(2)}, u32[]{:S(2)}) collective-permute-start(bf16[1296,1024]{1,0:T(8,128)(2,1)} %collective-permute-done.7.refs_12_.refs_7_.refs_9_), channel_id=1, source_target_pairs={{0,1},{1,0},{2,3},{3,2},{4,5},{5,4},{6,7},{7,6},{8,9},{9,8},{10,11... | collective-permute-start | bytes 7962632 | tf_op jit(solution)/shard_map/ppermute | solution.py:1066
  87.7 67.0 %collective-permute-start.9 = (bf16[1024,1024]{1,0:T(8,128)(2,1)}, bf16[1024,1024]{1,0:T(8,128)(2,1)}, u32[]{:S(2)}, u32[]{:S(2)}) collective-permute-start(bf16[1024,1024]{1,0:T(8,128)(2,1)} %refs_14_.1), channel_id=1, source_target_pairs={{0,2},{1,3},{2,0},{3,1},{4,6},{5,7},{6,4},{7,5},{8,10},{9,11},{10,... | collective-permute-start | bytes 6291464 | tf_op jit(solution)/shard_map/ppermute | solution.py:1058
  88.7 29.1 %collective-permute-start.4 = (bf16[2048,256]{1,0:T(8,128)(2,1)}, bf16[2048,256]{1,0:T(8,128)(2,1)S(1)}, u32[]{:S(2)}, u32[]{:S(2)}) collective-permute-start(bf16[2048,256]{1,0:T(8,128)(2,1)} %get-tuple-element.141.refs_5_), channel_id=1, source_target_pairs={{0,1},{1,0},{2,3},{3,2},{4,5},{5,4},{6,7},{7,6},{8,9},{9,8},{10,11... | collective-permute-start | bytes 3145736 | tf_op jit(solution)/shard_map/ppermute | solution.py:1066
  155.1 86.4 %collective-permute-start.13 = (bf16[1024,1024]{1,0:T(8,128)(2,1)}, bf16[1024,1024]{1,0:T(8,128)(2,1)S(1)}, u32[]{:S(2)}, u32[]{:S(2)}) collective-permute-start(bf16[1024,1024]{1,0:T(8,128)(2,1)} %refs_14_.1), channel_id=1, source_target_pairs={{0,1},{1,0},{2,3},{3,2},{4,5},{5,4},{6,7},{7,6},{8,9},{9,8},{10,11... | collective-permute-start | bytes 6291464 | tf_op jit(solution)/shard_map/ppermute | solution.py:1066
  233.6 61.2 %collective-permute-start.16 = (bf16[1024,1024]{1,0:T(8,128)(2,1)}, bf16[1024,1024]{1,0:T(8,128)(2,1)S(1)}, u32[]{:S(2)}, u32[]{:S(2)}) collective-permute-start(bf16[1024,1024]{1,0:T(8,128)(2,1)} %add_convert_fusion.4), channel_id=1, source_target_pairs={{0,2},{1,3},{2,0},{3,1},{4,6},{5,7},{6,4},{7,5},{8,10},{9,11},{10,... | collective-permute-start | bytes 6291464 | tf_op jit(solution)/shard_map/ppermute | solution.py:1058
  239.4 118.6 %collective-permute-start.22 = (bf16[1024,1024]{1,0:T(8,128)(2,1)}, bf16[1024,1024]{1,0:T(8,128)(2,1)}, u32[]{:S(2)}, u32[]{:S(2)}) collective-permute-start(bf16[1024,1024]{1,0:T(8,128)(2,1)} %add_convert_fusion.3), channel_id=1, source_target_pairs={{0,2},{1,3},{2,0},{3,1},{4,6},{5,7},{6,4},{7,5},{8,10},{9,11},{10,... | collective-permute-start | bytes 6291464 | tf_op jit(solution)/shard_map/ppermute | solution.py:1058
  297.5 30.7 %collective-permute-start.17 = (bf16[512,1024]{1,0:T(8,128)(2,1)}, bf16[512,1024]{1,0:T(8,128)(2,1)}, u32[]{:S(2)}, u32[]{:S(2)}) collective-permute-start(bf16[512,1024]{1,0:T(8,128)(2,1)} %constant_dynamic-slice_fusion.10), channel_id=1, source_target_pairs={{0,4},{4,0},{8,12},{12,8},{16,20},{20,16},{24,28},{28,24},{1,5},{5... | collective-permute-start | bytes 3145736 | tf_op jit(solution)/shard_map/ppermute | solution.py:883
  300.7 57.3 %collective-permute-start.24 = (bf16[256,1024]{1,0:T(8,128)(2,1)}, bf16[256,1024]{1,0:T(8,128)(2,1)}, u32[]{:S(2)}, u32[]{:S(2)}) collective-permute-start(bf16[256,1024]{1,0:T(8,128)(2,1)} %get-tuple-element.254), channel_id=1, source_target_pairs={{0,2},{1,3},{2,0},{3,1},{4,6},{5,7},{6,4},{7,5},{8,10},{9,11},{10,... | collective-permute-start | bytes 1572872 | tf_op jit(solution)/shard_map/ppermute | solution.py:1058
  300.7 123.7 %collective-permute-start.14 = (bf16[2048,256]{1,0:T(8,128)(2,1)}, bf16[2048,256]{1,0:T(8,128)(2,1)}, u32[]{:S(2)}, u32[]{:S(2)}) collective-permute-start(bf16[2048,256]{1,0:T(8,128)(2,1)} %copy-done.62), channel_id=1, source_target_pairs={{0,1},{1,0},{2,3},{3,2},{4,5},{5,4},{6,7},{7,6},{8,9},{9,8},{10,11... | collective-permute-start | bytes 3145736 | tf_op jit(solution)/shard_map/ppermute | solution.py:1066
  331.0 39.8 %collective-permute-start.21 = (bf16[256,1024]{1,0:T(8,128)(2,1)S(1)}, bf16[256,1024]{1,0:T(8,128)(2,1)S(1)}, u32[]{:S(2)}, u32[]{:S(2)}) collective-permute-start(bf16[256,1024]{1,0:T(8,128)(2,1)S(1)} %constant_dynamic-slice_fusion.9), channel_id=1, source_target_pairs={{0,8},{4,12},{8,0},{12,4},{16,24},{20,28},{24,16},{28,20},{1,9},{5... | collective-permute-start | bytes 1572872 | tf_op jit(solution)/shard_map/ppermute | solution.py:883
  368.8 50.4 %collective-permute-start.28 = (bf16[640,1024]{1,0:T(8,128)(2,1)}, bf16[640,1024]{1,0:T(8,128)(2,1)}, u32[]{:S(2)}, u32[]{:S(2)}) collective-permute-start(bf16[640,1024]{1,0:T(8,128)(2,1)} %constant_dynamic-slice_fusion.7), channel_id=1, source_target_pairs={{0,8},{4,12},{8,0},{12,4},{16,24},{20,28},{24,16},{28,20},{1,9},{5... | collective-permute-start | bytes 3932168 | tf_op jit(solution)/shard_map/ppermute | solution.py:883
  371.0 25.6 %collective-permute-start.25 = (bf16[128,1024]{1,0:T(8,128)(2,1)S(1)}, bf16[128,1024]{1,0:T(8,128)(2,1)S(1)}, u32[]{:S(2)}, u32[]{:S(2)}) collective-permute-start(bf16[128,1024]{1,0:T(8,128)(2,1)S(1)} %constant_dynamic-slice_fusion.8), channel_id=1, source_target_pairs={{0,16},{4,20},{8,24},{12,28},{16,0},{20,4},{24,8},{28,12},{1,17},{... | collective-permute-start | bytes 786440 | tf_op jit(solution)/shard_map/ppermute | solution.py:883
  405.8 51.0 %collective-permute-start.32 = (bf16[768,1024]{1,0:T(8,128)(2,1)S(1)}, bf16[768,1024]{1,0:T(8,128)(2,1)S(1)}, u32[]{:S(2)}, u32[]{:S(2)}) collective-permute-start(bf16[768,1024]{1,0:T(8,128)(2,1)S(1)} %convolution_add_fusion), channel_id=1, source_target_pairs={{0,2},{1,3},{2,0},{3,1},{4,6},{5,7},{6,4},{7,5},{8,10},{9,11},{10,... | collective-permute-start | bytes 4718600 | tf_op jit(solution)/shard_map/ppermute | solution.py:1058
  408.6 38.5 %collective-permute-start.27 = (bf16[256,1024]{1,0:T(8,128)(2,1)S(1)}, bf16[256,1024]{1,0:T(8,128)(2,1)S(1)}, u32[]{:S(2)}, u32[]{:S(2)}) collective-permute-start(bf16[256,1024]{1,0:T(8,128)(2,1)S(1)} %maximum_select_fusion.8), channel_id=1, source_target_pairs={{0,8},{4,12},{8,0},{12,4},{16,24},{20,28},{24,16},{28,20},{1,9},{5... | collective-permute-start | bytes 1572872 | tf_op jit(solution)/shard_map/ppermute | solution.py:883
  421.3 26.3 %collective-permute-start.29 = (bf16[160,1024]{1,0:T(8,128)(2,1)S(1)}, bf16[160,1024]{1,0:T(8,128)(2,1)S(1)}, u32[]{:S(2)}, u32[]{:S(2)}) collective-permute-start(bf16[160,1024]{1,0:T(8,128)(2,1)S(1)} %get-tuple-element.262), channel_id=1, source_target_pairs={{0,4},{4,0},{8,12},{12,8},{16,20},{20,16},{24,28},{28,24},{1,5},{5... | collective-permute-start | bytes 983048 | tf_op jit(solution)/shard_map/ppermute | solution.py:883
  421.4 26.3 %collective-permute-start.30 = (bf16[160,1024]{1,0:T(8,128)(2,1)S(1)}, bf16[160,1024]{1,0:T(8,128)(2,1)S(1)}, u32[]{:S(2)}, u32[]{:S(2)}) collective-permute-start(bf16[160,1024]{1,0:T(8,128)(2,1)S(1)} %get-tuple-element.261), channel_id=1, source_target_pairs={{0,16},{4,20},{8,24},{12,28},{16,0},{20,4},{24,8},{28,12},{1,17},{... | collective-permute-start | bytes 983048 | tf_op jit(solution)/shard_map/ppermute | solution.py:883
  424.4 27.3 %collective-permute-start.31 = (bf16[160,1024]{1,0:T(8,128)(2,1)S(1)}, bf16[160,1024]{1,0:T(8,128)(2,1)S(1)}, u32[]{:S(2)}, u32[]{:S(2)}) collective-permute-start(bf16[160,1024]{1,0:T(8,128)(2,1)S(1)} %get-tuple-element.260), channel_id=1, source_target_pairs={{0,20},{4,16},{8,28},{12,24},{16,4},{20,0},{24,12},{28,8},{1,21},{... | collective-permute-start | bytes 983048 | tf_op jit(solution)/shard_map/ppermute | solution.py:883
  447.1 59.5 %collective-permute-start.38 = (bf16[2048,768]{1,0:T(8,128)(2,1)}, bf16[2048,768]{1,0:T(8,128)(2,1)}, u32[]{:S(2)}, u32[]{:S(2)}) collective-permute-start(bf16[2048,768]{1,0:T(8,128)(2,1)} %get-tuple-element.223), channel_id=1, source_target_pairs={{0,1},{1,0},{2,3},{3,2},{4,5},{5,4},{6,7},{7,6},{8,9},{9,8},{10,11... | collective-permute-start | bytes 9437192 | tf_op jit(solution)/shard_map/ppermute | solution.py:1066
  447.6 41.8 %collective-permute-start.36 = (bf16[512,1024]{1,0:T(8,128)(2,1)S(1)}, bf16[512,1024]{1,0:T(8,128)(2,1)S(1)}, u32[]{:S(2)}, u32[]{:S(2)}) collective-permute-start(bf16[512,1024]{1,0:T(8,128)(2,1)S(1)} %maximum_select_fusion.4), channel_id=1, source_target_pairs={{0,4},{4,0},{8,12},{12,8},{16,20},{20,16},{24,28},{28,24},{1,5},{5... | collective-permute-start | bytes 3145736 | tf_op jit(solution)/shard_map/ppermute | solution.py:883
  451.9 35.4 %collective-permute-start.33 = (bf16[160,1024]{1,0:T(8,128)(2,1)S(1)}, bf16[160,1024]{1,0:T(8,128)(2,1)S(1)}, u32[]{:S(2)}, u32[]{:S(2)}) collective-permute-start(bf16[160,1024]{1,0:T(8,128)(2,1)S(1)} %add_convert_fusion.10), channel_id=1, source_target_pairs={{0,4},{4,0},{8,12},{12,8},{16,20},{20,16},{24,28},{28,24},{1,5},{5... | collective-permute-start | bytes 983048 | tf_op jit(solution)/shard_map/ppermute | solution.py:883
  453.5 33.9 %collective-permute-start.34 = (bf16[160,1024]{1,0:T(8,128)(2,1)S(1)}, bf16[160,1024]{1,0:T(8,128)(2,1)S(1)}, u32[]{:S(2)}, u32[]{:S(2)}) collective-permute-start(bf16[160,1024]{1,0:T(8,128)(2,1)S(1)} %add_convert_fusion.10), channel_id=1, source_target_pairs={{0,16},{4,20},{8,24},{12,28},{16,0},{20,4},{24,8},{28,12},{1,17},{... | collective-permute-start | bytes 983048 | tf_op jit(solution)/shard_map/ppermute | solution.py:883
  456.8 30.5 %collective-permute-start.35 = (bf16[160,1024]{1,0:T(8,128)(2,1)S(1)}, bf16[160,1024]{1,0:T(8,128)(2,1)S(1)}, u32[]{:S(2)}, u32[]{:S(2)}) collective-permute-start(bf16[160,1024]{1,0:T(8,128)(2,1)S(1)} %add_convert_fusion.10), channel_id=1, source_target_pairs={{0,20},{4,16},{8,28},{12,24},{16,4},{20,0},{24,12},{28,8},{1,21},{... | collective-permute-start | bytes 983048 | tf_op jit(solution)/shard_map/ppermute | solution.py:883
  492.4 29.1 %collective-permute-start.37 = (bf16[2048,768]{1,0:T(8,128)(2,1)}, bf16[2048,768]{1,0:T(8,128)(2,1)}, u32[]{:S(2)}, u32[]{:S(2)}) collective-permute-start(bf16[2048,768]{1,0:T(8,128)(2,1)} %get-tuple-element.221), channel_id=1, source_target_pairs={{0,1},{1,0},{2,3},{3,2},{4,5},{5,4},{6,7},{7,6},{8,9},{9,8},{10,11... | collective-permute-start | bytes 9437192 | tf_op jit(solution)/shard_map/ppermute | solution.py:1066
  492.4 29.1 %collective-permute-start.40 = (bf16[768,1024]{1,0:T(8,128)(2,1)S(1)}, bf16[768,1024]{1,0:T(8,128)(2,1)}, u32[]{:S(2)}, u32[]{:S(2)}) collective-permute-start(bf16[768,1024]{1,0:T(8,128)(2,1)S(1)} %copy-done.2), channel_id=1, source_target_pairs={{0,1},{1,0},{2,3},{3,2},{4,5},{5,4},{6,7},{7,6},{8,9},{9,8},{10,11... | collective-permute-start | bytes 4718600 | tf_op jit(solution)/shard_map/ppermute | solution.py:1066
  492.9 28.6 %collective-permute-start.41 = (bf16[768,1024]{1,0:T(8,128)(2,1)S(1)}, bf16[768,1024]{1,0:T(8,128)(2,1)}, u32[]{:S(2)}, u32[]{:S(2)}) collective-permute-start(bf16[768,1024]{1,0:T(8,128)(2,1)S(1)} %copy-done.4), channel_id=1, source_target_pairs={{0,1},{1,0},{2,3},{3,2},{4,5},{5,4},{6,7},{7,6},{8,9},{9,8},{10,11... | collective-permute-start | bytes 4718600 | tf_op jit(solution)/shard_map/ppermute | solution.py:1066
  506.1 38.1 %collective-permute-start.39 = (bf16[384,1024]{1,0:T(8,128)(2,1)}, bf16[384,1024]{1,0:T(8,128)(2,1)}, u32[]{:S(2)}, u32[]{:S(2)}) collective-permute-start(bf16[384,1024]{1,0:T(8,128)(2,1)} %constant_dynamic-slice_fusion.3), channel_id=1, source_target_pairs={{0,4},{4,0},{8,12},{12,8},{16,20},{20,16},{24,28},{28,24},{1,5},{5... | collective-permute-start | bytes 2359304 | tf_op jit(solution)/shard_map/ppermute | solution.py:883
  506.7 56.1 %collective-permute-start.49 = (bf16[640,1024]{1,0:T(8,128)(2,1)}, bf16[640,1024]{1,0:T(8,128)(2,1)S(1)}, u32[]{:S(2)}, u32[]{:S(2)}) collective-permute-start(bf16[640,1024]{1,0:T(8,128)(2,1)} %maximum_select_fusion.3), channel_id=1, source_target_pairs={{0,8},{4,12},{8,0},{12,4},{16,24},{20,28},{24,16},{28,20},{1,9},{5... | collective-permute-start | bytes 3932168 | tf_op jit(solution)/shard_map/ppermute | solution.py:883
  (108 other events, 1228.2 us)

commit v4 on v3

--- a/solution.py
+++ b/solution.py
@@ -211,38 +211,48 @@
 
     each_block(1, c - 2, unroll, blocks_from)
 
-    chunks = pl.cdiv(c * sh.length, sh.chunk)
     row = (1, sh.columns)
-    for j in (0, c - 1):
-        at = rows_of(j, sh.length)
-        q_all = spread_heads(rows[at, query : query + sh.lanes], sh)
-
-        def first(i, top):
-            keys = rows_of(i, sh.chunk)
-            scores = contract_cols(rows[keys, key : key + sh.lanes], q_all) * scale
-            scores = scores + widen(bias_ref[keys, : sh.bias_lanes], sh)
-            s_scr[keys, :] = scores
-            return jnp.maximum(top, jnp.max(scores, axis=0, keepdims=True))
-
-        top = lax.fori_loop(0, chunks, first, jnp.full(row, MASKED, jnp.float32))
-
-        def second(i, total):
-            keys = rows_of(i, sh.chunk)
-            shifted = jnp.exp2(s_scr[keys, :] - top)
-            s_scr[keys, :] = shifted
-            return total + jnp.sum(shifted, axis=0, keepdims=True)
-
-        total = lax.fori_loop(0, chunks, second, jnp.zeros(row, jnp.float32))
-        log_ref[pl.ds(j, 1), :] = top + jnp.log2(total)
-        inverse = 1.0 / total
-
-        def third(i, out):
-            keys = rows_of(i, sh.chunk)
-            probs = low(s_scr[keys, :] * inverse)
-            return out + contract_rows(probs, rows[keys, value : value + sh.lanes])
-
-        out = lax.fori_loop(0, chunks, third, jnp.zeros((sh.columns, sh.lanes), jnp.float32))
-        o_scr[at, :] = low(pick_heads(out, sh))
+    ends = [rows_of(j, sh.length) for j in (0, c - 1)]
+    q_ends = [spread_heads(rows[at, query : query + sh.lanes], sh) for at in ends]
+    chunks = sh.span // sh.chunk
+
+    def first(i, tops):
+        keys = rows_of(i, sh.chunk)
+        k_rows = rows[keys, key : key + sh.lanes]
+        mask = widen(bias_ref[keys, : sh.bias_lanes], sh)
+        highest = []
+        for n in range(2):
+            scores = contract_cols(k_rows, q_ends[n]) * scale + mask
+            s_scr[n, keys, :] = scores
+            highest.append(jnp.maximum(tops[n], jnp.max(scores, axis=0, keepdims=True)))
+        return tuple(highest)
+
+    lowest = jnp.full(row, MASKED, jnp.float32)
+    tops = lax.fori_loop(0, chunks, first, (lowest, lowest), unroll=2 - chunks % 2)
+
+    def second(i, carry):
+        keys = rows_of(i, sh.chunk)
+        v_rows = rows[keys, value : value + sh.lanes]
+        found = []
+        for n in range(2):
+            total, out = carry[n]
+            shifted = jnp.exp2(s_scr[n, keys, :] - tops[n])
+            total = total + jnp.sum(shifted, axis=0, keepdims=True)
+            found.append((total, out + contract_rows(low(shifted), v_rows)))
+        return tuple(found)
+
+    empty = (jnp.zeros(row, jnp.float32), jnp.zeros((sh.columns, sh.lanes), jnp.float32))
+    found = lax.fori_loop(0, chunks, second, (empty, empty), unroll=2 - chunks % 2)
+    square = (sh.columns, sh.columns)
+    diagonal = lax.broadcasted_iota(jnp.int32, square, 0) == lax.broadcasted_iota(
+        jnp.int32, square, 1
+    )
+    for n, j in enumerate((0, c - 1)):
+        total, out = found[n]
+        log_ref[pl.ds(j, 1), :] = tops[n] + jnp.log2(total)
+        inverse = jnp.broadcast_to(1.0 / total, square)
+        inverse = jnp.sum(jnp.where(diagonal, inverse, 0.0), axis=1, keepdims=True)
+        o_scr[ends[n], :] = low(pick_heads(out * inverse, sh))
 
     stores = [
         pltpu.make_async_copy(o_scr.at[place(r)], outs[r], sems.at[pieces + r])
@@ -353,12 +363,13 @@
                 random_add(ref, j + u, gained[u][which])
 
     steps = (c - 2) // unroll
-    begin, end = steps * part // parts * unroll, steps * (part + 1) // parts * unroll
+    shares = [-(-steps * n // parts) * unroll for n in (part, part + 1)]
+    begin, end = shares
     if part == parts - 1:
         end = c - 2
     each_block(1 + begin, end - begin, unroll, blocks_from)
 
-    chunks = pl.cdiv(c * length, sh.chunk)
+    chunks = sh.span // sh.chunk
     for j in (0, c - 1)[2 * part // parts : 2 * (part + 1) // parts]:
         at = rows_of(j, length)
         q_all = spread_heads(rows[at, query : query + sh.lanes], sh)
@@ -378,7 +389,8 @@
             va_scr[keys, :] += matmul(low(probs), g_all)
             return total + contract_rows(score_grad, k_all)
 
-        total = lax.fori_loop(0, chunks, chunk, jnp.zeros((sh.columns, sh.lanes), jnp.float32))
+        total = jnp.zeros((sh.columns, sh.lanes), jnp.float32)
+        total = lax.fori_loop(0, chunks, chunk, total, unroll=2 - chunks % 2)
         d_scr[at, : sh.lanes] = low(pick_heads(total, sh) * factor)
 
     for copy in carries:
@@ -414,7 +426,7 @@
     return cost(weight * sh.blocks * sh.slots * sh.length * sh.columns * sh.lanes)
 
 
-def attend_forward(sh, packed, lists, weight=16, unroll=6):
+def attend_forward(sh, packed, lists, weight=16, unroll=15):
     pieces = len(packed)
     used, member, idx, bidx, bias = lists
     rows_each = sh.span // pieces
@@ -427,7 +439,7 @@
         scratch_shapes=[
             pltpu.VMEM((sh.span, 3 * sh.lanes), jnp.bfloat16),
             pltpu.VMEM((sh.span, sh.lanes), jnp.bfloat16),
-            pltpu.VMEM((sh.span, sh.columns), jnp.float32),
+            pltpu.VMEM((2, sh.span, sh.columns), jnp.float32),
             pltpu.SemaphoreType.DMA((2 * pieces,)),
         ],
         compiler_params=pltpu.CompilerParams(vmem_limit_bytes=34 * MEGA),
@@ -437,7 +449,7 @@
     return outs[:pieces], outs[pieces]
 
 
-def attend_backward(sh, packed, tops, made, log_rows, lists, part=(0, 1), carried=(), weight=32, unroll=2):
+def attend_backward(sh, packed, tops, made, log_rows, lists, part=(0, 1), carried=(), weight=32, unroll=4):
     pieces = len(packed)
     used, member, idx, bidx, bias = lists
     rows_each = sh.span // pieces
@@ -1134,7 +1146,7 @@
             arrays = own_parts[r] if s == 0 else None
             if s:
                 early = item_sent[s][:1] if width == model else item_sent[s]
-                arrays = [from_member(array, -r) for array in after(early, packed[s])]
+                arrays = [from_member(array, -r) for array in after(early, made[-1][0])]
                 arrays += item_sent[s][len(early) :]
             part_weights[s, r] = [(arrays[n], row) for n, row in views]
 
@@ -1321,7 +1333,9 @@
         spot = (item + s) % items * members + (member - r) % members
         bias_rows = lax.dynamic_update_slice(bias_rows, bias_sums[s, r], (spot, 0))
     vectors.append(bias_rows)
-    vectors = after(vectors, end_sum.step(), inner_sum.step(pieces[-1][1]))
+    vectors = after(vectors, end_sum.step())
+    arriving = [others for *_, others in inner_sum.pending]
+    vectors = after(vectors, arriving)
     small = sum_all(jnp.concatenate([vector.reshape(-1) for vector in vectors]))
     bias_grad = lax.dynamic_slice_in_dim(small, 5 * model + place * width, width, 0)
     small = small[: 5 * model].reshape(5, model)

time: 620 us -> 604 us (0.974)
  Pallas kernels: 308 us -> 260 us
  waiting for transfers between devices: 53.2 us -> 94.8 us
  local copies, waits for them, and re-layouts: 51.4 us -> 41.3 us
    ppermute x30, waiting for transfers between devices: 36.1 us -> 62.8 us  [swap(): return lax.ppermute(values, axis, [(i, i ^ bit) for i in range(size)])]
    pallas_call x4, Pallas kernels: 89.7 us -> 63.7 us  [attend_backward(): pl.pallas_call(functools.partial(backward_kernel, sh, pieces, unroll, par...]
    pallas_call x2, Pallas kernels: 44.7 us -> 22.3 us  [attend_forward(): pl.pallas_call(functools.partial(forward_kernel, sh, pieces, unroll), in_...]
    ppermute x19, waiting for transfers between devices: 5.72 us -> 13.6 us  [from_member(): return lax.ppermute(values, 'tensor', pairs)]
    ppermute x8, waiting for transfers between devices: 11.3 us -> 18.5 us  [from_item(): return lax.ppermute(values, 'tensor', pairs)]
    unnamed x171 -> x179, local copies, waits for them, and re-layouts: 35.4 us -> 28.5 us
  transfers between devices with their start and end apart: 57 -> 57, of which waited for: 15 -> 15; matrix products, arithmetic and copies ran while one was open for 19% -> 19% of each run, Pallas kernels for 50% -> 44%
where the time goes in v4:
time: 604 us; the launch traced here: 593 us
  Pallas kernels  260 us (43%)
  waiting for transfers between devices  94.8 us (16%)
  starting transfers between devices  89.9 us (15%)
  matrix products  76.5 us (13%)
  local copies, waits for them, and re-layouts  41.3 us (7%)
  other arithmetic  25.9 us (4%)
    pallas_call x3, Pallas kernels, run_middle(): pl.pallas_call(functools.partial(middle_kernel, count, outs_count, head i...  115 us
    ppermute x30, starting transfers between devices, swap(): return lax.ppermute(values, axis, [(i, i ^ bit) for i in range(size)])  77.5 us
    dot_general x13, matrix products, contract_rows(): lax.dot_general(left, right, (((0,), (0,)), ((), ())), preferred_element_...  76.5 us
    pallas_call x4, Pallas kernels, attend_backward(): pl.pallas_call(functools.partial(backward_kernel, sh, pieces, unroll, par...  63.7 us
    ppermute x30, waiting for transfers between devices, swap(): return lax.ppermute(values, axis, [(i, i ^ bit) for i in range(size)])  62.8 us
    unnamed x179, local copies, waits for them, and re-layouts  28.5 us
    pallas_call x2, Pallas kernels, run_last(): pl.pallas_call(functools.partial(last_kernel, parts), grid=(part_rows //...  26.6 us
    pallas_call x2, Pallas kernels, attend_forward(): pl.pallas_call(functools.partial(forward_kernel, sh, pieces, unroll), in_...  22.3 us
  transfers between devices with their start and end apart: 57, of which 15 were waited for; matrix products, arithmetic and copies ran while one was open for 19% of the time, Pallas kernels for 44%

profile of v4, /device:TPU:18, one launch (start us, length us, event | category | flops | bytes accessed | tf_op | source)
XLA Modules:
  0.0 593.5 jit_solution(3090974559591791947)
XLA Ops:
  15.5 7.1 %first.3 = (bf16[2048,1024]{1,0:T(8,128)(2,1)S(1)}, bf16[2048,768]{1,0:T(8,128)(2,1)S(1)}) custom-call(bf16[2048,1024]{1,0:T(8,128)(2,1)S(1)} %copy-done, f32[1,1024]{1,0:T(1,128)S(1)} %bitcast.47, f32[1,1024]{1,0:T(1,128)S(1)} %bitcast.51, bf16[768,1024]{1,0:T(8,128)(2,1)S(1)} %copy-done.2), custom_call_target="tpu_custom_call" | custom-call | flops 2097152 | bytes 1000000 | tf_op jit(solution)/shard_map/first/pallas_call | solution.py:799
  29.9 8.7 %first.2 = (bf16[2048,1024]{1,0:T(8,128)(2,1)S(1)}, bf16[2048,768]{1,0:T(8,128)(2,1)S(1)}) custom-call(bf16[2048,1024]{1,0:T(8,128)(2,1)} %collective-permute-done.1.resid_ref, f32[1,1024]{1,0:T(1,128)S(1)} %bitcast.48, f32[1,1024]{1,0:T(1,128)S(1)} %bitcast.52, bf16[768,1024]{1,0:T(8,128)(2,1)S(1)} %copy-done.2), custom_call_target="tpu_custom_call" | custom-call | flops 2097152 | bytes 1000000 | tf_op jit(solution)/shard_map/first/pallas_call | solution.py:799
  39.4 11.3 %attend_forward.2 = (bf16[2048,256]{1,0:T(8,128)(2,1)S(1)}, bf16[2048,256]{1,0:T(8,128)(2,1)S(1)}, f32[64,256]{1,0:T(8,128)S(1)}) custom-call(s32[1]{0:T(128)} %bitcast.7.used, s32[1]{0:T(128)} %bitcast.8.member, s32[2048]{0:T(1024)S(1)} %squeeze.42.idx, s32[2048]{0:T(1024)S(1)} %squeeze.43.bidx, bf16[2048,768]{1,0:T(8,128)(2,1)S(1)} %copy-done.55, ...), custom_call_target="tpu_custom_call" | custom-call | flops 137438953472 | bytes 1000000 | tf_op jit(solution)/shard_map/attend_forward/pallas_call | solution.py:433
  62.0 11.0 %attend_forward.3 = (bf16[2048,256]{1,0:T(8,128)(2,1)S(1)}, bf16[2048,256]{1,0:T(8,128)(2,1)S(1)}, f32[64,256]{1,0:T(8,128)S(1)}) custom-call(s32[1]{0:T(128)} %bitcast.7.used, s32[1]{0:T(128)} %bitcast.8.member, s32[2048]{0:T(1024)S(1)} %squeeze.44.idx, s32[2048]{0:T(1024)S(1)} %squeeze.45.bidx, bf16[2048,768]{1,0:T(8,128)(2,1)S(1)} %project.2.refs_0_, ...), custom_call_target="tpu_custom_call" | custom-call | bytes 1000000 | tf_op jit(solution)/shard_map/attend_forward/pallas_call | solution.py:433
  73.0 14.5 %collective-permute-done.7.refs_12_.refs_7_.refs_9_ = bf16[1296,1024]{1,0:T(8,128)(2,1)} collective-permute-done((bf16[1296,1024]{1,0:T(8,128)(2,1)}, bf16[1296,1024]{1,0:T(8,128)(2,1)}, u32[]{:S(2)}, u32[]{:S(2)}) %collective-permute-start.7) | collective-permute-done | bytes 2654240 | tf_op jit(solution)/shard_map/ppermute | solution.py:1070
  95.6 34.1 %middle.3 = (bf16[2048,1024]{1,0:T(8,128)(2,1)S(1)}, f32[2048,1024]{1,0:T(8,128)}, bf16[2048,1024]{1,0:T(8,128)(2,1)}, f32[2048,1024]{1,0:T(8,128)}, f32[2048,10...) custom-call(bf16[2048,1024]{1,0:T(8,128)(2,1)} %refs_0_.11, ...), custom_call_target="tpu_custom_call" | custom-call | flops 2097152 | bytes 1000000 | tf_op jit(solution)/shard_map/middle/pallas_call | solution.py:707
  144.9 46.5 %middle.4 = (f32[2048,1024]{1,0:T(8,128)}, f32[2048,1024]{1,0:T(8,128)}, f32[1,2048]{1,0:T(1,128)S(1)}, bf16[2048,1024]{1,0:T(8,128)(2,1)S(1)}, bf16[2048,1024]{...) custom-call(bf16[2048,1024]{1,0:T(8,128)(2,1)} %refs_0_.11, ...), custom_call_target="tpu_custom_call" | custom-call | flops 2097152 | bytes 1000000 | tf_op jit(solution)/shard_map/middle/pallas_call | solution.py:707
  191.5 8.1 %convolution_convert_fusion.3 = bf16[1024,1024]{1,0:T(8,128)(2,1)} fusion(bf16[2048,1024]{1,0:T(8,128)(2,1)S(1)} %get-tuple-element.170, bf16[2048,1024]{1,0:T(8,128)(2,1)} %refs_0_.11), kind=kOutput, calls=%fused_computation.14 | convolution fusion | flops 4296015872 | bytes 10485760 | tf_op jit(solution)/shard_map/dot_general | solution.py:22
  199.7 6.2 %convolution_convert_fusion.2 = bf16[1024,1024]{1,0:T(8,128)(2,1)} fusion(bf16[2048,1024]{1,0:T(8,128)(2,1)S(1)} %copy-done.18, bf16[2048,1024]{1,0:T(8,128)(2,1)S(1)} %copy-done.85), kind=kOutput, calls=%fused_computation.13 | convolution fusion | flops 4296015872 | bytes 10485760 | tf_op jit(solution)/shard_map/dot_general | solution.py:22
  206.3 6.1 %fusion.13 = f32[1024,1024]{1,0:T(8,128)} fusion(bf16[2048,1024]{1,0:T(8,128)(2,1)S(1)} %copy-done.84, bf16[2048,1024]{1,0:T(8,128)(2,1)S(1)} %copy-done.68), kind=kOutput, calls=%fused_computation.98 | convolution fusion | flops 4294967296 | bytes 12582912 | tf_op jit(solution)/shard_map/dot_general | solution.py:22
  212.5 5.8 add_convert_fusion.4
  218.8 5.8 add_convert_fusion.3
  226.1 34.8 %middle.5 = (bf16[2048,1024]{1,0:T(8,128)(2,1)}, f32[2048,1024]{1,0:T(8,128)}, bf16[2048,1024]{1,0:T(8,128)(2,1)S(1)}, f32[1,1024]{1,0:T(1,128)S(1)}, f32[1,1024...) custom-call(bf16[2048,1024]{1,0:T(8,128)(2,1)} %refs_0_.11, ...), custom_call_target="tpu_custom_call" | custom-call | flops 2097152 | bytes 1000000 | tf_op jit(solution)/shard_map/middle/pallas_call | solution.py:707
  265.9 8.3 %convolution_convert_fusion = bf16[1024,1024]{1,0:T(8,128)(2,1)} fusion(bf16[2048,1024]{1,0:T(8,128)(2,1)S(1)} %copy-done.19, bf16[2048,1024]{1,0:T(8,128)(2,1)} %get-tuple-element.186), kind=kOutput, calls=%fused_computation.11 | convolution fusion | flops 4296015872 | bytes 10485760 | tf_op jit(solution)/shard_map/dot_general | solution.py:22
  296.8 14.7 %attend_backward.4 = (bf16[2048,768]{1,0:T(8,128)(2,1)S(1)}, bf16[2048,768]{1,0:T(8,128)(2,1)S(1)}) custom-call(s32[1]{0:T(128)} %bitcast.7.used, s32[1]{0:T(128)} %bitcast.8.member, s32[2048]{0:T(1024)S(1)} %squeeze.44.idx, s32[2048]{0:T(1024)S(1)} %squeeze.45.bidx, bf16[2048,768]{1,0:T(8,128)(2,1)S(1)} %copy-done.9, bf16[2048,768]{1,0:T(8,128)(2,1)S(1)} %copy-done.7, ...), custom_call_target="tpu_custom_call" | custom-call | bytes 1000000 | tf_op jit(solution)/shard_map/attend_backward/pallas_call | solution.py:456
  314.2 12.5 %collective-permute-start.21 = (bf16[256,1024]{1,0:T(8,128)(2,1)S(1)}, bf16[256,1024]{1,0:T(8,128)(2,1)S(1)}, u32[]{:S(2)}, u32[]{:S(2)}) collective-permute-start(bf16[256,1024]{1,0:T(8,128)(2,1)S(1)} %constant_dynamic-slice_fusion.9), channel_id=1, source_target_pairs={{0,8},{4,12},{8,0},{12,4},{16,24},{20,28},{24,16},{28,20},{1,9},{5... | collective-permute-start | bytes 1572872 | tf_op jit(solution)/shard_map/ppermute | solution.py:895
  326.7 6.0 %add_convert_fusion.refs_0_ = bf16[1024,1024]{1,0:T(8,128)(2,1)S(1)} fusion(bf16[1024,1024]{1,0:T(8,128)(2,1)} %collective-permute-done.19, bf16[2048,1024]{1,0:T(8,128)(2,1)S(1)} %copy-done.20, bf16[2048,1024]{1,0:T(8,128)(2,1)S(1)} %copy-done.82), kind=kOutput, calls=%fused_computation | convolution fusion | flops 4298113024 | bytes 12582912 | tf_op jit(solution)/shard_map/dot_general | solution.py:22
  339.7 17.7 %attend_backward.5 = (bf16[2048,768]{1,0:T(8,128)(2,1)S(1)}, bf16[2048,768]{1,0:T(8,128)(2,1)}) custom-call(s32[1]{0:T(128)} %bitcast.7.used, s32[1]{0:T(128)} %bitcast.8.member, s32[2048]{0:T(1024)S(1)} %squeeze.44.idx, s32[2048]{0:T(1024)S(1)} %squeeze.45.bidx, bf16[2048,768]{1,0:T(8,128)(2,1)} %copy-done.8, bf16[2048,768]{1,0:T(8,128)(2,1)} %copy-done.6, ...), custom_call_target="tpu_custom_call" | custom-call | flops 34359738368 | bytes 1000000 | tf_op jit(solution)/shard_map/attend_backward/pallas_call | solution.py:456
  357.4 11.5 %collective-permute-done.25 = bf16[128,1024]{1,0:T(8,128)(2,1)S(1)} collective-permute-done((bf16[128,1024]{1,0:T(8,128)(2,1)S(1)}, bf16[128,1024]{1,0:T(8,128)(2,1)S(1)}, u32[]{:S(2)}, u32[]{:S(2)}) %collective-permute-start.25) | collective-permute-done | bytes 262176 | tf_op jit(solution)/shard_map/ppermute | solution.py:895
  372.6 5.5 convolution_add_fusion
  383.9 7.9 %collective-permute-start.27 = (bf16[256,1024]{1,0:T(8,128)(2,1)S(1)}, bf16[256,1024]{1,0:T(8,128)(2,1)S(1)}, u32[]{:S(2)}, u32[]{:S(2)}) collective-permute-start(bf16[256,1024]{1,0:T(8,128)(2,1)S(1)} %maximum_select_fusion.8), channel_id=1, source_target_pairs={{0,8},{4,12},{8,0},{12,4},{16,24},{20,28},{24,16},{28,20},{1,9},{5... | collective-permute-start | bytes 1572872 | tf_op jit(solution)/shard_map/ppermute | solution.py:895
  394.0 11.0 %collective-permute-start.29 = (bf16[160,1024]{1,0:T(8,128)(2,1)S(1)}, bf16[160,1024]{1,0:T(8,128)(2,1)S(1)}, u32[]{:S(2)}, u32[]{:S(2)}) collective-permute-start(bf16[160,1024]{1,0:T(8,128)(2,1)S(1)} %get-tuple-element.272), channel_id=1, source_target_pairs={{0,4},{4,0},{8,12},{12,8},{16,20},{20,16},{24,28},{28,24},{1,5},{5... | collective-permute-start | bytes 983048 | tf_op jit(solution)/shard_map/ppermute | solution.py:895
  407.4 14.2 %attend_backward.6 = (bf16[2048,768]{1,0:T(8,128)(2,1)S(1)}, bf16[2048,768]{1,0:T(8,128)(2,1)S(1)}) custom-call(s32[1]{0:T(128)} %bitcast.7.used, s32[1]{0:T(128)} %bitcast.8.member, s32[2048]{0:T(1024)S(1)} %copy-done.49, s32[2048]{0:T(1024)S(1)} %copy-done.51, bf16[2048,768]{1,0:T(8,128)(2,1)S(1)} %copy-done.56, bf16[2048,768]{1,0:T(8,128)(2,1)S(1)} %copy-done.58, ...), custom_call_target="tpu_custom_call" | custom-call | flops 34359738368 | bytes 1000000 | tf_op jit(solution)/shard_map/attend_backward/pallas_call | solution.py:456
  423.8 10.2 %collective-permute-start.36 = (bf16[512,1024]{1,0:T(8,128)(2,1)S(1)}, bf16[512,1024]{1,0:T(8,128)(2,1)S(1)}, u32[]{:S(2)}, u32[]{:S(2)}) collective-permute-start(bf16[512,1024]{1,0:T(8,128)(2,1)S(1)} %maximum_select_fusion.4), channel_id=1, source_target_pairs={{0,4},{4,0},{8,12},{12,8},{16,20},{20,16},{24,28},{28,24},{1,5},{5... | collective-permute-start | bytes 3145736 | tf_op jit(solution)/shard_map/ppermute | solution.py:895
  438.9 17.1 %attend_backward.7 = (bf16[2048,768]{1,0:T(8,128)(2,1)S(1)}, bf16[2048,768]{1,0:T(8,128)(2,1)}) custom-call(s32[1]{0:T(128)} %bitcast.7.used, s32[1]{0:T(128)} %bitcast.8.member, s32[2048]{0:T(1024)S(1)} %copy-done.49, s32[2048]{0:T(1024)S(1)} %copy-done.51, bf16[2048,768]{1,0:T(8,128)(2,1)} %copy-done.54, bf16[2048,768]{1,0:T(8,128)(2,1)} %copy-done.57, ...), custom_call_target="tpu_custom_call" | custom-call | flops 34359738368 | bytes 1000000 | tf_op jit(solution)/shard_map/attend_backward/pallas_call | solution.py:456
  456.1 15.7 %collective-permute-done.33 = bf16[160,1024]{1,0:T(8,128)(2,1)S(1)} collective-permute-done((bf16[160,1024]{1,0:T(8,128)(2,1)S(1)}, bf16[160,1024]{1,0:T(8,128)(2,1)S(1)}, u32[]{:S(2)}, u32[]{:S(2)}) %collective-permute-start.33) | collective-permute-done | bytes 327712 | tf_op jit(solution)/shard_map/ppermute | solution.py:895
  477.7 6.3 %fusion.15 = f32[768,1024]{1,0:T(8,128)S(1)} fusion(bf16[2048,768]{1,0:T(8,128)(2,1)} %copy-done.26, bf16[2048,1024]{1,0:T(8,128)(2,1)} %copy-done.30), kind=kOutput, calls=%fused_computation.100 | convolution fusion | flops 3221225472 | bytes 10485760 | tf_op jit(solution)/shard_map/dot_general | solution.py:22
  502.1 13.3 %last.2 = (f32[2048,1024]{1,0:T(8,128)}, f32[1,1024]{1,0:T(1,128)S(1)}, f32[1,1024]{1,0:T(1,128)S(1)}) custom-call(bf16[2048,1024]{1,0:T(8,128)(2,1)S(1)} %copy-done.1, f32[2048,1024]{1,0:T(8,128)S(1)} %copy-done.5, f32[1,1024]{1,0:T(1,128)S(1)} %bitcast.49, bf16[2048,768]{1,0:T(8,128)(2,1)S(1)} %copy-done.27, ...), custom_call_target="tpu_custom_call" | custom-call | flops 6442450944 | bytes 20971520 | tf_op jit(solution)/shard_map/last/pallas_call | solution.py:872
  520.6 13.2 %last.3 = (f32[2048,1024]{1,0:T(8,128)}, f32[1,1024]{1,0:T(1,128)S(1)}, f32[1,1024]{1,0:T(1,128)S(1)}) custom-call(bf16[2048,1024]{1,0:T(8,128)(2,1)S(1)} %copy-done.1, f32[2048,1024]{1,0:T(8,128)S(1)} %copy-done.5, f32[1,1024]{1,0:T(1,128)S(1)} %bitcast.50, bf16[2048,768]{1,0:T(8,128)(2,1)S(1)} %copy-done.27, ...), custom_call_target="tpu_custom_call", output_to_operand_aliasing={{0}: (11, {})} | custom-call | flops 6442450944 | bytes 20971520 | tf_op jit(solution)/shard_map/last/pallas_call | solution.py:872
  539.2 7.9 %collective-permute-start.51 = (f32[9216]{0:T(1024)S(1)}, f32[9216]{0:T(1024)S(1)}, u32[]{:S(2)}, u32[]{:S(2)}) collective-permute-start(f32[9216]{0:T(1024)S(1)} %bitcast_dynamic-update-slice_fusion), channel_id=1, source_target_pairs={{0,2},{1,3},{2,0},{3,1},{4,6},{5,7},{6,4},{7,5},{8,10},{9,11},{10,... | collective-permute-start | bytes 110600 | tf_op jit(solution)/shard_map/ppermute | solution.py:895
  558.2 12.1 %collective-permute-done.47 = bf16[96,1024]{1,0:T(8,128)(2,1)S(1)} collective-permute-done((bf16[96,1024]{1,0:T(8,128)(2,1)S(1)}, bf16[96,1024]{1,0:T(8,128)(2,1)S(1)}, u32[]{:S(2)}, u32[]{:S(2)}) %collective-permute-start.47) | collective-permute-done | bytes 196640 | tf_op jit(solution)/shard_map/ppermute | solution.py:895
  577.6 11.7 %collective-permute-done.56 = f32[9216]{0:T(1024)S(1)} collective-permute-done((f32[9216]{0:T(1024)S(1)}, f32[9216]{0:T(1024)S(1)}, u32[]{:S(2)}, u32[]{:S(2)}) %collective-permute-start.56) | collective-permute-done | bytes 36896 | tf_op jit(solution)/shard_map/ppermute | solution.py:895
  (387 shorter events, 171.3 us)
Async XLA Ops:
  0.7 29.2 %collective-permute-start.1 = (bf16[2048,1024]{1,0:T(8,128)(2,1)}, bf16[2048,1024]{1,0:T(8,128)(2,1)}, u32[]{:S(2)}, u32[]{:S(2)}) collective-permute-start(bf16[2048,1024]{1,0:T(8,128)(2,1)} %refs_0_.13), channel_id=1, source_target_pairs={{0,1},{1,0},{2,3},{3,2},{4,5},{5,4},{6,7},{7,6},{8,9},{9,8},{10,11... | collective-permute-start | bytes 12582920 | tf_op jit(solution)/shard_map/ppermute | solution.py:1078
  5.2 22.5 %collective-permute-start = (bf16[384,1024]{1,0:T(8,128)(2,1)}, bf16[384,1024]{1,0:T(8,128)(2,1)}, u32[]{:S(2)}, u32[]{:S(2)}) collective-permute-start(bf16[384,1024]{1,0:T(8,128)(2,1)} %constant_dynamic-slice_fusion.11), channel_id=1, source_target_pairs={{0,2},{1,3},{2,0},{3,1},{4,6},{5,7},{6,4},{7,5},{8,10},{9,11},{10,... | collective-permute-start | bytes 2359304 | tf_op jit(solution)/shard_map/ppermute | solution.py:1070
  5.8 20.5 %collective-permute-start.3 = (s32[4,64,3]{1,2,0:T(4,128)S(1)}, s32[4,64,3]{1,2,0:T(4,128)S(1)}, u32[]{:S(2)}, u32[]{:S(2)}) collective-permute-start(s32[4,64,3]{1,2,0:T(4,128)S(1)} %copy.49), channel_id=1, source_target_pairs={{0,2},{1,3},{2,0},{3,1},{4,6},{5,7},{6,4},{7,5},{8,10},{9,11},{10,... | collective-permute-start | bytes 9224 | tf_op jit(solution)/shard_map/ppermute | solution.py:1070
  27.8 59.8 %collective-permute-start.7 = (bf16[1296,1024]{1,0:T(8,128)(2,1)}, bf16[1296,1024]{1,0:T(8,128)(2,1)}, u32[]{:S(2)}, u32[]{:S(2)}) collective-permute-start(bf16[1296,1024]{1,0:T(8,128)(2,1)} %bundle.2), channel_id=1, source_target_pairs={{0,2},{1,3},{2,0},{3,1},{4,6},{5,7},{6,4},{7,5},{8,10},{9,11},{10,... | collective-permute-start | bytes 7962632 | tf_op jit(solution)/shard_map/ppermute | solution.py:1070
  28.4 22.3 %collective-permute-start.5 = (bf16[384,1024]{1,0:T(8,128)(2,1)}, bf16[384,1024]{1,0:T(8,128)(2,1)S(1)}, u32[]{:S(2)}, u32[]{:S(2)}) collective-permute-start(bf16[384,1024]{1,0:T(8,128)(2,1)} %collective-permute-done), channel_id=1, source_target_pairs={{0,4},{4,0},{8,12},{12,8},{16,20},{20,16},{24,28},{28,24},{1,5},{5... | collective-permute-start | bytes 2359304 | tf_op jit(solution)/shard_map/ppermute | solution.py:895
  87.6 48.1 %collective-permute-start.9 = (bf16[1024,1024]{1,0:T(8,128)(2,1)S(1)}, bf16[1024,1024]{1,0:T(8,128)(2,1)}, u32[]{:S(2)}, u32[]{:S(2)}) collective-permute-start(bf16[1024,1024]{1,0:T(8,128)(2,1)S(1)} %copy-done.33), channel_id=1, source_target_pairs={{0,2},{1,3},{2,0},{3,1},{4,6},{5,7},{6,4},{7,5},{8,10},{9,11},{10,... | collective-permute-start | bytes 6291464 | tf_op jit(solution)/shard_map/ppermute | solution.py:1070
  135.7 90.4 %collective-permute-start.13 = (bf16[1024,1024]{1,0:T(8,128)(2,1)}, bf16[1024,1024]{1,0:T(8,128)(2,1)S(1)}, u32[]{:S(2)}, u32[]{:S(2)}) collective-permute-start(bf16[1024,1024]{1,0:T(8,128)(2,1)} %refs_14_.1), channel_id=1, source_target_pairs={{0,1},{1,0},{2,3},{3,2},{4,5},{5,4},{6,7},{7,6},{8,9},{9,8},{10,11... | collective-permute-start | bytes 6291464 | tf_op jit(solution)/shard_map/ppermute | solution.py:1078
  218.2 61.3 %collective-permute-start.16 = (bf16[1024,1024]{1,0:T(8,128)(2,1)}, bf16[1024,1024]{1,0:T(8,128)(2,1)S(1)}, u32[]{:S(2)}, u32[]{:S(2)}) collective-permute-start(bf16[1024,1024]{1,0:T(8,128)(2,1)} %add_convert_fusion.4), channel_id=1, source_target_pairs={{0,2},{1,3},{2,0},{3,1},{4,6},{5,7},{6,4},{7,5},{8,10},{9,11},{10,... | collective-permute-start | bytes 6291464 | tf_op jit(solution)/shard_map/ppermute | solution.py:1070
  224.6 102.1 %collective-permute-start.22 = (bf16[1024,1024]{1,0:T(8,128)(2,1)}, bf16[1024,1024]{1,0:T(8,128)(2,1)}, u32[]{:S(2)}, u32[]{:S(2)}) collective-permute-start(bf16[1024,1024]{1,0:T(8,128)(2,1)} %add_convert_fusion.3), channel_id=1, source_target_pairs={{0,2},{1,3},{2,0},{3,1},{4,6},{5,7},{6,4},{7,5},{8,10},{9,11},{10,... | collective-permute-start | bytes 6291464 | tf_op jit(solution)/shard_map/ppermute | solution.py:1070
  282.2 29.2 %collective-permute-start.17 = (bf16[512,1024]{1,0:T(8,128)(2,1)}, bf16[512,1024]{1,0:T(8,128)(2,1)}, u32[]{:S(2)}, u32[]{:S(2)}) collective-permute-start(bf16[512,1024]{1,0:T(8,128)(2,1)} %constant_dynamic-slice_fusion.10), channel_id=1, source_target_pairs={{0,4},{4,0},{8,12},{12,8},{16,20},{20,16},{24,28},{28,24},{1,5},{5... | collective-permute-start | bytes 3145736 | tf_op jit(solution)/shard_map/ppermute | solution.py:895
  288.6 38.1 %collective-permute-start.24 = (bf16[256,1024]{1,0:T(8,128)(2,1)}, bf16[256,1024]{1,0:T(8,128)(2,1)}, u32[]{:S(2)}, u32[]{:S(2)}) collective-permute-start(bf16[256,1024]{1,0:T(8,128)(2,1)} %get-tuple-element.264), channel_id=1, source_target_pairs={{0,2},{1,3},{2,0},{3,1},{4,6},{5,7},{6,4},{7,5},{8,10},{9,11},{10,... | collective-permute-start | bytes 1572872 | tf_op jit(solution)/shard_map/ppermute | solution.py:1070
  288.9 116.9 %collective-permute-start.14 = (bf16[2048,256]{1,0:T(8,128)(2,1)}, bf16[2048,256]{1,0:T(8,128)(2,1)}, u32[]{:S(2)}, u32[]{:S(2)}) collective-permute-start(bf16[2048,256]{1,0:T(8,128)(2,1)} %copy-done.65), channel_id=1, source_target_pairs={{0,1},{1,0},{2,3},{3,2},{4,5},{5,4},{6,7},{7,6},{8,9},{9,8},{10,11... | collective-permute-start | bytes 3145736 | tf_op jit(solution)/shard_map/ppermute | solution.py:1078
  314.2 25.1 %collective-permute-start.21 = (bf16[256,1024]{1,0:T(8,128)(2,1)S(1)}, bf16[256,1024]{1,0:T(8,128)(2,1)S(1)}, u32[]{:S(2)}, u32[]{:S(2)}) collective-permute-start(bf16[256,1024]{1,0:T(8,128)(2,1)S(1)} %constant_dynamic-slice_fusion.9), channel_id=1, source_target_pairs={{0,8},{4,12},{8,0},{12,4},{16,24},{20,28},{24,16},{28,20},{1,9},{5... | collective-permute-start | bytes 1572872 | tf_op jit(solution)/shard_map/ppermute | solution.py:895
  336.3 55.6 %collective-permute-start.28 = (bf16[640,1024]{1,0:T(8,128)(2,1)}, bf16[640,1024]{1,0:T(8,128)(2,1)}, u32[]{:S(2)}, u32[]{:S(2)}) collective-permute-start(bf16[640,1024]{1,0:T(8,128)(2,1)} %constant_dynamic-slice_fusion.7), channel_id=1, source_target_pairs={{0,8},{4,12},{8,0},{12,4},{16,24},{20,28},{24,16},{28,20},{1,9},{5... | collective-permute-start | bytes 3932168 | tf_op jit(solution)/shard_map/ppermute | solution.py:895
  339.5 29.3 %collective-permute-start.25 = (bf16[128,1024]{1,0:T(8,128)(2,1)S(1)}, bf16[128,1024]{1,0:T(8,128)(2,1)S(1)}, u32[]{:S(2)}, u32[]{:S(2)}) collective-permute-start(bf16[128,1024]{1,0:T(8,128)(2,1)S(1)} %constant_dynamic-slice_fusion.8), channel_id=1, source_target_pairs={{0,16},{4,20},{8,24},{12,28},{16,0},{20,4},{24,8},{28,12},{1,17},{... | collective-permute-start | bytes 786440 | tf_op jit(solution)/shard_map/ppermute | solution.py:895
  378.1 59.6 %collective-permute-start.32 = (bf16[768,1024]{1,0:T(8,128)(2,1)S(1)}, bf16[768,1024]{1,0:T(8,128)(2,1)S(1)}, u32[]{:S(2)}, u32[]{:S(2)}) collective-permute-start(bf16[768,1024]{1,0:T(8,128)(2,1)S(1)} %convolution_add_fusion), channel_id=1, source_target_pairs={{0,2},{1,3},{2,0},{3,1},{4,6},{5,7},{6,4},{7,5},{8,10},{9,11},{10,... | collective-permute-start | bytes 4718600 | tf_op jit(solution)/shard_map/ppermute | solution.py:1070
  383.9 39.3 %collective-permute-start.27 = (bf16[256,1024]{1,0:T(8,128)(2,1)S(1)}, bf16[256,1024]{1,0:T(8,128)(2,1)S(1)}, u32[]{:S(2)}, u32[]{:S(2)}) collective-permute-start(bf16[256,1024]{1,0:T(8,128)(2,1)S(1)} %maximum_select_fusion.8), channel_id=1, source_target_pairs={{0,8},{4,12},{8,0},{12,4},{16,24},{20,28},{24,16},{28,20},{1,9},{5... | collective-permute-start | bytes 1572872 | tf_op jit(solution)/shard_map/ppermute | solution.py:895
  394.0 29.8 %collective-permute-start.29 = (bf16[160,1024]{1,0:T(8,128)(2,1)S(1)}, bf16[160,1024]{1,0:T(8,128)(2,1)S(1)}, u32[]{:S(2)}, u32[]{:S(2)}) collective-permute-start(bf16[160,1024]{1,0:T(8,128)(2,1)S(1)} %get-tuple-element.272), channel_id=1, source_target_pairs={{0,4},{4,0},{8,12},{12,8},{16,20},{20,16},{24,28},{28,24},{1,5},{5... | collective-permute-start | bytes 983048 | tf_op jit(solution)/shard_map/ppermute | solution.py:895
  404.9 29.0 %collective-permute-start.30 = (bf16[160,1024]{1,0:T(8,128)(2,1)S(1)}, bf16[160,1024]{1,0:T(8,128)(2,1)S(1)}, u32[]{:S(2)}, u32[]{:S(2)}) collective-permute-start(bf16[160,1024]{1,0:T(8,128)(2,1)S(1)} %get-tuple-element.271), channel_id=1, source_target_pairs={{0,16},{4,20},{8,24},{12,28},{16,0},{20,4},{24,8},{28,12},{1,17},{... | collective-permute-start | bytes 983048 | tf_op jit(solution)/shard_map/ppermute | solution.py:895
  405.8 28.2 %collective-permute-start.31 = (bf16[160,1024]{1,0:T(8,128)(2,1)S(1)}, bf16[160,1024]{1,0:T(8,128)(2,1)S(1)}, u32[]{:S(2)}, u32[]{:S(2)}) collective-permute-start(bf16[160,1024]{1,0:T(8,128)(2,1)S(1)} %get-tuple-element.270), channel_id=1, source_target_pairs={{0,20},{4,16},{8,28},{12,24},{16,4},{20,0},{24,12},{28,8},{1,21},{... | collective-permute-start | bytes 983048 | tf_op jit(solution)/shard_map/ppermute | solution.py:895
  423.3 69.2 %collective-permute-start.38 = (bf16[2048,768]{1,0:T(8,128)(2,1)}, bf16[2048,768]{1,0:T(8,128)(2,1)}, u32[]{:S(2)}, u32[]{:S(2)}) collective-permute-start(bf16[2048,768]{1,0:T(8,128)(2,1)} %get-tuple-element.228), channel_id=1, source_target_pairs={{0,1},{1,0},{2,3},{3,2},{4,5},{5,4},{6,7},{7,6},{8,9},{9,8},{10,11... | collective-permute-start | bytes 9437192 | tf_op jit(solution)/shard_map/ppermute | solution.py:1078
  423.8 50.2 %collective-permute-start.36 = (bf16[512,1024]{1,0:T(8,128)(2,1)S(1)}, bf16[512,1024]{1,0:T(8,128)(2,1)S(1)}, u32[]{:S(2)}, u32[]{:S(2)}) collective-permute-start(bf16[512,1024]{1,0:T(8,128)(2,1)S(1)} %maximum_select_fusion.4), channel_id=1, source_target_pairs={{0,4},{4,0},{8,12},{12,8},{16,20},{20,16},{24,28},{28,24},{1,5},{5... | collective-permute-start | bytes 3145736 | tf_op jit(solution)/shard_map/ppermute | solution.py:895
  434.2 37.6 %collective-permute-start.33 = (bf16[160,1024]{1,0:T(8,128)(2,1)S(1)}, bf16[160,1024]{1,0:T(8,128)(2,1)S(1)}, u32[]{:S(2)}, u32[]{:S(2)}) collective-permute-start(bf16[160,1024]{1,0:T(8,128)(2,1)S(1)} %add_convert_fusion.10), channel_id=1, source_target_pairs={{0,4},{4,0},{8,12},{12,8},{16,20},{20,16},{24,28},{28,24},{1,5},{5... | collective-permute-start | bytes 983048 | tf_op jit(solution)/shard_map/ppermute | solution.py:895
  434.3 37.5 %collective-permute-start.34 = (bf16[160,1024]{1,0:T(8,128)(2,1)S(1)}, bf16[160,1024]{1,0:T(8,128)(2,1)S(1)}, u32[]{:S(2)}, u32[]{:S(2)}) collective-permute-start(bf16[160,1024]{1,0:T(8,128)(2,1)S(1)} %add_convert_fusion.10), channel_id=1, source_target_pairs={{0,16},{4,20},{8,24},{12,28},{16,0},{20,4},{24,8},{28,12},{1,17},{... | collective-permute-start | bytes 983048 | tf_op jit(solution)/shard_map/ppermute | solution.py:895
  437.8 34.1 %collective-permute-start.35 = (bf16[160,1024]{1,0:T(8,128)(2,1)S(1)}, bf16[160,1024]{1,0:T(8,128)(2,1)S(1)}, u32[]{:S(2)}, u32[]{:S(2)}) collective-permute-start(bf16[160,1024]{1,0:T(8,128)(2,1)S(1)} %add_convert_fusion.10), channel_id=1, source_target_pairs={{0,20},{4,16},{8,28},{12,24},{16,4},{20,0},{24,12},{28,8},{1,21},{... | collective-permute-start | bytes 983048 | tf_op jit(solution)/shard_map/ppermute | solution.py:895
  490.5 24.9 %collective-permute-start.39 = (bf16[384,1024]{1,0:T(8,128)(2,1)}, bf16[384,1024]{1,0:T(8,128)(2,1)}, u32[]{:S(2)}, u32[]{:S(2)}) collective-permute-start(bf16[384,1024]{1,0:T(8,128)(2,1)} %constant_dynamic-slice_fusion.3), channel_id=1, source_target_pairs={{0,4},{4,0},{8,12},{12,8},{16,20},{20,16},{24,28},{28,24},{1,5},{5... | collective-permute-start | bytes 2359304 | tf_op jit(solution)/shard_map/ppermute | solution.py:895
  492.5 45.6 %collective-permute-start.49 = (bf16[640,1024]{1,0:T(8,128)(2,1)}, bf16[640,1024]{1,0:T(8,128)(2,1)S(1)}, u32[]{:S(2)}, u32[]{:S(2)}) collective-permute-start(bf16[640,1024]{1,0:T(8,128)(2,1)} %maximum_select_fusion.3), channel_id=1, source_target_pairs={{0,8},{4,12},{8,0},{12,4},{16,24},{20,28},{24,16},{28,20},{1,9},{5... | collective-permute-start | bytes 3932168 | tf_op jit(solution)/shard_map/ppermute | solution.py:895
  519.4 18.6 %collective-permute-start.44 = (bf16[96,1024]{1,0:T(8,128)(2,1)S(1)}, bf16[96,1024]{1,0:T(8,128)(2,1)S(1)}, u32[]{:S(2)}, u32[]{:S(2)}) collective-permute-start(bf16[96,1024]{1,0:T(8,128)(2,1)S(1)} %get-tuple-element.273), channel_id=1, source_target_pairs={{0,24},{4,28},{8,16},{12,20},{16,8},{20,12},{24,0},{28,4},{1,25},{... | collective-permute-start | bytes 589832 | tf_op jit(solution)/shard_map/ppermute | solution.py:895
  548.2 22.2 %collective-permute-start.47 = (bf16[96,1024]{1,0:T(8,128)(2,1)S(1)}, bf16[96,1024]{1,0:T(8,128)(2,1)S(1)}, u32[]{:S(2)}, u32[]{:S(2)}) collective-permute-start(bf16[96,1024]{1,0:T(8,128)(2,1)S(1)} %add_convert_fusion.12), channel_id=1, source_target_pairs={{0,24},{4,28},{8,16},{12,20},{16,8},{20,12},{24,0},{28,4},{1,25},{... | collective-permute-start | bytes 589832 | tf_op jit(solution)/shard_map/ppermute | solution.py:895
  550.7 20.8 %collective-permute-start.53 = (f32[9216]{0:T(1024)S(1)}, f32[9216]{0:T(1024)S(1)}, u32[]{:S(2)}, u32[]{:S(2)}) collective-permute-start(f32[9216]{0:T(1024)S(1)} %add_add_fusion.1), channel_id=1, source_target_pairs={{0,8},{4,12},{8,0},{12,4},{16,24},{20,28},{24,16},{28,20},{1,9},{5... | collective-permute-start | bytes 110600 | tf_op jit(solution)/shard_map/ppermute | solution.py:895
  551.6 19.8 %collective-permute-start.54 = (f32[9216]{0:T(1024)S(1)}, f32[9216]{0:T(1024)S(1)}, u32[]{:S(2)}, u32[]{:S(2)}) collective-permute-start(f32[9216]{0:T(1024)S(1)} %add_add_fusion.1), channel_id=1, source_target_pairs={{0,16},{4,20},{8,24},{12,28},{16,0},{20,4},{24,8},{28,12},{1,17},{... | collective-permute-start | bytes 110600 | tf_op jit(solution)/shard_map/ppermute | solution.py:895
  570.7 19.2 %collective-permute-start.48 = (bf16[384,1024]{1,0:T(8,128)(2,1)S(1)}, bf16[384,1024]{1,0:T(8,128)(2,1)S(1)}, u32[]{:S(2)}, u32[]{:S(2)}) collective-permute-start(bf16[384,1024]{1,0:T(8,128)(2,1)S(1)} %maximum_select_fusion.5), channel_id=1, source_target_pairs={{0,4},{4,0},{8,12},{12,8},{16,20},{20,16},{24,28},{28,24},{1,5},{5... | collective-permute-start | bytes 2359304 | tf_op jit(solution)/shard_map/ppermute | solution.py:895
  (112 other events, 1538.1 us)

commit v5 on v4

--- a/solution.py
+++ b/solution.py
@@ -266,12 +266,12 @@
 
 def backward_kernel(sh, pieces, unroll, part, used, member, idx, bidx, *refs):
     part, parts = part
-    packed, tops, made = refs[:pieces], refs[pieces : 2 * pieces], refs[2 * pieces : 3 * pieces]
-    refs = refs[3 * pieces :]
+    packed, tops = refs[:pieces], refs[pieces : 2 * pieces]
+    refs = refs[2 * pieces :]
     (bias_ref, log_ref), refs = refs[:2], refs[2:]
     carried, refs = refs[: pieces * (part > 0)], refs[pieces * (part > 0) :]
     outs, refs = refs[:pieces], refs[pieces:]
-    rows, grads, merged, d_scr, ka_scr, va_scr, sems = refs[:7]
+    rows, grads, d_scr, ka_scr, va_scr, p_scr, sems = refs[:7]
     c = used[0]
     factor = sh.head_size ** (-0.5)
     scale = factor * LOG2E
@@ -284,7 +284,7 @@
         return rows_of(lax.rem(member[0] + r, pieces), rows_each)
 
     loads = []
-    for n, (sources, target) in enumerate(((packed, rows), (tops, grads), (made, merged))):
+    for n, (sources, target) in enumerate(((packed, rows), (tops, grads))):
         for r in range(pieces):
             copy = pltpu.make_async_copy(
                 sources[r], target.at[place(r)], sems.at[n * pieces + r]
@@ -293,7 +293,7 @@
             copy.start()
     carries = []
     for r in range(pieces if part else 0):
-        copy = pltpu.make_async_copy(carried[r], refs[7].at[place(r)], sems.at[4 * pieces + r])
+        copy = pltpu.make_async_copy(carried[r], refs[7].at[place(r)], sems.at[3 * pieces + r])
         carries.append(copy)
         copy.start()
     d_scr[:, : sh.lanes] = jnp.zeros((sh.span, sh.lanes), d_scr.dtype)
@@ -302,26 +302,19 @@
     for copy in loads:
         copy.wait()
 
-    def equal_rows(products):
-        row = lax.broadcasted_iota(jnp.int32, products.shape, 0)
-        column = lax.broadcasted_iota(jnp.int32, products.shape, 1)
-        return jnp.sum(
-            jnp.where(column % length == row, products, 0.0), axis=0, keepdims=True
-        )
-
     def block(j):
         at = rows_of(j, length)
         q_all = spread_heads(rows[at, query : query + sh.lanes], sh)
         g_all = spread_heads(grads[at, :], sh)
         k_all = gather_rows(rows, key, idx, j, sh)
-        v_all = jnp.concatenate([gather_rows(rows, value, idx, j, sh), merged[at, :]], axis=0)
+        v_all = gather_rows(rows, value, idx, j, sh)
         cuts = [keys_each // 2]
         scores = split_rows(contract_cols, k_all, q_all, cuts) * scale
         prob_grad = split_rows(contract_cols, v_all, g_all, cuts)
-        delta = equal_rows(prob_grad[keys_each:])
         scores = scores + gather_bias(bias_ref, bidx, j, sh)
         probs = jnp.exp2(scores - log_ref[pl.ds(j, 1), :])
-        score_grad = low(probs * (prob_grad[:keys_each] - delta))
+        delta = jnp.sum(probs * prob_grad, axis=0, keepdims=True)
+        score_grad = low(probs * (prob_grad - delta))
         query_grad = pick_heads(contract_rows(score_grad, k_all), sh) * factor
         d_scr[at, : sh.lanes] = low(query_grad)
         return (
@@ -374,20 +367,28 @@
         at = rows_of(j, length)
         q_all = spread_heads(rows[at, query : query + sh.lanes], sh)
         g_all = spread_heads(grads[at, :], sh)
-        delta = equal_rows(contract_cols(merged[at, :], g_all))
         log_row = log_ref[pl.ds(j, 1), :]
+
+        def probs_of(keys):
+            scores = contract_cols(rows[keys, key : key + sh.lanes], q_all) * scale
+            return jnp.exp2(scores + widen(bias_ref[keys, : sh.bias_lanes], sh) - log_row)
+
+        def scan(i, delta):
+            keys = rows_of(i, sh.chunk)
+            prob_grad = contract_cols(rows[keys, value : value + sh.lanes], g_all)
+            p_scr[keys, :] = prob_grad
+            return delta + jnp.sum(probs_of(keys) * prob_grad, axis=0, keepdims=True)
+
+        delta = jnp.zeros((1, sh.columns), jnp.float32)
+        delta = lax.fori_loop(0, chunks, scan, delta, unroll=2 - chunks % 2)
 
         def chunk(i, total):
             keys = rows_of(i, sh.chunk)
-            k_all = rows[keys, key : key + sh.lanes]
-            scores = contract_cols(k_all, q_all) * scale
-            scores = scores + widen(bias_ref[keys, : sh.bias_lanes], sh)
-            probs = jnp.exp2(scores - log_row)
-            prob_grad = contract_cols(rows[keys, value : value + sh.lanes], g_all)
-            score_grad = low(probs * (prob_grad - delta))
+            probs = probs_of(keys)
+            score_grad = low(probs * (p_scr[keys, :] - delta))
             ka_scr[keys, :] += matmul(score_grad, q_all)
             va_scr[keys, :] += matmul(low(probs), g_all)
-            return total + contract_rows(score_grad, k_all)
+            return total + contract_rows(score_grad, rows[keys, key : key + sh.lanes])
 
         total = jnp.zeros((sh.columns, sh.lanes), jnp.float32)
         total = lax.fori_loop(0, chunks, chunk, total, unroll=2 - chunks % 2)
@@ -404,7 +405,7 @@
     d_scr[:, key : key + sh.lanes] = low(with_carried(key, ka_scr[...] * factor))
     d_scr[:, value : value + sh.lanes] = low(with_carried(value, va_scr[...]))
     stores = [
-        pltpu.make_async_copy(d_scr.at[place(r)], outs[r], sems.at[3 * pieces + r])
+        pltpu.make_async_copy(d_scr.at[place(r)], outs[r], sems.at[2 * pieces + r])
         for r in range(pieces)
     ]
     for copy in stores:
@@ -449,14 +450,14 @@
     return outs[:pieces], outs[pieces]
 
 
-def attend_backward(sh, packed, tops, made, log_rows, lists, part=(0, 1), carried=(), weight=32, unroll=4):
+def attend_backward(sh, packed, tops, log_rows, lists, part=(0, 1), carried=(), weight=32, unroll=4):
     pieces = len(packed)
     used, member, idx, bidx, bias = lists
     rows_each = sh.span // pieces
     return pl.pallas_call(
         functools.partial(backward_kernel, sh, pieces, unroll, part),
         in_specs=[SCALARS] * 4
-        + [ANYWHERE] * (3 * pieces)
+        + [ANYWHERE] * (2 * pieces)
         + [ON_CHIP] * 2
         + [ANYWHERE] * len(carried),
         out_specs=[ANYWHERE] * pieces,
@@ -464,19 +465,19 @@
         scratch_shapes=[
             pltpu.VMEM((sh.span, 3 * sh.lanes), jnp.bfloat16),
             pltpu.VMEM((sh.span, sh.lanes), jnp.bfloat16),
-            pltpu.VMEM((sh.span, sh.lanes), jnp.bfloat16),
             pltpu.VMEM((sh.span, 3 * sh.lanes), jnp.bfloat16),
             pltpu.VMEM((sh.span, sh.lanes), jnp.float32),
             pltpu.VMEM((sh.span, sh.lanes), jnp.float32),
-            pltpu.SemaphoreType.DMA((5 * pieces,)),
+            pltpu.VMEM((sh.span, sh.columns), jnp.float32),
+            pltpu.SemaphoreType.DMA((4 * pieces,)),
         ]
         + [pltpu.VMEM((sh.span, 3 * sh.lanes), jnp.bfloat16)] * (len(carried) > 0),
         compiler_params=pltpu.CompilerParams(
-            vmem_limit_bytes=(40 if carried else 34) * MEGA
+            vmem_limit_bytes=(42 if carried else 36) * MEGA
         ),
         cost_estimate=attend_cost(sh, weight // part[1]),
         name="attend_backward",
-    )(used, member, idx, bidx, *packed, *tops, *made, bias, log_rows, *carried)
+    )(used, member, idx, bidx, *packed, *tops, bias, log_rows, *carried)
 
 
 GELU_A = (2 / 3.141592653589793) ** 0.5
@@ -1275,7 +1276,6 @@
                 sh,
                 packed[s],
                 after(top_rows[s], waits),
-                made[s],
                 logs[s],
                 lists[s],
                 (part, BACK_PARTS),

time: 604 us -> 608 us (level)
  Pallas kernels: 260 us -> 287 us
  waiting for transfers between devices: 94.8 us -> 79.5 us
    pallas_call x4, Pallas kernels: 63.7 us -> 80.3 us  [attend_backward(): pl.pallas_call(functools.partial(backward_kernel, sh, pieces, unroll, par...]
    pallas_call x2, Pallas kernels: 22.3 us -> 32.3 us  [attend_forward(): pl.pallas_call(functools.partial(forward_kernel, sh, pieces, unroll), in_...]
    ppermute x8, waiting for transfers between devices: 18.5 us -> 9.27 us  [from_item(): return lax.ppermute(values, 'tensor', pairs)]
    ppermute x30, starting transfers between devices: 77.5 us -> 70.6 us  [swap(): return lax.ppermute(values, axis, [(i, i ^ bit) for i in range(size)])]
    ppermute x30, waiting for transfers between devices: 62.8 us -> 56.7 us  [swap(): return lax.ppermute(values, axis, [(i, i ^ bit) for i in range(size)])]
    unnamed x179 -> x161, local copies, waits for them, and re-layouts: 28.5 us -> 27.8 us
  transfers between devices with their start and end apart: 57 -> 57, of which waited for: 15 -> 15; matrix products, arithmetic and copies ran while one was open for 19% -> 19% of each run, Pallas kernels for 44% -> 48%
where the time goes in v5:
time: 608 us; the launch traced here: 598 us
  Pallas kernels  287 us (47%)
  starting transfers between devices  84.4 us (14%)
  waiting for transfers between devices  79.5 us (13%)
  matrix products  74.1 us (12%)
  local copies, waits for them, and re-layouts  40.6 us (7%)
  other arithmetic  27.2 us (4%)
    pallas_call x3, Pallas kernels, run_middle(): pl.pallas_call(functools.partial(middle_kernel, count, outs_count, head i...  116 us
    pallas_call x4, Pallas kernels, attend_backward(): pl.pallas_call(functools.partial(backward_kernel, sh, pieces, unroll, par...  80.3 us
    dot_general x13, matrix products, contract_rows(): lax.dot_general(left, right, (((0,), (0,)), ((), ())), preferred_element_...  74.1 us
    ppermute x30, starting transfers between devices, swap(): return lax.ppermute(values, axis, [(i, i ^ bit) for i in range(size)])  70.6 us
    ppermute x30, waiting for transfers between devices, swap(): return lax.ppermute(values, axis, [(i, i ^ bit) for i in range(size)])  56.7 us
    pallas_call x2, Pallas kernels, attend_forward(): pl.pallas_call(functools.partial(forward_kernel, sh, pieces, unroll), in_...  32.3 us
    unnamed x161, local copies, waits for them, and re-layouts  27.8 us
    pallas_call x2, Pallas kernels, run_last(): pl.pallas_call(functools.partial(last_kernel, parts), grid=(part_rows //...  26.6 us
  transfers between devices with their start and end apart: 57, of which 15 were waited for; matrix products, arithmetic and copies ran while one was open for 19% of the time, Pallas kernels for 48%

profile of v5, /device:TPU:18, one launch (start us, length us, event | category | flops | bytes accessed | tf_op | source)
XLA Modules:
  0.0 597.9 jit_solution(8144575477720986310)
XLA Ops:
  15.5 7.1 %first.3 = (bf16[2048,1024]{1,0:T(8,128)(2,1)S(1)}, bf16[2048,768]{1,0:T(8,128)(2,1)S(1)}) custom-call(bf16[2048,1024]{1,0:T(8,128)(2,1)S(1)} %copy-done, f32[1,1024]{1,0:T(1,128)S(1)} %bitcast.47, f32[1,1024]{1,0:T(1,128)S(1)} %bitcast.51, bf16[768,1024]{1,0:T(8,128)(2,1)S(1)} %copy-done.2), custom_call_target="tpu_custom_call" | custom-call | flops 2097152 | bytes 1000000 | tf_op jit(solution)/shard_map/first/pallas_call | solution.py:800
  29.9 8.7 %first.2 = (bf16[2048,1024]{1,0:T(8,128)(2,1)S(1)}, bf16[2048,768]{1,0:T(8,128)(2,1)S(1)}) custom-call(bf16[2048,1024]{1,0:T(8,128)(2,1)} %collective-permute-done.1.resid_ref, f32[1,1024]{1,0:T(1,128)S(1)} %bitcast.48, f32[1,1024]{1,0:T(1,128)S(1)} %bitcast.52, bf16[768,1024]{1,0:T(8,128)(2,1)S(1)} %copy-done.2), custom_call_target="tpu_custom_call" | custom-call | flops 2097152 | bytes 1000000 | tf_op jit(solution)/shard_map/first/pallas_call | solution.py:800
  39.4 15.9 %attend_forward.2 = (bf16[2048,256]{1,0:T(8,128)(2,1)S(1)}, bf16[2048,256]{1,0:T(8,128)(2,1)S(1)}, f32[64,256]{1,0:T(8,128)S(1)}) custom-call(s32[1]{0:T(128)} %bitcast.7.used, s32[1]{0:T(128)} %bitcast.8.member, s32[2048]{0:T(1024)S(1)} %squeeze.42.idx, s32[2048]{0:T(1024)S(1)} %squeeze.43.bidx, bf16[2048,768]{1,0:T(8,128)(2,1)S(1)} %copy-done.47, ...), custom_call_target="tpu_custom_call" | custom-call | flops 137438953472 | bytes 1000000 | tf_op jit(solution)/shard_map/attend_forward/pallas_call | solution.py:434
  65.9 16.4 %attend_forward.3 = (bf16[2048,256]{1,0:T(8,128)(2,1)S(1)}, bf16[2048,256]{1,0:T(8,128)(2,1)S(1)}, f32[64,256]{1,0:T(8,128)S(1)}) custom-call(s32[1]{0:T(128)} %bitcast.7.used, s32[1]{0:T(128)} %bitcast.8.member, s32[2048]{0:T(1024)S(1)} %squeeze.44.idx, s32[2048]{0:T(1024)S(1)} %squeeze.45.bidx, bf16[2048,768]{1,0:T(8,128)(2,1)S(1)} %project.2.refs_0_, ...), custom_call_target="tpu_custom_call" | custom-call | bytes 1000000 | tf_op jit(solution)/shard_map/attend_forward/pallas_call | solution.py:434
  82.3 5.3 collective-permute-done.7.refs_12_.refs_7_.refs_9_
  88.6 5.4 collective-permute-done.4.refs_7_
  95.6 34.1 %middle.3 = (bf16[2048,1024]{1,0:T(8,128)(2,1)S(1)}, f32[2048,1024]{1,0:T(8,128)}, bf16[2048,1024]{1,0:T(8,128)(2,1)}, f32[2048,1024]{1,0:T(8,128)}, f32[2048,10...) custom-call(bf16[2048,1024]{1,0:T(8,128)(2,1)} %refs_0_.11, ...), custom_call_target="tpu_custom_call" | custom-call | flops 2097152 | bytes 1000000 | tf_op jit(solution)/shard_map/middle/pallas_call | solution.py:708
  144.9 46.5 %middle.4 = (f32[2048,1024]{1,0:T(8,128)}, f32[2048,1024]{1,0:T(8,128)}, f32[1,2048]{1,0:T(1,128)S(1)}, bf16[2048,1024]{1,0:T(8,128)(2,1)S(1)}, bf16[2048,1024]{...) custom-call(bf16[2048,1024]{1,0:T(8,128)(2,1)} %refs_0_.11, ...), custom_call_target="tpu_custom_call" | custom-call | flops 2097152 | bytes 1000000 | tf_op jit(solution)/shard_map/middle/pallas_call | solution.py:708
  191.4 8.1 %convolution_convert_fusion.3 = bf16[1024,1024]{1,0:T(8,128)(2,1)} fusion(bf16[2048,1024]{1,0:T(8,128)(2,1)S(1)} %get-tuple-element.170, bf16[2048,1024]{1,0:T(8,128)(2,1)} %refs_0_.11), kind=kOutput, calls=%fused_computation.14 | convolution fusion | flops 4296015872 | bytes 10485760 | tf_op jit(solution)/shard_map/dot_general | solution.py:22
  205.1 6.2 %fusion.13 = f32[1024,1024]{1,0:T(8,128)} fusion(bf16[2048,1024]{1,0:T(8,128)(2,1)S(1)} %copy-done.74, bf16[2048,1024]{1,0:T(8,128)(2,1)S(1)} %copy-done.58), kind=kOutput, calls=%fused_computation.98 | convolution fusion | flops 4294967296 | bytes 12582912 | tf_op jit(solution)/shard_map/dot_general | solution.py:22
  211.3 7.0 %add_convert_fusion.4 = bf16[1024,1024]{1,0:T(8,128)(2,1)} fusion(bf16[1024,1024]{1,0:T(8,128)(2,1)} %collective-permute-done.11, bf16[2048,1024]{1,0:T(8,128)(2,1)S(1)} %get-tuple-element.169, bf16[2048,1024]{1,0:T(8,128)(2,1)S(1)} %copy-done.58), kind=kOutput, calls=%fused_computation.4 | convolution fusion | flops 4298113024 | bytes 12582912 | tf_op jit(solution)/shard_map/dot_general | solution.py:22
  218.9 5.8 add_convert_fusion.3
  226.2 35.1 %middle.5 = (bf16[2048,1024]{1,0:T(8,128)(2,1)}, f32[2048,1024]{1,0:T(8,128)}, bf16[2048,1024]{1,0:T(8,128)(2,1)S(1)}, f32[1,1024]{1,0:T(1,128)S(1)}, f32[1,1024...) custom-call(bf16[2048,1024]{1,0:T(8,128)(2,1)} %refs_0_.11, ...), custom_call_target="tpu_custom_call" | custom-call | flops 2097152 | bytes 1000000 | tf_op jit(solution)/shard_map/middle/pallas_call | solution.py:708
  266.3 5.9 convolution_convert_fusion
  281.9 12.1 %collective-permute-start.17 = (bf16[512,1024]{1,0:T(8,128)(2,1)}, bf16[512,1024]{1,0:T(8,128)(2,1)}, u32[]{:S(2)}, u32[]{:S(2)}) collective-permute-start(bf16[512,1024]{1,0:T(8,128)(2,1)} %constant_dynamic-slice_fusion.10), channel_id=1, source_target_pairs={{0,4},{4,0},{8,12},{12,8},{16,20},{20,16},{24,28},{28,24},{1,5},{5... | collective-permute-start | bytes 3145736 | tf_op jit(solution)/shard_map/ppermute | solution.py:896
  302.7 18.8 %attend_backward.4 = (bf16[2048,768]{1,0:T(8,128)(2,1)S(1)}, bf16[2048,768]{1,0:T(8,128)(2,1)S(1)}) custom-call(s32[1]{0:T(128)} %bitcast.7.used, s32[1]{0:T(128)} %bitcast.8.member, s32[2048]{0:T(1024)S(1)} %squeeze.44.idx, s32[2048]{0:T(1024)S(1)} %squeeze.45.bidx, bf16[2048,768]{1,0:T(8,128)(2,1)S(1)} %copy-done.9, bf16[2048,768]{1,0:T(8,128)(2,1)S(1)} %copy-done.7, ...), custom_call_target="tpu_custom_call" | custom-call | bytes 1000000 | tf_op jit(solution)/shard_map/attend_backward/pallas_call | solution.py:457
  326.3 6.0 %add_convert_fusion.refs_0_ = bf16[1024,1024]{1,0:T(8,128)(2,1)S(1)} fusion(bf16[1024,1024]{1,0:T(8,128)(2,1)} %collective-permute-done.19, bf16[2048,1024]{1,0:T(8,128)(2,1)S(1)} %copy-done.20, bf16[2048,1024]{1,0:T(8,128)(2,1)S(1)} %copy-done.72), kind=kOutput, calls=%fused_computation | convolution fusion | flops 4298113024 | bytes 12582912 | tf_op jit(solution)/shard_map/dot_general | solution.py:22
  340.9 22.0 %attend_backward.5 = (bf16[2048,768]{1,0:T(8,128)(2,1)S(1)}, bf16[2048,768]{1,0:T(8,128)(2,1)}) custom-call(s32[1]{0:T(128)} %bitcast.7.used, s32[1]{0:T(128)} %bitcast.8.member, s32[2048]{0:T(1024)S(1)} %squeeze.44.idx, s32[2048]{0:T(1024)S(1)} %squeeze.45.bidx, bf16[2048,768]{1,0:T(8,128)(2,1)} %copy-done.8, bf16[2048,768]{1,0:T(8,128)(2,1)} %copy-done.6, ...), custom_call_target="tpu_custom_call" | custom-call | flops 34359738368 | bytes 1000000 | tf_op jit(solution)/shard_map/attend_backward/pallas_call | solution.py:457
  362.9 10.2 %collective-permute-done.25 = bf16[128,1024]{1,0:T(8,128)(2,1)S(1)} collective-permute-done((bf16[128,1024]{1,0:T(8,128)(2,1)S(1)}, bf16[128,1024]{1,0:T(8,128)(2,1)S(1)}, u32[]{:S(2)}, u32[]{:S(2)}) %collective-permute-start.25) | collective-permute-done | bytes 262176 | tf_op jit(solution)/shard_map/ppermute | solution.py:896
  376.8 5.4 convolution_add_fusion
  390.4 14.0 %collective-permute-start.29 = (bf16[160,1024]{1,0:T(8,128)(2,1)S(1)}, bf16[160,1024]{1,0:T(8,128)(2,1)S(1)}, u32[]{:S(2)}, u32[]{:S(2)}) collective-permute-start(bf16[160,1024]{1,0:T(8,128)(2,1)S(1)} %get-tuple-element.272), channel_id=1, source_target_pairs={{0,4},{4,0},{8,12},{12,8},{16,20},{20,16},{24,28},{28,24},{1,5},{5... | collective-permute-start | bytes 983048 | tf_op jit(solution)/shard_map/ppermute | solution.py:896
  406.9 18.2 %attend_backward.6 = (bf16[2048,768]{1,0:T(8,128)(2,1)S(1)}, bf16[2048,768]{1,0:T(8,128)(2,1)S(1)}) custom-call(s32[1]{0:T(128)} %bitcast.7.used, s32[1]{0:T(128)} %bitcast.8.member, s32[2048]{0:T(1024)S(1)} %copy-done.41, s32[2048]{0:T(1024)S(1)} %copy-done.43, bf16[2048,768]{1,0:T(8,128)(2,1)S(1)} %copy-done.48, bf16[2048,768]{1,0:T(8,128)(2,1)S(1)} %copy-done.50, ...), custom_call_target="tpu_custom_call" | custom-call | flops 34359738368 | bytes 1000000 | tf_op jit(solution)/shard_map/attend_backward/pallas_call | solution.py:457
  427.3 16.3 %collective-permute-start.36 = (bf16[512,1024]{1,0:T(8,128)(2,1)S(1)}, bf16[512,1024]{1,0:T(8,128)(2,1)S(1)}, u32[]{:S(2)}, u32[]{:S(2)}) collective-permute-start(bf16[512,1024]{1,0:T(8,128)(2,1)S(1)} %maximum_select_fusion.4), channel_id=1, source_target_pairs={{0,4},{4,0},{8,12},{12,8},{16,20},{20,16},{24,28},{28,24},{1,5},{5... | collective-permute-start | bytes 3145736 | tf_op jit(solution)/shard_map/ppermute | solution.py:896
  448.3 21.4 %attend_backward.7 = (bf16[2048,768]{1,0:T(8,128)(2,1)S(1)}, bf16[2048,768]{1,0:T(8,128)(2,1)}) custom-call(s32[1]{0:T(128)} %bitcast.7.used, s32[1]{0:T(128)} %bitcast.8.member, s32[2048]{0:T(1024)S(1)} %copy-done.41, s32[2048]{0:T(1024)S(1)} %copy-done.43, bf16[2048,768]{1,0:T(8,128)(2,1)} %copy-done.46, bf16[2048,768]{1,0:T(8,128)(2,1)} %copy-done.49, ...), custom_call_target="tpu_custom_call" | custom-call | flops 34359738368 | bytes 1000000 | tf_op jit(solution)/shard_map/attend_backward/pallas_call | solution.py:457
  469.7 11.8 %collective-permute-done.33 = bf16[160,1024]{1,0:T(8,128)(2,1)S(1)} collective-permute-done((bf16[160,1024]{1,0:T(8,128)(2,1)S(1)}, bf16[160,1024]{1,0:T(8,128)(2,1)S(1)}, u32[]{:S(2)}, u32[]{:S(2)}) %collective-permute-start.33) | collective-permute-done | bytes 327712 | tf_op jit(solution)/shard_map/ppermute | solution.py:896
  487.1 6.3 %fusion.15 = f32[768,1024]{1,0:T(8,128)S(1)} fusion(bf16[2048,768]{1,0:T(8,128)(2,1)} %copy-done.26, bf16[2048,1024]{1,0:T(8,128)(2,1)} %copy-done.30), kind=kOutput, calls=%fused_computation.100 | convolution fusion | flops 3221225472 | bytes 10485760 | tf_op jit(solution)/shard_map/dot_general | solution.py:22
  493.5 5.4 add_convert_fusion.5
  511.8 13.3 %last.2 = (f32[2048,1024]{1,0:T(8,128)}, f32[1,1024]{1,0:T(1,128)S(1)}, f32[1,1024]{1,0:T(1,128)S(1)}) custom-call(bf16[2048,1024]{1,0:T(8,128)(2,1)S(1)} %copy-done.1, f32[2048,1024]{1,0:T(8,128)S(1)} %copy-done.5, f32[1,1024]{1,0:T(1,128)S(1)} %bitcast.49, bf16[2048,768]{1,0:T(8,128)(2,1)S(1)} %copy-done.27, ...), custom_call_target="tpu_custom_call" | custom-call | flops 6442450944 | bytes 20971520 | tf_op jit(solution)/shard_map/last/pallas_call | solution.py:873
  530.4 13.2 %last.3 = (f32[2048,1024]{1,0:T(8,128)}, f32[1,1024]{1,0:T(1,128)S(1)}, f32[1,1024]{1,0:T(1,128)S(1)}) custom-call(bf16[2048,1024]{1,0:T(8,128)(2,1)S(1)} %copy-done.1, f32[2048,1024]{1,0:T(8,128)S(1)} %copy-done.5, f32[1,1024]{1,0:T(1,128)S(1)} %bitcast.50, bf16[2048,768]{1,0:T(8,128)(2,1)S(1)} %copy-done.27, ...), custom_call_target="tpu_custom_call", output_to_operand_aliasing={{0}: (11, {})} | custom-call | flops 6442450944 | bytes 20971520 | tf_op jit(solution)/shard_map/last/pallas_call | solution.py:873
  561.1 5.8 collective-permute-done.46
  566.9 7.4 %collective-permute-done.47 = bf16[96,1024]{1,0:T(8,128)(2,1)S(1)} collective-permute-done((bf16[96,1024]{1,0:T(8,128)(2,1)S(1)}, bf16[96,1024]{1,0:T(8,128)(2,1)S(1)}, u32[]{:S(2)}, u32[]{:S(2)}) %collective-permute-start.47) | collective-permute-done | bytes 196640 | tf_op jit(solution)/shard_map/ppermute | solution.py:896
  581.6 11.9 %collective-permute-done.56 = f32[9216]{0:T(1024)S(1)} collective-permute-done((f32[9216]{0:T(1024)S(1)}, f32[9216]{0:T(1024)S(1)}, u32[]{:S(2)}, u32[]{:S(2)}) %collective-permute-start.56) | collective-permute-done | bytes 36896 | tf_op jit(solution)/shard_map/ppermute | solution.py:896
  (369 shorter events, 165.5 us)
Async XLA Ops:
  0.7 29.2 %collective-permute-start.1 = (bf16[2048,1024]{1,0:T(8,128)(2,1)}, bf16[2048,1024]{1,0:T(8,128)(2,1)}, u32[]{:S(2)}, u32[]{:S(2)}) collective-permute-start(bf16[2048,1024]{1,0:T(8,128)(2,1)} %refs_0_.13), channel_id=1, source_target_pairs={{0,1},{1,0},{2,3},{3,2},{4,5},{5,4},{6,7},{7,6},{8,9},{9,8},{10,11... | collective-permute-start | bytes 12582920 | tf_op jit(solution)/shard_map/ppermute | solution.py:1079
  5.2 22.6 %collective-permute-start = (bf16[384,1024]{1,0:T(8,128)(2,1)}, bf16[384,1024]{1,0:T(8,128)(2,1)}, u32[]{:S(2)}, u32[]{:S(2)}) collective-permute-start(bf16[384,1024]{1,0:T(8,128)(2,1)} %constant_dynamic-slice_fusion.11), channel_id=1, source_target_pairs={{0,2},{1,3},{2,0},{3,1},{4,6},{5,7},{6,4},{7,5},{8,10},{9,11},{10,... | collective-permute-start | bytes 2359304 | tf_op jit(solution)/shard_map/ppermute | solution.py:1071
  5.8 20.5 %collective-permute-start.3 = (s32[4,64,3]{1,2,0:T(4,128)S(1)}, s32[4,64,3]{1,2,0:T(4,128)S(1)}, u32[]{:S(2)}, u32[]{:S(2)}) collective-permute-start(s32[4,64,3]{1,2,0:T(4,128)S(1)} %copy.49), channel_id=1, source_target_pairs={{0,2},{1,3},{2,0},{3,1},{4,6},{5,7},{6,4},{7,5},{8,10},{9,11},{10,... | collective-permute-start | bytes 9224 | tf_op jit(solution)/shard_map/ppermute | solution.py:1071
  27.8 59.8 %collective-permute-start.7 = (bf16[1296,1024]{1,0:T(8,128)(2,1)}, bf16[1296,1024]{1,0:T(8,128)(2,1)}, u32[]{:S(2)}, u32[]{:S(2)}) collective-permute-start(bf16[1296,1024]{1,0:T(8,128)(2,1)} %bundle.2), channel_id=1, source_target_pairs={{0,2},{1,3},{2,0},{3,1},{4,6},{5,7},{6,4},{7,5},{8,10},{9,11},{10,... | collective-permute-start | bytes 7962632 | tf_op jit(solution)/shard_map/ppermute | solution.py:1071
  28.4 26.9 %collective-permute-start.5 = (bf16[384,1024]{1,0:T(8,128)(2,1)}, bf16[384,1024]{1,0:T(8,128)(2,1)S(1)}, u32[]{:S(2)}, u32[]{:S(2)}) collective-permute-start(bf16[384,1024]{1,0:T(8,128)(2,1)} %collective-permute-done), channel_id=1, source_target_pairs={{0,4},{4,0},{8,12},{12,8},{16,20},{20,16},{24,28},{28,24},{1,5},{5... | collective-permute-start | bytes 2359304 | tf_op jit(solution)/shard_map/ppermute | solution.py:896
  87.6 48.1 %collective-permute-start.9 = (bf16[1024,1024]{1,0:T(8,128)(2,1)S(1)}, bf16[1024,1024]{1,0:T(8,128)(2,1)}, u32[]{:S(2)}, u32[]{:S(2)}) collective-permute-start(bf16[1024,1024]{1,0:T(8,128)(2,1)S(1)} %copy-done.33), channel_id=1, source_target_pairs={{0,2},{1,3},{2,0},{3,1},{4,6},{5,7},{6,4},{7,5},{8,10},{9,11},{10,... | collective-permute-start | bytes 6291464 | tf_op jit(solution)/shard_map/ppermute | solution.py:1071
  135.7 90.4 %collective-permute-start.13 = (bf16[1024,1024]{1,0:T(8,128)(2,1)}, bf16[1024,1024]{1,0:T(8,128)(2,1)S(1)}, u32[]{:S(2)}, u32[]{:S(2)}) collective-permute-start(bf16[1024,1024]{1,0:T(8,128)(2,1)} %refs_14_.1), channel_id=1, source_target_pairs={{0,1},{1,0},{2,3},{3,2},{4,5},{5,4},{6,7},{7,6},{8,9},{9,8},{10,11... | collective-permute-start | bytes 6291464 | tf_op jit(solution)/shard_map/ppermute | solution.py:1079
  218.3 59.2 %collective-permute-start.16 = (bf16[1024,1024]{1,0:T(8,128)(2,1)}, bf16[1024,1024]{1,0:T(8,128)(2,1)}, u32[]{:S(2)}, u32[]{:S(2)}) collective-permute-start(bf16[1024,1024]{1,0:T(8,128)(2,1)} %add_convert_fusion.4), channel_id=1, source_target_pairs={{0,2},{1,3},{2,0},{3,1},{4,6},{5,7},{6,4},{7,5},{8,10},{9,11},{10,... | collective-permute-start | bytes 6291464 | tf_op jit(solution)/shard_map/ppermute | solution.py:1071
  224.7 99.6 %collective-permute-start.22 = (bf16[1024,1024]{1,0:T(8,128)(2,1)}, bf16[1024,1024]{1,0:T(8,128)(2,1)}, u32[]{:S(2)}, u32[]{:S(2)}) collective-permute-start(bf16[1024,1024]{1,0:T(8,128)(2,1)} %add_convert_fusion.3), channel_id=1, source_target_pairs={{0,2},{1,3},{2,0},{3,1},{4,6},{5,7},{6,4},{7,5},{8,10},{9,11},{10,... | collective-permute-start | bytes 6291464 | tf_op jit(solution)/shard_map/ppermute | solution.py:1071
  272.2 25.1 %collective-permute-start.19 = (bf16[1024,1024]{1,0:T(8,128)(2,1)}, bf16[1024,1024]{1,0:T(8,128)(2,1)}, u32[]{:S(2)}, u32[]{:S(2)}) collective-permute-start(bf16[1024,1024]{1,0:T(8,128)(2,1)} %convolution_convert_fusion), channel_id=1, source_target_pairs={{0,1},{1,0},{2,3},{3,2},{4,5},{5,4},{6,7},{7,6},{8,9},{9,8},{10,11... | collective-permute-start | bytes 6291464 | tf_op jit(solution)/shard_map/ppermute | solution.py:1079
  277.5 19.8 %collective-permute-start.18 = (bf16[2048,256]{1,0:T(8,128)(2,1)}, bf16[2048,256]{1,0:T(8,128)(2,1)}, u32[]{:S(2)}, u32[]{:S(2)}) collective-permute-start(bf16[2048,256]{1,0:T(8,128)(2,1)} %get-tuple-element.185), channel_id=1, source_target_pairs={{0,1},{1,0},{2,3},{3,2},{4,5},{5,4},{6,7},{7,6},{8,9},{9,8},{10,11... | collective-permute-start | bytes 3145736 | tf_op jit(solution)/shard_map/ppermute | solution.py:1079
  281.9 39.6 %collective-permute-start.17 = (bf16[512,1024]{1,0:T(8,128)(2,1)}, bf16[512,1024]{1,0:T(8,128)(2,1)}, u32[]{:S(2)}, u32[]{:S(2)}) collective-permute-start(bf16[512,1024]{1,0:T(8,128)(2,1)} %constant_dynamic-slice_fusion.10), channel_id=1, source_target_pairs={{0,4},{4,0},{8,12},{12,8},{16,20},{20,16},{24,28},{28,24},{1,5},{5... | collective-permute-start | bytes 3145736 | tf_op jit(solution)/shard_map/ppermute | solution.py:896
  297.0 27.2 %collective-permute-start.24 = (bf16[256,1024]{1,0:T(8,128)(2,1)}, bf16[256,1024]{1,0:T(8,128)(2,1)}, u32[]{:S(2)}, u32[]{:S(2)}) collective-permute-start(bf16[256,1024]{1,0:T(8,128)(2,1)} %get-tuple-element.264), channel_id=1, source_target_pairs={{0,2},{1,3},{2,0},{3,1},{4,6},{5,7},{6,4},{7,5},{8,10},{9,11},{10,... | collective-permute-start | bytes 1572872 | tf_op jit(solution)/shard_map/ppermute | solution.py:1071
  297.3 108.9 %collective-permute-start.14 = (bf16[2048,256]{1,0:T(8,128)(2,1)}, bf16[2048,256]{1,0:T(8,128)(2,1)}, u32[]{:S(2)}, u32[]{:S(2)}) collective-permute-start(bf16[2048,256]{1,0:T(8,128)(2,1)} %copy-done.55), channel_id=1, source_target_pairs={{0,1},{1,0},{2,3},{3,2},{4,5},{5,4},{6,7},{7,6},{8,9},{9,8},{10,11... | collective-permute-start | bytes 3145736 | tf_op jit(solution)/shard_map/ppermute | solution.py:1079
  335.8 52.1 %collective-permute-start.28 = (bf16[640,1024]{1,0:T(8,128)(2,1)}, bf16[640,1024]{1,0:T(8,128)(2,1)}, u32[]{:S(2)}, u32[]{:S(2)}) collective-permute-start(bf16[640,1024]{1,0:T(8,128)(2,1)} %constant_dynamic-slice_fusion.7), channel_id=1, source_target_pairs={{0,8},{4,12},{8,0},{12,4},{16,24},{20,28},{24,16},{28,20},{1,9},{5... | collective-permute-start | bytes 3932168 | tf_op jit(solution)/shard_map/ppermute | solution.py:896
  338.8 34.2 %collective-permute-start.25 = (bf16[128,1024]{1,0:T(8,128)(2,1)S(1)}, bf16[128,1024]{1,0:T(8,128)(2,1)S(1)}, u32[]{:S(2)}, u32[]{:S(2)}) collective-permute-start(bf16[128,1024]{1,0:T(8,128)(2,1)S(1)} %constant_dynamic-slice_fusion.8), channel_id=1, source_target_pairs={{0,16},{4,20},{8,24},{12,28},{16,0},{20,4},{24,8},{28,12},{1,17},{... | collective-permute-start | bytes 786440 | tf_op jit(solution)/shard_map/ppermute | solution.py:896
  382.3 61.8 %collective-permute-start.32 = (bf16[768,1024]{1,0:T(8,128)(2,1)S(1)}, bf16[768,1024]{1,0:T(8,128)(2,1)S(1)}, u32[]{:S(2)}, u32[]{:S(2)}) collective-permute-start(bf16[768,1024]{1,0:T(8,128)(2,1)S(1)} %convolution_add_fusion), channel_id=1, source_target_pairs={{0,2},{1,3},{2,0},{3,1},{4,6},{5,7},{6,4},{7,5},{8,10},{9,11},{10,... | collective-permute-start | bytes 4718600 | tf_op jit(solution)/shard_map/ppermute | solution.py:1071
  387.2 39.5 %collective-permute-start.27 = (bf16[256,1024]{1,0:T(8,128)(2,1)S(1)}, bf16[256,1024]{1,0:T(8,128)(2,1)S(1)}, u32[]{:S(2)}, u32[]{:S(2)}) collective-permute-start(bf16[256,1024]{1,0:T(8,128)(2,1)S(1)} %maximum_select_fusion.8), channel_id=1, source_target_pairs={{0,8},{4,12},{8,0},{12,4},{16,24},{20,28},{24,16},{28,20},{1,9},{5... | collective-permute-start | bytes 1572872 | tf_op jit(solution)/shard_map/ppermute | solution.py:896
  390.4 36.8 %collective-permute-start.29 = (bf16[160,1024]{1,0:T(8,128)(2,1)S(1)}, bf16[160,1024]{1,0:T(8,128)(2,1)S(1)}, u32[]{:S(2)}, u32[]{:S(2)}) collective-permute-start(bf16[160,1024]{1,0:T(8,128)(2,1)S(1)} %get-tuple-element.272), channel_id=1, source_target_pairs={{0,4},{4,0},{8,12},{12,8},{16,20},{20,16},{24,28},{28,24},{1,5},{5... | collective-permute-start | bytes 983048 | tf_op jit(solution)/shard_map/ppermute | solution.py:896
  404.4 39.2 %collective-permute-start.30 = (bf16[160,1024]{1,0:T(8,128)(2,1)S(1)}, bf16[160,1024]{1,0:T(8,128)(2,1)S(1)}, u32[]{:S(2)}, u32[]{:S(2)}) collective-permute-start(bf16[160,1024]{1,0:T(8,128)(2,1)S(1)} %get-tuple-element.271), channel_id=1, source_target_pairs={{0,16},{4,20},{8,24},{12,28},{16,0},{20,4},{24,8},{28,12},{1,17},{... | collective-permute-start | bytes 983048 | tf_op jit(solution)/shard_map/ppermute | solution.py:896
  406.2 37.4 %collective-permute-start.31 = (bf16[160,1024]{1,0:T(8,128)(2,1)S(1)}, bf16[160,1024]{1,0:T(8,128)(2,1)S(1)}, u32[]{:S(2)}, u32[]{:S(2)}) collective-permute-start(bf16[160,1024]{1,0:T(8,128)(2,1)S(1)} %get-tuple-element.270), channel_id=1, source_target_pairs={{0,20},{4,16},{8,28},{12,24},{16,4},{20,0},{24,12},{28,8},{1,21},{... | collective-permute-start | bytes 983048 | tf_op jit(solution)/shard_map/ppermute | solution.py:896
  426.8 75.5 %collective-permute-start.38 = (bf16[2048,768]{1,0:T(8,128)(2,1)}, bf16[2048,768]{1,0:T(8,128)(2,1)}, u32[]{:S(2)}, u32[]{:S(2)}) collective-permute-start(bf16[2048,768]{1,0:T(8,128)(2,1)} %get-tuple-element.228), channel_id=1, source_target_pairs={{0,1},{1,0},{2,3},{3,2},{4,5},{5,4},{6,7},{7,6},{8,9},{9,8},{10,11... | collective-permute-start | bytes 9437192 | tf_op jit(solution)/shard_map/ppermute | solution.py:1079
  427.3 56.4 %collective-permute-start.36 = (bf16[512,1024]{1,0:T(8,128)(2,1)S(1)}, bf16[512,1024]{1,0:T(8,128)(2,1)S(1)}, u32[]{:S(2)}, u32[]{:S(2)}) collective-permute-start(bf16[512,1024]{1,0:T(8,128)(2,1)S(1)} %maximum_select_fusion.4), channel_id=1, source_target_pairs={{0,4},{4,0},{8,12},{12,8},{16,20},{20,16},{24,28},{28,24},{1,5},{5... | collective-permute-start | bytes 3145736 | tf_op jit(solution)/shard_map/ppermute | solution.py:896
  443.9 37.6 %collective-permute-start.33 = (bf16[160,1024]{1,0:T(8,128)(2,1)S(1)}, bf16[160,1024]{1,0:T(8,128)(2,1)S(1)}, u32[]{:S(2)}, u32[]{:S(2)}) collective-permute-start(bf16[160,1024]{1,0:T(8,128)(2,1)S(1)} %add_convert_fusion.10), channel_id=1, source_target_pairs={{0,4},{4,0},{8,12},{12,8},{16,20},{20,16},{24,28},{28,24},{1,5},{5... | collective-permute-start | bytes 983048 | tf_op jit(solution)/shard_map/ppermute | solution.py:896
  443.9 37.5 %collective-permute-start.34 = (bf16[160,1024]{1,0:T(8,128)(2,1)S(1)}, bf16[160,1024]{1,0:T(8,128)(2,1)S(1)}, u32[]{:S(2)}, u32[]{:S(2)}) collective-permute-start(bf16[160,1024]{1,0:T(8,128)(2,1)S(1)} %add_convert_fusion.10), channel_id=1, source_target_pairs={{0,16},{4,20},{8,24},{12,28},{16,0},{20,4},{24,8},{28,12},{1,17},{... | collective-permute-start | bytes 983048 | tf_op jit(solution)/shard_map/ppermute | solution.py:896
  444.0 37.5 %collective-permute-start.35 = (bf16[160,1024]{1,0:T(8,128)(2,1)S(1)}, bf16[160,1024]{1,0:T(8,128)(2,1)S(1)}, u32[]{:S(2)}, u32[]{:S(2)}) collective-permute-start(bf16[160,1024]{1,0:T(8,128)(2,1)S(1)} %add_convert_fusion.10), channel_id=1, source_target_pairs={{0,20},{4,16},{8,28},{12,24},{16,4},{20,0},{24,12},{28,8},{1,21},{... | collective-permute-start | bytes 983048 | tf_op jit(solution)/shard_map/ppermute | solution.py:896
  500.0 25.2 %collective-permute-start.39 = (bf16[384,1024]{1,0:T(8,128)(2,1)}, bf16[384,1024]{1,0:T(8,128)(2,1)}, u32[]{:S(2)}, u32[]{:S(2)}) collective-permute-start(bf16[384,1024]{1,0:T(8,128)(2,1)} %constant_dynamic-slice_fusion.3), channel_id=1, source_target_pairs={{0,4},{4,0},{8,12},{12,8},{16,20},{20,16},{24,28},{28,24},{1,5},{5... | collective-permute-start | bytes 2359304 | tf_op jit(solution)/shard_map/ppermute | solution.py:896
  502.3 45.7 %collective-permute-start.49 = (bf16[640,1024]{1,0:T(8,128)(2,1)}, bf16[640,1024]{1,0:T(8,128)(2,1)S(1)}, u32[]{:S(2)}, u32[]{:S(2)}) collective-permute-start(bf16[640,1024]{1,0:T(8,128)(2,1)} %maximum_select_fusion.3), channel_id=1, source_target_pairs={{0,8},{4,12},{8,0},{12,4},{16,24},{20,28},{24,16},{28,20},{1,9},{5... | collective-permute-start | bytes 3932168 | tf_op jit(solution)/shard_map/ppermute | solution.py:896
  552.8 21.5 %collective-permute-start.47 = (bf16[96,1024]{1,0:T(8,128)(2,1)S(1)}, bf16[96,1024]{1,0:T(8,128)(2,1)S(1)}, u32[]{:S(2)}, u32[]{:S(2)}) collective-permute-start(bf16[96,1024]{1,0:T(8,128)(2,1)S(1)} %add_convert_fusion.12), channel_id=1, source_target_pairs={{0,24},{4,28},{8,16},{12,20},{16,8},{20,12},{24,0},{28,4},{1,25},{... | collective-permute-start | bytes 589832 | tf_op jit(solution)/shard_map/ppermute | solution.py:896
  554.4 21.0 %collective-permute-start.53 = (f32[9216]{0:T(1024)S(1)}, f32[9216]{0:T(1024)S(1)}, u32[]{:S(2)}, u32[]{:S(2)}) collective-permute-start(f32[9216]{0:T(1024)S(1)} %add_add_fusion.1), channel_id=1, source_target_pairs={{0,8},{4,12},{8,0},{12,4},{16,24},{20,28},{24,16},{28,20},{1,9},{5... | collective-permute-start | bytes 110600 | tf_op jit(solution)/shard_map/ppermute | solution.py:896
  555.4 20.0 %collective-permute-start.54 = (f32[9216]{0:T(1024)S(1)}, f32[9216]{0:T(1024)S(1)}, u32[]{:S(2)}, u32[]{:S(2)}) collective-permute-start(f32[9216]{0:T(1024)S(1)} %add_add_fusion.1), channel_id=1, source_target_pairs={{0,16},{4,20},{8,24},{12,28},{16,0},{20,4},{24,8},{28,12},{1,17},{... | collective-permute-start | bytes 110600 | tf_op jit(solution)/shard_map/ppermute | solution.py:896
  574.7 19.4 %collective-permute-start.48 = (bf16[384,1024]{1,0:T(8,128)(2,1)S(1)}, bf16[384,1024]{1,0:T(8,128)(2,1)S(1)}, u32[]{:S(2)}, u32[]{:S(2)}) collective-permute-start(bf16[384,1024]{1,0:T(8,128)(2,1)S(1)} %maximum_select_fusion.5), channel_id=1, source_target_pairs={{0,4},{4,0},{8,12},{12,8},{16,20},{20,16},{24,28},{28,24},{1,5},{5... | collective-permute-start | bytes 2359304 | tf_op jit(solution)/shard_map/ppermute | solution.py:896
  (103 other events, 1288.1 us)
